TPU v7x, 32 devices: a whole 2x2x4 slice. The times are simulated.
32 devices in a mesh: row: 4 (over z), col: 8 (over y, x, core).
Axes of the slice: x: 2, y: 2, z: 4, core: 2. Of those that a mesh axis runs over, the one named last changes fastest.
Arguments:
- matrix: float32 [3072, 3072], P('row', 'col'), may hold values from -6 to 6
- panel_t: float32 [512, 3072], P('col', 'row'), may hold values from -0.25 to 0.25
- inverse_lower: float32 [512, 512], replicated, as said below
- pivot_rows: int32 [512], replicated, may hold values from 0 to 3071, as said below
Outputs:
- updated: float32 [3072, 3072], P('row', 'col')
Inputs may be any that keep to these rules, and one draw needn't show every extreme that they name: `pivot_rows`: entries are distinct; entry j is either j itself or a row at or past 768, so the interchanges are disjoint swaps. Exactly 256 entries differ from their position. The rows of one index of row are named by at most 128 entries, and in every draw some index of row is named by exactly 128. `inverse_lower`: zero above the diagonal and one on it.
All inputs are finite; a program needn't handle non-finite values.
Results may differ from a plain program's by a relative error of at most 0.000058.
Values sent between devices are 32-bit elements; how exact they have to be, the bound alone decides.
No kernel may reach another device: no remote copies, remote signals or barrier semaphores. Data moves between devices by JAX's collectives and lax.ppermute only.
A program may use at most 64 MiB of HBM per device.

v0:
```python
import jax
import jax.numpy as jnp
from jax import lax
from jax.sharding import PartitionSpec as P


def local(matrix, panel_t, inverse_lower, pivot_rows):
    rows, cols = matrix.shape
    width = inverse_lower.shape[0]
    first = lax.axis_index("row") * rows
    places = jnp.arange(width, dtype=jnp.int32)
    local_src = pivot_rows - first
    inside = (local_src >= 0) & (local_src < rows)
    fetched = jnp.take(matrix, jnp.clip(local_src, 0, rows - 1), axis=0)
    picked = jnp.where(inside[:, None], fetched, jnp.zeros_like(fetched))
    row_count = lax.axis_size("row")
    slot_count = width // row_count
    moved = pivot_rows != places
    destination = pivot_rows // rows
    owners = jnp.arange(row_count, dtype=jnp.int32)
    member = ((destination[:, None] == owners[None, :]) & moved[:, None]).astype(jnp.int32)
    earlier = jnp.cumsum(member, axis=0) - member
    slot_index = jnp.sum(earlier * member, axis=1)
    position = jnp.where(moved, destination * slot_count + slot_index, width)
    outgoing = jnp.zeros((width, cols), jnp.float32).at[position].set(matrix[:width], mode="drop")
    outgoing = jnp.where(first == 0, outgoing, jnp.zeros_like(outgoing))
    arrived = lax.all_to_all(outgoing, "row", split_axis=0, concat_axis=0, tiled=True)
    landing = (
        jnp.full((width,), rows, jnp.int32)
        .at[position]
        .set(pivot_rows - destination * rows, mode="drop")
    )
    my_landing = lax.dynamic_slice_in_dim(
        landing, lax.axis_index("row") * slot_count, slot_count, 0
    )
    swapped = matrix.at[my_landing].set(arrived[:slot_count], mode="drop")
    stacked = lax.psum(picked, "row")
    upper = jnp.dot(
        inverse_lower, stacked, precision=lax.Precision.HIGHEST, preferred_element_type=jnp.float32
    )
    product = lax.dot_general(
        lax.all_gather(panel_t, "col", axis=0, tiled=True),
        upper,
        (((0,), (0,)), ((), ())),
        precision=lax.Precision.HIGHEST,
        preferred_element_type=jnp.float32,
    )
    updated = swapped - product
    head = jnp.where(first == 0, upper, updated[:width])
    updated = lax.dynamic_update_slice_in_dim(updated, head, 0, 0)
    return updated


def solution(mesh):
    in_specs = (P("row", "col"), P("col", "row"), P(), P())
    out_specs = P("row", "col")
    return jax.shard_map(local, mesh=mesh, in_specs=in_specs, out_specs=out_specs, check_vma=False)
```

profile of v0, /device:TPU:0, one launch (start us, length us, event | category | flops | bytes accessed | tf_op | source)
XLA Modules:
  0.0 86.1 jit_solution(17809134601115859135)
XLA Ops:
  7.4 1.4 %copy.23 = f32[768,384]{1,0:T(8,128)S(1)} copy(f32[768,384]{1,0:T(8,128)} %param.4) | data formatting | bytes 2359296
  8.8 2.3 %gather_fusion = f32[512,384]{1,0:T(8,128)} fusion(f32[768,384]{1,0:T(8,128)S(1)} %copy.23, s32[1024]{0:T(1024)S(1)} %pad_clamp_fusion), kind=kCustom, calls=%fused_computation | custom fusion | bytes 1574912 | tf_op jit(solution)/shard_map/jit(_take)/gather | solution.py:14
  11.1 1.4 %copy.13 = f32[512,384]{0,1:T(8,128)S(1)} copy(f32[512,384]{1,0:T(8,128)} %gather_fusion) | data formatting | bytes 1572864 | tf_op jit(solution)/shard_map/jit(_take)/gather | solution.py:14
  12.5 1.0 %select_select_fusion = f32[512,384]{0,1:T(8,128)} fusion(f32[512,384]{0,1:T(8,128)S(1)} %copy.13, pred[512]{0:T(512)(128)(4,1)S(1)} %get-tuple-element.11, pred[512]{0:T(512)(128)(4,1)S(1)} %get-tuple-element.9), kind=kLoop, calls=%fused_computation.8 | loop fusion | flops 393216 | bytes 1573888 | tf_op jit(solution)/shard_map/jit(_where)/select_n | solution.py:15
  13.5 0.0 all-gather.2.cloned.1.call-start
  13.5 0.5 all-gather.2.cloned.1.call-update
  14.1 1.2 %reduce-window.6 = s32[4,4,128]{2,1,0:T(4,128)S(1)} reduce-window(s32[4,4,128]{2,1,0:T(4,128)S(1)} %fusion.11, s32[]{:T(128)} %constant.17.clone.1), window={size=1x1x128 pad=0_0x0_0x127_0}, to_apply=%region_0.1 | reduce-window | flops 260096 | bytes 16388 | tf_op jit(solution)/shard_map/reduce-window
  15.3 0.2 slice_reduce_fusion
  15.5 0.2 reduce-window.9
  15.7 0.1 add_bitcast_fusion
  15.8 2.5 %scatter_custom_fusion.1 = f32[512,384]{1,0:T(8,128)S(1)} fusion(s32[512]{0:T(512)S(1)} %compare_select_fusion.1, f32[768,384]{1,0:T(8,128)S(1)} %copy.23, f32[]{:T(128)} %constant.30.clone.1), kind=kCustom, calls=%fused_computation.9 | custom fusion | bytes 1572868 | tf_op jit(solution)/shard_map/scatter | solution.py:25
  18.3 1.1 %copy.11 = f32[512,384]{0,1:T(8,128)} copy(f32[512,384]{1,0:T(8,128)S(1)} %scatter_custom_fusion.1) | data formatting | bytes 1572864 | tf_op jit(solution)/shard_map/scatter | solution.py:25
  19.5 1.2 %broadcast_select_fusion = f32[512,384]{0,1:T(8,128)S(1)} fusion(f32[512,384]{0,1:T(8,128)} %copy.11, pred[]{:T(512)S(6)} %eq.34), kind=kLoop, calls=%fused_computation.12 | loop fusion | flops 196608 | bytes 1572865 | tf_op jit(solution)/shard_map/jit(_where)/select_n | solution.py:26
  20.7 1.1 %copy.16 = f32[512,384]{1,0:T(8,128)} copy(f32[512,384]{0,1:T(8,128)S(1)} %broadcast_select_fusion) | data formatting | bytes 1572864 | tf_op jit(solution)/shard_map/all_to_all | solution.py:27
  21.8 5.2 %all-to-all-start = ((f32[4,128,384]{2,1,0:T(8,128)}), f32[4,128,384]{2,1,0:T(8,128)}, u32[]{:S(2)}, u32[]{:S(2)}) async-start(f32[4,128,384]{2,1,0:T(8,128)} %bitcast.3), calls=%async_computation | async-start | bytes 1572864 | tf_op jit(solution)/shard_map/all_to_all | solution.py:27
  27.0 2.4 %scatter_custom_fusion = s32[512]{0:T(512)S(1)} fusion(s32[512]{0:T(512)S(1)} %compare_select_fusion.1, s32[512]{0:T(512)S(1)} %get-tuple-element.7, s32[]{:T(128)} %constant.15.clone.1), kind=kCustom, calls=%fused_computation.38 | custom fusion | bytes 2052 | tf_op jit(solution)/shard_map/scatter | solution.py:31
  29.5 0.1 compare_select_fusion.2
  29.5 37.8 %all-reduce.2.cloned.1.call-done = f32[512,384]{0,1:T(8,128)} async-done(((f32[512,384]{0,1:T(8,128)}), f32[512,384]{0,1:T(8,128)}) %all-reduce.2.cloned.1.call-update) | async-done | bytes 786448 | tf_op jit(solution)/shard_map/psum | solution.py:37
  67.4 2.6 %fusion.15 = f32[384,512]{1,0:T(8,128)S(1)} fusion(f32[512,384]{0,1:T(8,128)} %all-reduce.2.cloned.1.call-done, f32[512,512]{1,0:T(8,128)S(1)} %copy-done), kind=kOutput, calls=%fused_computation.40 | convolution fusion | flops 1207959552 | bytes 2621440 | tf_op jit(solution)/shard_map/dot_general | solution.py:38
  70.0 1.9 %scatter_custom_fusion.2 = f32[768,384]{1,0:T(8,128)S(1)} fusion(f32[768,384]{1,0:T(8,128)S(1)} %copy.23, s32[128]{0:T(128)S(1)} %compare_select_fusion.2, f32[4,128,384]{2,1,0:T(8,128)} %all-to-all-done), kind=kCustom, calls=%fused_computation.14 | custom fusion | bytes 1376256 | tf_op jit(solution)/shard_map/scatter | solution.py:36
  71.9 1.4 %copy.14 = f32[768,384]{0,1:T(8,128)} copy(f32[768,384]{1,0:T(8,128)S(1)} %scatter_custom_fusion.2) | data formatting | bytes 2359296 | tf_op jit(solution)/shard_map/scatter | solution.py:36
  73.2 3.8 %fusion = f32[768,384]{0,1:T(8,128)S(1)} fusion(f32[768,384]{0,1:T(8,128)} %copy.14, f32[384,512]{1,0:T(8,128)S(1)} %fusion.15, f32[512,768]{1,0:T(8,128)} %all-gather.2.cloned.1.call-done), kind=kOutput, calls=%fused_computation.5 | convolution fusion | flops 1812234240 | bytes 4718592 | tf_op jit(solution)/shard_map/dot_general | solution.py:41
  77.1 0.2 fusion.1
  77.3 1.4 %copy.15 = f32[768,384]{1,0:T(8,128)} copy(f32[768,384]{0,1:T(8,128)S(1)} %fusion.1) | data formatting | bytes 2359296 | tf_op jit(solution)/shard_map/dynamic_update_slice | solution.py:50
  (14 shorter events, 0.1 us)
Async XLA Ops:
  7.4 60.0 %copy-start = (f32[512,512]{1,0:T(8,128)S(1)}, f32[512,512]{1,0:T(8,128)}, u32[]{:S(2)}) copy-start(f32[512,512]{1,0:T(8,128)} %param.6) | copy-start | bytes 3145732
  7.4 1.4 %copy-start.1 = (s32[512]{0:T(512)S(1)}, s32[512]{0:T(512)}, u32[]{:S(2)}) copy-start(s32[512]{0:T(512)} %param.7) | copy-start | bytes 6148
  7.4 60.0 %all-reduce.2.cloned.1.call-start = ((), (), s32[]{:S(2)}) async-start(), calls=%async_computation.1 | async-start | bytes 1572864 | tf_op jit(solution)/shard_map/psum | solution.py:37
  13.5 59.8 %all-gather.2.cloned.1.call-start = ((), (), s32[]{:S(2)}) async-start(), calls=%async_computation.2 | async-start | bytes 1769472 | tf_op jit(solution)/shard_map/all_gather | solution.py:42
  21.8 48.1 %all-to-all-start = ((f32[4,128,384]{2,1,0:T(8,128)}), f32[4,128,384]{2,1,0:T(8,128)}, u32[]{:S(2)}, u32[]{:S(2)}) async-start(f32[4,128,384]{2,1,0:T(8,128)} %bitcast.3), calls=%async_computation | async-start | bytes 1572864 | tf_op jit(solution)/shard_map/all_to_all | solution.py:27
Sparse Core Ops, SparseCore 0:
  13.6 53.7 all-reduce.1
Sparse Core Ops, SparseCore 1:
  15.8 28.2 all-gather.1
where the time goes:
time: 86.5 us; the launch traced here: 86.1 us
  waiting for transfers between devices  38.4 us (44%)
  local copies, waits for them, and re-layouts  17.1 us (20%)
  between operations  15 us (17%)
  matrix products  6.41 us (7%)
  starting transfers between devices  5.23 us (6%)
  other arithmetic  4 us (5%)
    psum x1, waiting for transfers between devices, local(): stacked = lax.psum(picked, 'row')  37.8 us
    all_to_all x1, starting transfers between devices, local(): lax.all_to_all(outgoing, 'row', split_axis=0, concat_axis=0, tiled=True)  5.19 us
    dot_general x1, matrix products, local(): lax.dot_general(lax.all_gather(panel_t, 'col', axis=0, tiled=True), upper...  3.84 us
    gather x2, local copies, waits for them, and re-layouts, local(): fetched = jnp.take(matrix, jnp.clip(local_src, 0, rows - 1), axis=0)  3.68 us
    scatter x2, local copies, waits for them, and re-layouts, local(): jnp.zeros((width, cols), jnp.float32).at[position]  3.64 us
    scatter x2, local copies, waits for them, and re-layouts, local(): swapped = matrix.at[my_landing].set(arrived[:slot_count], mode='drop')  3.26 us
    dot_general x1, matrix products, local(): jnp.dot(inverse_lower, stacked, precision=lax.Precision.HIGHEST, preferre...  2.57 us
    scatter x1, local copies, waits for them, and re-layouts, local(): landing = jnp.full((width,), rows, jnp.int32).at[position].set(pivot_rows...  2.43 us
  transfers between devices with their start and end apart: 3, of which 1 were waited for; matrix products, arithmetic and copies ran while one was open for 19% of the time, Pallas kernels for 0%

commit v1 on v0

v1 whole, which is shorter than its diff:
```python
import functools

import jax
import jax.numpy as jnp
from jax import lax
from jax.experimental import pallas as pl
from jax.experimental.pallas import tpu as pltpu
from jax.sharding import PartitionSpec as P

F32 = jnp.float32
BF16 = jnp.bfloat16
VMEM = pl.BlockSpec(memory_space=pltpu.VMEM)
SMEM = pl.BlockSpec(memory_space=pltpu.SMEM)
LIMIT = 48 * 1024 * 1024


def halves(x):
    high = x.astype(BF16)
    low = (x - high.astype(F32)).astype(BF16)
    return high, low


def thirds(x):
    high = x.astype(BF16)
    rest = x - high.astype(F32)
    middle = rest.astype(BF16)
    low = (rest - middle.astype(F32)).astype(BF16)
    return high, middle, low


def mm(a, b):
    return jnp.dot(a, b, preferred_element_type=F32)


def mm_nt(a, b):
    return lax.dot_general(a, b, (((1,), (1,)), ((), ())), preferred_element_type=F32)


def mm_tn(a, b):
    return lax.dot_general(a, b, (((0,), (0,)), ((), ())), preferred_element_type=F32)


def classify(pivot, count, rows):
    width = pivot.shape[1]
    lanes = lax.broadcasted_iota(jnp.int32, (1, width), 1)
    kind = jnp.where(pivot != lanes, pivot // rows, 0)
    padded = -(-count // 16) * 16
    owner = lax.broadcasted_iota(jnp.int32, (padded, width), 0)
    member = owner == kind
    before = lax.broadcasted_iota(jnp.int32, (width, width), 0) < lax.broadcasted_iota(
        jnp.int32, (width, width), 1
    )
    ranks = mm(member.astype(BF16), before.astype(BF16))
    place = jnp.sum(jnp.where(member, ranks, 0.0), axis=0, keepdims=True)
    return kind, place.astype(jnp.int32)


def one_hot(position, slots):
    slot = lax.broadcasted_iota(jnp.int32, (slots, position.shape[1]), 0)
    return slot == position


def pick_kernel(count, me_ref, pivot_ref, matrix_ref, stay_ref, send_ref):
    rows, cols = matrix_ref.shape
    width = pivot_ref.shape[1]
    slot = width // count
    me = me_ref[0]
    pivot = pivot_ref[...]
    kind, place = classify(pivot, count, rows)

    @pl.when(me == 0)
    def _():
        parts = thirds(matrix_ref[:width, :])
        stay = one_hot(jnp.where(kind == 0, place, -1), stay_ref.shape[0]).astype(BF16)
        stay_ref[...] = sum(mm(stay, part) for part in reversed(parts))
        moved = one_hot(jnp.where(kind == 0, -1, kind * slot + place), width).astype(BF16)
        send_ref[...] = sum(mm(moved, part) for part in reversed(parts))

    @pl.when(me != 0)
    def _():
        parts = thirds(matrix_ref[...])
        mine = one_hot(jnp.where(kind == me, place, -1), slot)
        source = jnp.sum(jnp.where(mine, pivot - me * rows, 0), axis=1, keepdims=True)
        pick = lax.broadcasted_iota(jnp.int32, (slot, rows), 1) == source
        pick = pick.astype(BF16)
        got = sum(mm(pick, part) for part in reversed(parts))
        stay_ref[...] = jnp.zeros_like(stay_ref)
        for d in range(count):
            send_ref[pl.ds(d * slot, slot), :] = got


def coefficient_kernel(count, me_ref, shard_ids, pivot_ref, inverse_ref, matrix_ref, *refs):
    shards = refs[:-3]
    base_ref, high_ref, low_ref = refs[-3:]
    rows, cols = matrix_ref.shape
    width = pivot_ref.shape[1]
    slot = width // count
    stay = width // 2
    depth = shards[0].shape[0]
    total = stay + width
    me = me_ref[0]
    pivot = pivot_ref[...]
    kind, place = classify(pivot, count, rows)
    position = jnp.where(kind == 0, place, stay + kind * slot + place)
    spread = one_hot(position, total).astype(BF16)
    inv_high, inv_low = halves(inverse_ref[...])
    col_high = mm_nt(inv_high, spread).astype(BF16)
    col_low = mm_nt(inv_low, spread).astype(BF16)

    acc = jnp.zeros((rows, total), F32)
    pan = jnp.concatenate([s[...] for s in shards], axis=0)
    pan_high, pan_low = halves(pan)
    order_a, order_b = [], []
    for k in range(len(shards)):
        start = pl.multiple_of(shard_ids[k] * depth, depth)
        order_a.append(start)
    shard_of = lax.broadcasted_iota(jnp.int32, (width, 1), 0)
    source = jnp.zeros((width, 1), jnp.int32)
    for k in range(len(shards)):
        inside = (shard_of >= k * depth) & (shard_of < (k + 1) * depth)
        source = jnp.where(inside, shard_of - k * depth + shard_ids[k] * depth, source)
    order = (lax.broadcasted_iota(jnp.int32, (width, width), 1) == source).astype(BF16)
    ord_high = mm(order, col_high).astype(BF16)
    ord_low = mm(order, col_low).astype(BF16)
    acc = mm_tn(pan_low, ord_high) + mm_tn(pan_high, ord_low) + mm_tn(pan_high, ord_high)
    value = -acc

    local = pivot - me * rows
    row_ids = lax.broadcasted_iota(jnp.int32, (rows, width), 0)
    landing = (row_ids == local) & (kind == me) & (kind != 0)
    mine = one_hot(jnp.where((kind == me) & (kind != 0), place, -1), slot).astype(BF16)
    land = mm_nt(landing.astype(BF16), mine)
    value = jnp.concatenate([value[:, :stay], land, value[:, stay + slot :]], axis=1)
    taken = jnp.sum(landing.astype(F32), axis=1, keepdims=True)
    high, low = halves(value)
    high_ref[...] = high
    low_ref[...] = low
    base_ref[...] = jnp.where(taken > 0.5, 0.0, matrix_ref[...])

    @pl.when(me == 0)
    def _():
        high_ref[:width, :] = col_high
        low_ref[:width, :] = col_low
        base_ref[:width, :] = jnp.zeros((width, cols), F32)


def update_kernel(base_ref, high_ref, low_ref, moved_ref, *refs):
    stays, out_ref = refs[:-1], refs[-1]
    stay_rows = stays[0].shape[0]
    stay = stays[0][...]
    for other in stays[1:]:
        stay = stay + other[...]
    s_high, s_low = halves(stay)
    m_high, m_low = halves(moved_ref[...])
    high, low = high_ref[...], low_ref[...]
    s_part = mm(low[:, :stay_rows], s_high) + mm(high[:, :stay_rows], s_low) + mm(high[:, :stay_rows], s_high)
    m_part = mm(low[:, stay_rows:], m_high) + mm(high[:, stay_rows:], m_low) + mm(high[:, stay_rows:], m_high)
    out_ref[...] = base_ref[...] + (s_part + m_part)


def gather_shards(shard, count):
    held, masks = [shard], [0]
    bits = []
    bit = 1
    while bit < count:
        bits.append(bit)
        bit *= 2
    while bits:
        group = [bits.pop()]
        if bits and bits[-1] > 1:
            group.append(bits.pop())
        steps = [group[0]] if len(group) == 1 else [group[0], group[1], group[0] | group[1]]
        new, new_masks = [], []
        for step in steps:
            pairs = [(i, i ^ step) for i in range(count)]
            for piece, mask in zip(held, masks):
                new.append(lax.ppermute(piece, "col", pairs))
                new_masks.append(mask ^ step)
        held, masks = held + new, masks + new_masks
    return held, masks


def spread_rows(stay, count):
    middle = count // 2
    first = lax.ppermute(stay, "row", [(0, middle)])
    parts = [stay, first]
    up = down = first
    for k in range(1, count):
        if middle + k < count:
            up = lax.ppermute(up, "row", [(middle + k - 1, middle + k)])
            parts.append(up)
        if middle - k > 0:
            down = lax.ppermute(down, "row", [(middle - k + 1, middle - k)])
            parts.append(down)
    return parts


def local(row_count, col_count, matrix, panel_t, inverse_lower, pivot_rows):
    rows, cols = matrix.shape
    width = inverse_lower.shape[0]
    slot = width // row_count
    stay = width // 2
    me = lax.axis_index("row").astype(jnp.int32).reshape(1)
    column = lax.axis_index("col").astype(jnp.int32)
    pivot = pivot_rows.reshape(1, width)
    params = pltpu.CompilerParams(vmem_limit_bytes=LIMIT)

    stayed, sent = pl.pallas_call(
        functools.partial(pick_kernel, row_count),
        out_shape=(
            jax.ShapeDtypeStruct((stay, cols), F32),
            jax.ShapeDtypeStruct((width, cols), F32),
        ),
        in_specs=[SMEM, VMEM, VMEM],
        out_specs=(VMEM, VMEM),
        compiler_params=params,
        name="pick",
    )(me, pivot, matrix)

    stays = spread_rows(stayed, row_count)
    moved = lax.all_to_all(sent, "row", split_axis=0, concat_axis=0, tiled=True)
    shards, masks = gather_shards(panel_t, col_count)
    ids = column ^ jnp.array(masks, jnp.int32)

    base, high, low = pl.pallas_call(
        functools.partial(coefficient_kernel, row_count),
        out_shape=(
            jax.ShapeDtypeStruct((rows, cols), F32),
            jax.ShapeDtypeStruct((rows, stay + width), BF16),
            jax.ShapeDtypeStruct((rows, stay + width), BF16),
        ),
        in_specs=[SMEM, SMEM] + [VMEM] * (3 + len(shards)),
        out_specs=(VMEM, VMEM, VMEM),
        compiler_params=params,
        name="coefficients",
    )(me, ids, pivot, inverse_lower, matrix, *shards)

    return pl.pallas_call(
        update_kernel,
        out_shape=jax.ShapeDtypeStruct((rows, cols), F32),
        in_specs=[VMEM] * (4 + len(stays)),
        out_specs=VMEM,
        compiler_params=params,
        name="update",
    )(base, high, low, moved, *stays)


def solution(mesh):
    in_specs = (P("row", "col"), P("col", "row"), P(), P())
    out_specs = P("row", "col")
    return jax.shard_map(
        functools.partial(local, mesh.shape["row"], mesh.shape["col"]),
        mesh=mesh,
        in_specs=in_specs,
        out_specs=out_specs,
        check_vma=False,
    )
```

time: 86.5 us -> 57.9 us (0.67)
  the two profiles are of different devices: /device:TPU:0 before, /device:TPU:23 now
where the time goes in v1:
time: 57.9 us; the launch traced here: 57.3 us
  starting transfers between devices  16.9 us (29%)
  waiting for transfers between devices  15.8 us (27%)
  local copies, waits for them, and re-layouts  12.8 us (22%)
  Pallas kernels  11.7 us (20%)
    ppermute x1, waiting for transfers between devices, spread_rows(): first = lax.ppermute(stay, 'row', [(0, middle)])  15.4 us
    unnamed x34, local copies, waits for them, and re-layouts  12.8 us
    ppermute x7, starting transfers between devices, gather_shards(): new.append(lax.ppermute(piece, 'col', pairs))  6.91 us
    pallas_call x1, Pallas kernels, local(): pl.pallas_call(functools.partial(coefficient_kernel, row_count), out_shap...  5.65 us
    all_to_all x1, starting transfers between devices, local(): moved = lax.all_to_all(sent, 'row', split_axis=0, concat_axis=0, tiled=True)  4.64 us
    pallas_call x1, Pallas kernels, local(): pl.pallas_call(update_kernel, out_shape=jax.ShapeDtypeStruct((rows, cols)...  4.3 us
    ppermute x1, starting transfers between devices, spread_rows(): down = lax.ppermute(down, 'row', [(middle - k + 1, middle - k)])  2.07 us
    ppermute x1, starting transfers between devices, spread_rows(): up = lax.ppermute(up, 'row', [(middle + k - 1, middle + k)])  2.05 us
  transfers between devices with their start and end apart: 11, of which 2 were waited for; matrix products, arithmetic and copies ran while one was open for 0% of the time, Pallas kernels for 10%

profile of v1, /device:TPU:23, one launch (start us, length us, event | category | flops | bytes accessed | tf_op | source)
XLA Modules:
  0.0 57.3 jit_solution(11422766715691119836)
XLA Ops:
  0.0 1.3 %copy-done = f32[768,384]{1,0:T(8,128)S(1)} copy-done((f32[768,384]{1,0:T(8,128)S(1)}, f32[768,384]{1,0:T(8,128)}, u32[]{:S(2)}) %copy-start) | copy-done | bytes 1179672
  1.3 0.7 %copy-done.14 = s32[512]{0:T(512)S(1)} copy-done((s32[512]{0:T(512)S(1)}, s32[512]{0:T(512)}, u32[]{:S(2)}) %copy-start.14) | copy-done | bytes 2072
  2.0 1.7 %pick.1 = (f32[256,384]{1,0:T(8,128)S(1)}, f32[512,384]{1,0:T(8,128)}) custom-call(s32[1]{0:T(128)} %bitcast.me_ref, s32[1,512]{1,0:T(1,128)S(1)} %bitcast.5, f32[768,384]{1,0:T(8,128)S(1)} %copy-done), custom_call_target="tpu_custom_call" | custom-call | tf_op jit(solution)/shard_map/pick/pallas_call | solution.py:208
  3.7 4.6 %all-to-all-start = ((f32[4,128,384]{2,1,0:T(8,128)}), f32[4,128,384]{2,1,0:T(8,128)S(1)}, u32[]{:S(2)}, u32[]{:S(2)}) async-start(f32[4,128,384]{2,1,0:T(8,128)} %bitcast.2), calls=%async_computation | async-start | bytes 1572864 | tf_op jit(solution)/shard_map/all_to_all | solution.py:221
  8.3 1.3 %collective-permute-start.7 = (f32[256,384]{1,0:T(8,128)S(1)}, f32[256,384]{1,0:T(8,128)}, u32[]{:S(2)}, u32[]{:S(2)}) collective-permute-start(f32[256,384]{1,0:T(8,128)S(1)} %get-tuple-element.14.refs_0_), channel_id=1, source_target_pairs={{0,16},{1,17},{2,18},{3,19},{4,20},{5,21},{6,22},{7,23}} | collective-permute-start | bytes 1179656 | tf_op jit(solution)/shard_map/ppermute | solution.py:185
  10.2 2.2 %collective-permute-start.2 = (f32[64,768]{1,0:T(8,128)S(1)}, f32[64,768]{1,0:T(8,128)S(1)}, u32[]{:S(2)}, u32[]{:S(2)}) collective-permute-start(f32[64,768]{1,0:T(8,128)S(1)} %copy-done.4), channel_id=1, source_target_pairs={{0,6},{1,7},{2,4},{3,5},{4,2},{5,3},{6,0},{7,1},{8,14},{9,15},{10,... | collective-permute-start | bytes 589832 | tf_op jit(solution)/shard_map/ppermute | solution.py:177
  12.3 2.1 %collective-permute-start.3 = (f32[64,768]{1,0:T(8,128)S(1)}, f32[64,768]{1,0:T(8,128)S(1)}, u32[]{:S(2)}, u32[]{:S(2)}) collective-permute-start(f32[64,768]{1,0:T(8,128)S(1)} %copy-done.4), channel_id=1, source_target_pairs={{0,1},{1,0},{2,3},{3,2},{4,5},{5,4},{6,7},{7,6},{8,9},{9,8},{10,11... | collective-permute-start | bytes 589832 | tf_op jit(solution)/shard_map/ppermute | solution.py:177
  14.4 15.4 %collective-permute-done.7.refs_1_ = f32[256,384]{1,0:T(8,128)} collective-permute-done((f32[256,384]{1,0:T(8,128)S(1)}, f32[256,384]{1,0:T(8,128)}, u32[]{:S(2)}, u32[]{:S(2)}) %collective-permute-start.7) | collective-permute-done | bytes 393248 | tf_op jit(solution)/shard_map/ppermute | solution.py:185
  29.8 2.1 %collective-permute-start.8 = (f32[256,384]{1,0:T(8,128)}, f32[256,384]{1,0:T(8,128)}, u32[]{:S(2)}, u32[]{:S(2)}) collective-permute-start(f32[256,384]{1,0:T(8,128)} %collective-permute-done.7.refs_1_), channel_id=1, source_target_pairs={{16,24},{17,25},{18,26},{19,27},{20,28},{21,29},{22,30},{23,31}} | collective-permute-start | bytes 1179656 | tf_op jit(solution)/shard_map/ppermute | solution.py:190
  31.9 2.1 %collective-permute-start.9 = (f32[256,384]{1,0:T(8,128)}, f32[256,384]{1,0:T(8,128)}, u32[]{:S(2)}, u32[]{:S(2)}) collective-permute-start(f32[256,384]{1,0:T(8,128)} %collective-permute-done.7.refs_1_), channel_id=1, source_target_pairs={{16,8},{17,9},{18,10},{19,11},{20,12},{21,13},{22,14},{23,15}} | collective-permute-start | bytes 1179656 | tf_op jit(solution)/shard_map/ppermute | solution.py:193
  34.0 1.6 %collective-permute-start.4 = (f32[64,768]{1,0:T(8,128)S(1)}, f32[64,768]{1,0:T(8,128)S(1)}, u32[]{:S(2)}, u32[]{:S(2)}) collective-permute-start(f32[64,768]{1,0:T(8,128)S(1)} %collective-permute-done.refs_1_), channel_id=1, source_target_pairs={{0,1},{1,0},{2,3},{3,2},{4,5},{5,4},{6,7},{7,6},{8,9},{9,8},{10,11... | collective-permute-start | bytes 589832 | tf_op jit(solution)/shard_map/ppermute | solution.py:177
  35.6 0.7 %copy-done.6 = f32[64,768]{1,0:T(8,128)} copy-done((f32[64,768]{1,0:T(8,128)}, f32[64,768]{1,0:T(8,128)S(1)}, u32[]{:S(2)}) %copy-start.6) | copy-done | bytes 196632
  36.3 0.7 %copy-done.8 = f32[64,768]{1,0:T(8,128)} copy-done((f32[64,768]{1,0:T(8,128)}, f32[64,768]{1,0:T(8,128)S(1)}, u32[]{:S(2)}) %copy-start.8) | copy-done | bytes 196632
  38.1 0.7 %copy-done.10 = f32[64,768]{1,0:T(8,128)} copy-done((f32[64,768]{1,0:T(8,128)}, f32[64,768]{1,0:T(8,128)S(1)}, u32[]{:S(2)}) %copy-start.10) | copy-done | bytes 196632
  39.2 1.2 %copy-done.3 = f32[512,512]{1,0:T(8,128)S(1)} copy-done((f32[512,512]{1,0:T(8,128)S(1)}, f32[512,512]{1,0:T(8,128)}, u32[]{:S(2)}) %copy-start.3) | copy-done | bytes 1048600
  40.4 0.9 %copy-done.5 = f32[64,768]{1,0:T(8,128)S(1)} copy-done((f32[64,768]{1,0:T(8,128)S(1)}, f32[64,768]{1,0:T(8,128)}, u32[]{:S(2)}) %copy-start.5) | copy-done | bytes 196632
  41.4 0.9 %copy-done.7 = f32[64,768]{1,0:T(8,128)S(1)} copy-done((f32[64,768]{1,0:T(8,128)S(1)}, f32[64,768]{1,0:T(8,128)}, u32[]{:S(2)}) %copy-start.7) | copy-done | bytes 196632
  42.3 0.9 %copy-done.9 = f32[64,768]{1,0:T(8,128)S(1)} copy-done((f32[64,768]{1,0:T(8,128)S(1)}, f32[64,768]{1,0:T(8,128)}, u32[]{:S(2)}) %copy-start.9) | copy-done | bytes 196632
  43.2 0.9 %copy-done.11 = f32[64,768]{1,0:T(8,128)S(1)} copy-done((f32[64,768]{1,0:T(8,128)S(1)}, f32[64,768]{1,0:T(8,128)}, u32[]{:S(2)}) %copy-start.11) | copy-done | bytes 196632
  44.1 0.9 %copy-done.13 = f32[64,768]{1,0:T(8,128)S(1)} copy-done((f32[64,768]{1,0:T(8,128)S(1)}, f32[64,768]{1,0:T(8,128)}, u32[]{:S(2)}) %copy-start.13) | copy-done | bytes 196632
  45.1 5.6 %coefficients.1 = (f32[768,384]{1,0:T(8,128)S(1)}, bf16[768,768]{1,0:T(8,128)(2,1)S(1)}, bf16[768,768]{1,0:T(8,128)(2,1)S(1)}) custom-call(s32[1]{0:T(128)} %bitcast.me_ref, s32[8]{0:T(128)S(1)} %broadcast_xor_fusion.shard_ids, s32[1,512]{1,0:T(1,128)S(1)} %bitcast.6, f32[512,512]{1,0:T(8,128)S(1)} %copy-done.3, f32[768,384]{1,0:T(8,128)} %matrix_ref.3, ...), custom_call_target="tpu_custom_call" | custom-call | tf_op jit(solution)/shard_map/coefficients/pallas_call | solution.py:225
  50.7 1.0 %copy-done.1 = bf16[768,768]{1,0:T(8,128)(2,1)} copy-done((bf16[768,768]{1,0:T(8,128)(2,1)}, bf16[768,768]{1,0:T(8,128)(2,1)S(1)}, u32[]{:S(2)}) %copy-start.1) | copy-done | bytes 1179672
  51.8 1.3 %copy-done.2 = bf16[768,768]{1,0:T(8,128)(2,1)S(1)} copy-done((bf16[768,768]{1,0:T(8,128)(2,1)S(1)}, bf16[768,768]{1,0:T(8,128)(2,1)}, u32[]{:S(2)}) %copy-start.2) | copy-done | bytes 1179672
  53.0 4.3 %update.1 = f32[768,384]{1,0:T(8,128)} custom-call(f32[768,384]{1,0:T(8,128)S(1)} %get-tuple-element.10.base_ref, bf16[768,768]{1,0:T(8,128)(2,1)S(1)} %get-tuple-element.11.high_ref, bf16[768,768]{1,0:T(8,128)(2,1)S(1)} %copy-done.2, f32[512,384]{1,0:T(8,128)S(1)} %bitcast.4, f32[256,384]{1,0:T(8,128)S(1)} %get-tuple-element.14.refs_0_, ...), custom_call_target="tpu_custom_call" | custom-call | tf_op jit(solution)/shard_map/update/pallas_call | solution.py:238
  (36 shorter events, 2.2 us)
Async XLA Ops:
  0.0 1.3 %copy-start = (f32[768,384]{1,0:T(8,128)S(1)}, f32[768,384]{1,0:T(8,128)}, u32[]{:S(2)}) copy-start(f32[768,384]{1,0:T(8,128)} %matrix_ref.3) | copy-start | bytes 3538948
  2.0 7.7 %copy-start.4 = (f32[64,768]{1,0:T(8,128)S(1)}, f32[64,768]{1,0:T(8,128)}, u32[]{:S(2)}) copy-start(f32[64,768]{1,0:T(8,128)} %refs_0_.1) | copy-start | bytes 589828
  2.0 36.8 %copy-start.16 = (s32[8]{0:T(128)S(1)}, s32[8]{0:T(128)}, u32[]{:S(2)}) copy-start(s32[8]{0:T(128)} %constant.10.clone) | copy-start | bytes 100
  2.0 37.2 %copy-start.15 = (s32[512]{0:T(512)S(1)}, s32[512]{0:T(512)}, u32[]{:S(2)}) copy-start(s32[512]{0:T(512)} %param.8) | copy-start | bytes 6148
  3.7 48.1 %all-to-all-start = ((f32[4,128,384]{2,1,0:T(8,128)}), f32[4,128,384]{2,1,0:T(8,128)S(1)}, u32[]{:S(2)}, u32[]{:S(2)}) async-start(f32[4,128,384]{2,1,0:T(8,128)} %bitcast.2), calls=%async_computation | async-start | bytes 1572864 | tf_op jit(solution)/shard_map/all_to_all | solution.py:221
  8.3 21.5 %collective-permute-start.7 = (f32[256,384]{1,0:T(8,128)S(1)}, f32[256,384]{1,0:T(8,128)}, u32[]{:S(2)}, u32[]{:S(2)}) collective-permute-start(f32[256,384]{1,0:T(8,128)S(1)} %get-tuple-element.14.refs_0_), channel_id=1, source_target_pairs={{0,16},{1,17},{2,18},{3,19},{4,20},{5,21},{6,22},{7,23}} | collective-permute-start | bytes 1179656 | tf_op jit(solution)/shard_map/ppermute | solution.py:185
  9.6 22.3 %collective-permute-start = (f32[64,768]{1,0:T(8,128)S(1)}, f32[64,768]{1,0:T(8,128)S(1)}, u32[]{:S(2)}, u32[]{:S(2)}) collective-permute-start(f32[64,768]{1,0:T(8,128)S(1)} %copy-done.4), channel_id=1, source_target_pairs={{0,4},{1,5},{2,6},{3,7},{4,0},{5,1},{6,2},{7,3},{8,12},{9,13},{10,... | collective-permute-start | bytes 589832 | tf_op jit(solution)/shard_map/ppermute | solution.py:177
  9.9 24.0 %collective-permute-start.1 = (f32[64,768]{1,0:T(8,128)S(1)}, f32[64,768]{1,0:T(8,128)S(1)}, u32[]{:S(2)}, u32[]{:S(2)}) collective-permute-start(f32[64,768]{1,0:T(8,128)S(1)} %copy-done.4), channel_id=1, source_target_pairs={{0,2},{1,3},{2,0},{3,1},{4,6},{5,7},{6,4},{7,5},{8,10},{9,11},{10,... | collective-permute-start | bytes 589832 | tf_op jit(solution)/shard_map/ppermute | solution.py:177
  10.2 26.1 %collective-permute-start.2 = (f32[64,768]{1,0:T(8,128)S(1)}, f32[64,768]{1,0:T(8,128)S(1)}, u32[]{:S(2)}, u32[]{:S(2)}) collective-permute-start(f32[64,768]{1,0:T(8,128)S(1)} %copy-done.4), channel_id=1, source_target_pairs={{0,6},{1,7},{2,4},{3,5},{4,2},{5,3},{6,0},{7,1},{8,14},{9,15},{10,... | collective-permute-start | bytes 589832 | tf_op jit(solution)/shard_map/ppermute | solution.py:177
  12.3 24.6 %collective-permute-start.3 = (f32[64,768]{1,0:T(8,128)S(1)}, f32[64,768]{1,0:T(8,128)S(1)}, u32[]{:S(2)}, u32[]{:S(2)}) collective-permute-start(f32[64,768]{1,0:T(8,128)S(1)} %copy-done.4), channel_id=1, source_target_pairs={{0,1},{1,0},{2,3},{3,2},{4,5},{5,4},{6,7},{7,6},{8,9},{9,8},{10,11... | collective-permute-start | bytes 589832 | tf_op jit(solution)/shard_map/ppermute | solution.py:177
  29.8 21.9 %collective-permute-start.8 = (f32[256,384]{1,0:T(8,128)}, f32[256,384]{1,0:T(8,128)}, u32[]{:S(2)}, u32[]{:S(2)}) collective-permute-start(f32[256,384]{1,0:T(8,128)} %collective-permute-done.7.refs_1_), channel_id=1, source_target_pairs={{16,24},{17,25},{18,26},{19,27},{20,28},{21,29},{22,30},{23,31}} | collective-permute-start | bytes 1179656 | tf_op jit(solution)/shard_map/ppermute | solution.py:190
  31.9 19.9 %collective-permute-start.9 = (f32[256,384]{1,0:T(8,128)}, f32[256,384]{1,0:T(8,128)}, u32[]{:S(2)}, u32[]{:S(2)}) collective-permute-start(f32[256,384]{1,0:T(8,128)} %collective-permute-done.7.refs_1_), channel_id=1, source_target_pairs={{16,8},{17,9},{18,10},{19,11},{20,12},{21,13},{22,14},{23,15}} | collective-permute-start | bytes 1179656 | tf_op jit(solution)/shard_map/ppermute | solution.py:193
  34.0 4.9 %collective-permute-start.4 = (f32[64,768]{1,0:T(8,128)S(1)}, f32[64,768]{1,0:T(8,128)S(1)}, u32[]{:S(2)}, u32[]{:S(2)}) collective-permute-start(f32[64,768]{1,0:T(8,128)S(1)} %collective-permute-done.refs_1_), channel_id=1, source_target_pairs={{0,1},{1,0},{2,3},{3,2},{4,5},{5,4},{6,7},{7,6},{8,9},{9,8},{10,11... | collective-permute-start | bytes 589832 | tf_op jit(solution)/shard_map/ppermute | solution.py:177
  36.2 2.6 %collective-permute-start.5 = (f32[64,768]{1,0:T(8,128)S(1)}, f32[64,768]{1,0:T(8,128)S(1)}, u32[]{:S(2)}, u32[]{:S(2)}) collective-permute-start(f32[64,768]{1,0:T(8,128)S(1)} %collective-permute-done.1.refs_2_), channel_id=1, source_target_pairs={{0,1},{1,0},{2,3},{3,2},{4,5},{5,4},{6,7},{7,6},{8,9},{9,8},{10,11... | collective-permute-start | bytes 589832 | tf_op jit(solution)/shard_map/ppermute | solution.py:177
  36.2 0.7 %copy-start.8 = (f32[64,768]{1,0:T(8,128)}, f32[64,768]{1,0:T(8,128)S(1)}, u32[]{:S(2)}) copy-start(f32[64,768]{1,0:T(8,128)S(1)} %collective-permute-done.1.refs_2_) | copy-start | bytes 589828
  37.6 1.6 %collective-permute-start.6 = (f32[64,768]{1,0:T(8,128)S(1)}, f32[64,768]{1,0:T(8,128)S(1)}, u32[]{:S(2)}, u32[]{:S(2)}) collective-permute-start(f32[64,768]{1,0:T(8,128)S(1)} %collective-permute-done.2.refs_3_), channel_id=1, source_target_pairs={{0,1},{1,0},{2,3},{3,2},{4,5},{5,4},{6,7},{7,6},{8,9},{9,8},{10,11... | collective-permute-start | bytes 589832 | tf_op jit(solution)/shard_map/ppermute | solution.py:177
  39.2 1.2 %copy-start.3 = (f32[512,512]{1,0:T(8,128)S(1)}, f32[512,512]{1,0:T(8,128)}, u32[]{:S(2)}) copy-start(f32[512,512]{1,0:T(8,128)} %inverse_ref.1) | copy-start | bytes 3145732
  40.4 0.9 %copy-start.5 = (f32[64,768]{1,0:T(8,128)S(1)}, f32[64,768]{1,0:T(8,128)}, u32[]{:S(2)}) copy-start(f32[64,768]{1,0:T(8,128)} %refs_0_.1) | copy-start | bytes 589828
  41.4 0.9 %copy-start.7 = (f32[64,768]{1,0:T(8,128)S(1)}, f32[64,768]{1,0:T(8,128)}, u32[]{:S(2)}) copy-start(f32[64,768]{1,0:T(8,128)} %copy-done.6) | copy-start | bytes 589828
  42.3 0.9 %copy-start.9 = (f32[64,768]{1,0:T(8,128)S(1)}, f32[64,768]{1,0:T(8,128)}, u32[]{:S(2)}) copy-start(f32[64,768]{1,0:T(8,128)} %copy-done.8) | copy-start | bytes 589828
  43.2 0.9 %copy-start.11 = (f32[64,768]{1,0:T(8,128)S(1)}, f32[64,768]{1,0:T(8,128)}, u32[]{:S(2)}) copy-start(f32[64,768]{1,0:T(8,128)} %copy-done.10) | copy-start | bytes 589828
  44.1 0.9 %copy-start.13 = (f32[64,768]{1,0:T(8,128)S(1)}, f32[64,768]{1,0:T(8,128)}, u32[]{:S(2)}) copy-start(f32[64,768]{1,0:T(8,128)} %copy-done.12) | copy-start | bytes 589828
  50.7 1.0 %copy-start.1 = (bf16[768,768]{1,0:T(8,128)(2,1)}, bf16[768,768]{1,0:T(8,128)(2,1)S(1)}, u32[]{:S(2)}) copy-start(bf16[768,768]{1,0:T(8,128)(2,1)S(1)} %get-tuple-element.12.low_ref) | copy-start | bytes 3538948
  51.7 1.3 %copy-start.2 = (bf16[768,768]{1,0:T(8,128)(2,1)S(1)}, bf16[768,768]{1,0:T(8,128)(2,1)}, u32[]{:S(2)}) copy-start(bf16[768,768]{1,0:T(8,128)(2,1)} %copy-done.1) | copy-start | bytes 3538948
  (4 other events, 2.7 us)

commit v2 on v1

v2 whole, which is shorter than its diff:
```python
import functools

import jax
import jax.numpy as jnp
from jax import lax
from jax.experimental import pallas as pl
from jax.experimental.pallas import tpu as pltpu
from jax.sharding import PartitionSpec as P

F32 = jnp.float32
BF16 = jnp.bfloat16
VMEM = pl.BlockSpec(memory_space=pltpu.VMEM)
SMEM = pl.BlockSpec(memory_space=pltpu.SMEM)
HBM = pl.BlockSpec(memory_space=pltpu.HBM)
PARAMS = pltpu.CompilerParams(vmem_limit_bytes=20 * 1024 * 1024)


def halves(x):
    high = x.astype(BF16)
    low = (x - high.astype(F32)).astype(BF16)
    return high, low


def thirds(x):
    high = x.astype(BF16)
    rest = x - high.astype(F32)
    middle = rest.astype(BF16)
    low = (rest - middle.astype(F32)).astype(BF16)
    return high, middle, low


def mm(a, b):
    return jnp.dot(a, b, preferred_element_type=F32)


def mm_nt(a, b):
    return lax.dot_general(a, b, (((1,), (1,)), ((), ())), preferred_element_type=F32)


def mm_tn(a, b):
    return lax.dot_general(a, b, (((0,), (0,)), ((), ())), preferred_element_type=F32)


def classify(pivot, count, rows):
    width = pivot.shape[1]
    lanes = lax.broadcasted_iota(jnp.int32, (1, width), 1)
    kind = jnp.where(pivot != lanes, pivot // rows, 0)
    padded = -(-count // 16) * 16
    owner = lax.broadcasted_iota(jnp.int32, (padded, width), 0)
    member = owner == kind
    before = lax.broadcasted_iota(jnp.int32, (width, width), 0) < lax.broadcasted_iota(
        jnp.int32, (width, width), 1
    )
    ranks = mm(member.astype(BF16), before.astype(BF16))
    place = jnp.sum(jnp.where(member, ranks, 0.0), axis=0, keepdims=True)
    return kind, place.astype(jnp.int32)


def one_hot(position, slots):
    slot = lax.broadcasted_iota(jnp.int32, (slots, position.shape[1]), 0)
    return (slot == position).astype(BF16)


def picked(pick, rows):
    high, middle, low = thirds(rows)
    return mm(pick, low) + mm(pick, middle) + mm(pick, high)


def plan(count):
    middle, chunks = count // 2, count // 2
    first = [(0, middle, ("stay", c)) for c in range(chunks)]
    relays, down, late = [], [], []
    for c in range(chunks):
        for k in range(1, count):
            if middle + k < count:
                relays.append((middle + k - 1, middle + k, ("stay", c)))
            if middle - k > 0:
                relays.append((middle - k + 1, middle - k, ("stay", c)))
    for gap in range(count - 1, 0, -1):
        down += [(r, r - gap, ("pick", r)) for r in range(count - 1, gap - 1, -1) if r > 0]
    for gap in range(1, count):
        down += [(r, r + gap, ("pick", r)) for r in range(middle, count - gap)]
    for s in [1] + list(range(count - 1, 1, -1)):
        late.append((0, s, ("moved", s)))
    for gap in range(1, count):
        late += [(r, r + gap, ("pick", r)) for r in range(1, min(middle, count - gap))]
    ready = {(0, ("stay", c)): 0 for c in range(chunks)}
    rounds = []
    while first or relays or down or late:
        now, senders, targets = [], set(), set()
        waiting = len(rounds) <= chunks
        for queue in (first, relays, down, [] if waiting else late):
            for move in list(queue):
                s, t, item = move
                known = item[0] != "stay" or ready.get((s, item), len(rounds) + 1) <= len(rounds)
                if known and s not in senders and t not in targets:
                    now.append(move)
                    senders.add(s)
                    targets.add(t)
                    queue.remove(move)
        for s, t, item in now:
            ready[t, item] = len(rounds) + 3
        rounds.append(now)
    return rounds


def pick_kernel(count, order, me_ref, pivot_ref, matrix_ref, *refs):
    outs, (rows_ref, pivot_v, sem) = refs[:-3], refs[-3:]
    rows, cols = matrix_ref.shape
    width = pivot_ref.shape[1]
    slot = width // count
    me = me_ref[0]
    point = pltpu.make_async_copy(pivot_ref, pivot_v, sem.at[0])
    head = pltpu.make_async_copy(matrix_ref.at[:width], rows_ref.at[:width], sem.at[1])
    tail = pltpu.make_async_copy(matrix_ref.at[width:], rows_ref.at[width:], sem.at[2])
    point.start()
    head.start()
    tail.start()
    point.wait()
    pivot = pivot_v[...]
    kind, place = classify(pivot, count, rows)
    head.wait()
    tail.wait()

    @pl.when(me == 0)
    def _():
        start = jnp.full(kind.shape, -count * width, jnp.int32)
        for k, (name, which) in enumerate(order):
            if name == "moved":
                start = jnp.where(kind == which, k * slot, start)
            else:
                inside = (kind == 0) & (place >= which * slot) & (place < (which + 1) * slot)
                start = jnp.where(inside, (k - which) * slot, start)
        got = picked(one_hot(start + place, len(order) * slot), rows_ref[:width, :])
        for k, out in enumerate(outs):
            out[...] = got[k * slot : (k + 1) * slot, :]

    @pl.when(me != 0)
    def _():
        mine = lax.broadcasted_iota(jnp.int32, (slot, width), 0) == jnp.where(kind == me, place, -1)
        source = jnp.sum(jnp.where(mine, pivot - me * rows, 0), axis=1, keepdims=True)
        pick = (lax.broadcasted_iota(jnp.int32, (slot, rows), 1) == source).astype(BF16)
        got = picked(pick, rows_ref[...])
        for out in outs:
            out[...] = got


def coefficient_kernel(count, me_ref, ids_ref, pivot_ref, inverse_ref, matrix_ref, *refs):
    shards = refs[:-8]
    base_ref, high_ref, low_ref, pivot_v, inv_ref, pan_ref, rows_ref, sem = refs[-8:]
    rows, cols = matrix_ref.shape
    width = pivot_ref.shape[1]
    slot = width // count
    stay = width // 2
    depth = shards[0].shape[0]
    total = stay + width
    me = me_ref[0]
    copies = [
        pltpu.make_async_copy(pivot_ref, pivot_v, sem.at[0]),
        pltpu.make_async_copy(inverse_ref, inv_ref, sem.at[1]),
        pltpu.make_async_copy(matrix_ref, rows_ref, sem.at[2]),
    ]
    for copy in copies:
        copy.start()
    for k, shard in enumerate(shards):
        pan_ref[pl.ds(pl.multiple_of(ids_ref[k] * depth, depth), depth), :] = shard[...]
    copies[0].wait()
    pivot = pivot_v[...]
    kind, place = classify(pivot, count, rows)
    spread = one_hot(jnp.where(kind == 0, place, stay + kind * slot + place), total)

    local_row = jnp.where((kind == me) & (kind != 0), pivot - me * rows, -1)
    landing = (lax.broadcasted_iota(jnp.int32, (rows, width), 0) == local_row).astype(BF16)
    mine = one_hot(jnp.where((kind == me) & (kind != 0), place, -1), slot)
    land = mm_nt(landing, mine)
    taken = jnp.sum(land, axis=1, keepdims=True)
    copies[1].wait()
    inv_high, inv_low = halves(inv_ref[...])
    col_high = mm_nt(inv_high, spread).astype(BF16)
    col_low = mm_nt(inv_low, spread).astype(BF16)
    copies[2].wait()
    base_ref[...] = jnp.where(taken > 0.5, 0.0, rows_ref[...])

    pan_high, pan_low = halves(pan_ref[...])
    value = mm_tn(pan_low, col_high) + mm_tn(pan_high, col_low) + mm_tn(pan_high, col_high)
    high, low = halves(-value)
    high_ref[...] = high
    low_ref[...] = low
    high_ref[:, stay : stay + slot] = land.astype(BF16)
    low_ref[:, stay : stay + slot] = jnp.zeros((rows, slot), BF16)

    @pl.when(me == 0)
    def _():
        high_ref[:width, :] = col_high
        low_ref[:width, :] = col_low
        base_ref[:width, :] = jnp.zeros((width, cols), F32)


def update_kernel(count, places, me_ref, base_ref, high_ref, low_ref, *refs):
    arrays, (out_ref, row_high, row_low) = refs[:-3], refs[-3:]
    slot = arrays[0].shape[0]
    me = me_ref[0]
    for r in range(count):

        @pl.when(me == r)
        def _(r=r):
            for block, k in enumerate(places[r]):
                part = pl.ds(block * slot, slot)
                if k is None:
                    row_high[part, :] = jnp.zeros(arrays[0].shape, BF16)
                    row_low[part, :] = jnp.zeros(arrays[0].shape, BF16)
                else:
                    row_high[part, :], row_low[part, :] = halves(arrays[k][...])

    high = high_ref[...]
    part = mm(low_ref[...], row_high[...]) + mm(high, row_low[...]) + mm(high, row_high[...])
    out_ref[...] = base_ref[...] + part


def gather_shards(shard, count):
    held, masks = [shard], [0]
    bits = []
    bit = 1
    while bit < count:
        bits.append(bit)
        bit *= 2
    while bits:
        group = [bits.pop()]
        if bits and bits[-1] > 1:
            group.append(bits.pop())
        steps = [group[0]] if len(group) == 1 else [group[0], group[1], group[0] | group[1]]
        new, new_masks = [], []
        for step in steps:
            pairs = [(i, i ^ step) for i in range(count)]
            for piece, mask in zip(held, masks):
                new.append(lax.ppermute(piece, "col", pairs))
                new_masks.append(mask ^ step)
        held, masks = held + new, masks + new_masks
    return held, masks


def local(row_count, col_count, matrix, panel_t, inverse_lower, pivot_rows):
    rows, cols = matrix.shape
    width = inverse_lower.shape[0]
    slot = width // row_count
    stay = width // 2
    me = lax.axis_index("row").astype(jnp.int32)
    column = lax.axis_index("col").astype(jnp.int32)
    here = me.reshape(1)
    pivot = pivot_rows.reshape(1, width)
    item_shape = jax.ShapeDtypeStruct((slot, cols), F32)

    rounds = plan(row_count)
    order = [item for moves in rounds for s, t, item in moves if s == 0]
    own = pl.pallas_call(
        functools.partial(pick_kernel, row_count, order),
        out_shape=(item_shape,) * len(order),
        in_specs=[SMEM, HBM, HBM],
        out_specs=(VMEM,) * len(order),
        scratch_shapes=[
            pltpu.VMEM((rows, cols), F32),
            pltpu.VMEM((1, width), jnp.int32),
            pltpu.SemaphoreType.DMA((3,)),
        ],
        compiler_params=PARAMS,
        name="pick",
    )(here, pivot, matrix)

    arrays = list(own)
    found = [{} for _ in range(row_count)]
    for k, item in enumerate(order):
        found[0][item] = k
    for r in range(1, row_count):
        found[r]["pick", r] = 0
    for moves in rounds:
        leaving = [item for s, t, item in moves if s == 0]
        operand = own[order.index(leaving[0])] if leaving else own[0]
        for s, t, item in moves:
            if s != 0 and item[0] == "stay":
                operand = jnp.where(me == s, arrays[found[s][item]], operand)
        for s, t, item in moves:
            found[t][item] = len(arrays)
        arrays.append(lax.ppermute(operand, "row", [(s, t) for s, t, item in moves]))
    blocks = [("stay", c) for c in range(row_count // 2)]
    places = [
        [found[r].get(item) for item in blocks + [("moved", r)] + [("pick", p) for p in range(1, row_count)]]
        for r in range(row_count)
    ]

    shards, masks = gather_shards(panel_t, col_count)
    ids = column ^ jnp.array(masks, jnp.int32)

    total = stay + width
    base, high, low = pl.pallas_call(
        functools.partial(coefficient_kernel, row_count),
        out_shape=(
            jax.ShapeDtypeStruct((rows, cols), F32),
            jax.ShapeDtypeStruct((rows, total), BF16),
            jax.ShapeDtypeStruct((rows, total), BF16),
        ),
        in_specs=[SMEM, SMEM, HBM, HBM, HBM] + [VMEM] * len(shards),
        out_specs=(VMEM,) * 3,
        scratch_shapes=[
            pltpu.VMEM((1, width), jnp.int32),
            pltpu.VMEM((width, width), F32),
            pltpu.VMEM((width, rows), F32),
            pltpu.VMEM((rows, cols), F32),
            pltpu.SemaphoreType.DMA((3,)),
        ],
        compiler_params=PARAMS,
        name="coefficients",
    )(here, ids, pivot, inverse_lower, matrix, *shards)

    return pl.pallas_call(
        functools.partial(update_kernel, row_count, places),
        out_shape=jax.ShapeDtypeStruct((rows, cols), F32),
        in_specs=[SMEM] + [VMEM] * (3 + len(arrays)),
        out_specs=VMEM,
        scratch_shapes=[pltpu.VMEM((total, cols), BF16), pltpu.VMEM((total, cols), BF16)],
        compiler_params=PARAMS,
        name="update",
    )(here, base, high, low, *arrays)


def solution(mesh):
    in_specs = (P("row", "col"), P("col", "row"), P(), P())
    out_specs = P("row", "col")
    return jax.shard_map(
        functools.partial(local, mesh.shape["row"], mesh.shape["col"]),
        mesh=mesh,
        in_specs=in_specs,
        out_specs=out_specs,
        check_vma=False,
    )
```

time: 57.9 us -> 51.1 us (0.88)
  the two profiles are of different devices: /device:TPU:23 before, /device:TPU:28 now
where the time goes in v2:
time: 51.1 us; the launch traced here: 50.8 us
  starting transfers between devices  23.5 us (46%)
  waiting for transfers between devices  14.2 us (28%)
  Pallas kernels  10.7 us (21%)
  local copies, waits for them, and re-layouts  1.98 us (4%)
    ppermute x7, starting transfers between devices, local(): lax.ppermute(operand, 'row', [(s, t) for s, t, item in moves])  19.4 us
    ppermute x7, waiting for transfers between devices, local(): lax.ppermute(operand, 'row', [(s, t) for s, t, item in moves])  14.2 us
    pallas_call x1, Pallas kernels, local(): pl.pallas_call(functools.partial(coefficient_kernel, row_count), out_shap...  6.41 us
    ppermute x7, starting transfers between devices, gather_shards(): new.append(lax.ppermute(piece, 'col', pairs))  4.12 us
    pallas_call x1, Pallas kernels, local(): pl.pallas_call(functools.partial(update_kernel, row_count, places), out_s...  3.23 us
    unnamed x14, local copies, waits for them, and re-layouts  1.98 us
    pallas_call x1, Pallas kernels, local(): pl.pallas_call(functools.partial(pick_kernel, row_count, order), out_shap...  1.08 us
  transfers between devices with their start and end apart: 14, of which 5 were waited for; matrix products, arithmetic and copies ran while one was open for 0% of the time, Pallas kernels for 13%

profile of v2, /device:TPU:28, one launch (start us, length us, event | category | flops | bytes accessed | tf_op | source)
XLA Modules:
  0.0 50.8 jit_solution(2588884290207557028)
XLA Ops:
  0.0 1.3 %copy-done = f32[768,384]{1,0:T(8,128)S(1)} copy-done((f32[768,384]{1,0:T(8,128)S(1)}, f32[768,384]{1,0:T(8,128)}, u32[]{:S(2)}) %copy-start) | copy-done | bytes 1179672
  1.3 0.7 %copy-done.4 = s32[512]{0:T(512)S(1)} copy-done((s32[512]{0:T(512)S(1)}, s32[512]{0:T(512)}, u32[]{:S(2)}) %copy-start.4) | copy-done | bytes 2072
  2.0 1.1 %pick.1 = (f32[128,384]{1,0:T(8,128)S(1)}, f32[128,384]{1,0:T(8,128)S(1)}, f32[128,384]{1,0:T(8,128)S(1)}, f32[128,384]{1,0:T(8,128)S(1)}, f32[128,384]{1,0:T(8,128)S(1)}) custom-call(s32[1]{0:T(128)} %bitcast.me_ref, s32[1,512]{1,0:T(1,128)S(1)} %bitcast.2, f32[768,384]{1,0:T(8,128)S(1)} %copy-done), custom_call_target="tpu_custom_call" | custom-call | tf_op jit(solution)/shard_map/pick/pallas_call | solution.py:255
  3.0 0.0 copy-start.6
  3.1 2.4 %collective-permute-start.8 = (f32[128,384]{1,0:T(8,128)S(1)}, f32[128,384]{1,0:T(8,128)S(1)}, u32[]{:S(2)}, u32[]{:S(2)}) collective-permute-start(f32[128,384]{1,0:T(8,128)S(1)} %get-tuple-element.17.refs_1_), channel_id=1, source_target_pairs={{0,16},{24,8},{16,0},{1,17},{25,9},{17,1},{2,18},{26,10},{18,2},{3... | collective-permute-start | bytes 589832 | tf_op jit(solution)/shard_map/ppermute | solution.py:283
  5.5 0.6 %collective-permute-start = (f32[64,768]{1,0:T(8,128)}, f32[64,768]{1,0:T(8,128)}, u32[]{:S(2)}, u32[]{:S(2)}) collective-permute-start(f32[64,768]{1,0:T(8,128)} %refs_0_.1), channel_id=1, source_target_pairs={{0,4},{1,5},{2,6},{3,7},{4,0},{5,1},{6,2},{7,3},{8,12},{9,13},{10,... | collective-permute-start | bytes 589832 | tf_op jit(solution)/shard_map/ppermute | solution.py:236
  6.0 1.5 %collective-permute-start.1 = (f32[64,768]{1,0:T(8,128)}, f32[64,768]{1,0:T(8,128)}, u32[]{:S(2)}, u32[]{:S(2)}) collective-permute-start(f32[64,768]{1,0:T(8,128)} %refs_0_.1), channel_id=1, source_target_pairs={{0,2},{1,3},{2,0},{3,1},{4,6},{5,7},{6,4},{7,5},{8,10},{9,11},{10,... | collective-permute-start | bytes 589832 | tf_op jit(solution)/shard_map/ppermute | solution.py:236
  7.5 1.5 %collective-permute-start.2 = (f32[64,768]{1,0:T(8,128)}, f32[64,768]{1,0:T(8,128)}, u32[]{:S(2)}, u32[]{:S(2)}) collective-permute-start(f32[64,768]{1,0:T(8,128)} %refs_0_.1), channel_id=1, source_target_pairs={{0,6},{1,7},{2,4},{3,5},{4,2},{5,3},{6,0},{7,1},{8,14},{9,15},{10,... | collective-permute-start | bytes 589832 | tf_op jit(solution)/shard_map/ppermute | solution.py:236
  9.0 0.6 %collective-permute-done.8.refs_6_ = f32[128,384]{1,0:T(8,128)S(1)} collective-permute-done((f32[128,384]{1,0:T(8,128)S(1)}, f32[128,384]{1,0:T(8,128)S(1)}, u32[]{:S(2)}, u32[]{:S(2)}) %collective-permute-start.8) | collective-permute-done | bytes 196640 | tf_op jit(solution)/shard_map/ppermute | solution.py:283
  9.7 9.9 %collective-permute-start.7 = (f32[128,384]{1,0:T(8,128)S(1)}, f32[128,384]{1,0:T(8,128)S(1)}, u32[]{:S(2)}, u32[]{:S(2)}) collective-permute-start(f32[128,384]{1,0:T(8,128)S(1)} %get-tuple-element.16.refs_0_), channel_id=1, source_target_pairs={{0,16},{24,0},{16,8},{1,17},{25,1},{17,9},{2,18},{26,2},{18,10},{3... | collective-permute-start | bytes 589832 | tf_op jit(solution)/shard_map/ppermute | solution.py:283
  19.7 1.9 %collective-permute-start.9 = (f32[128,384]{1,0:T(8,128)S(1)}, f32[128,384]{1,0:T(8,128)S(1)}, u32[]{:S(2)}, u32[]{:S(2)}) collective-permute-start(f32[128,384]{1,0:T(8,128)S(1)} %get-tuple-element.16.refs_0_), channel_id=1, source_target_pairs={{24,16},{8,0},{16,24},{25,17},{9,1},{17,25},{26,18},{10,2},{18,26}... | collective-permute-start | bytes 589832 | tf_op jit(solution)/shard_map/ppermute | solution.py:283
  21.6 0.1 collective-permute-start.4
  21.7 0.5 collective-permute-start.5
  22.2 2.8 %collective-permute-done.7.refs_5_ = f32[128,384]{1,0:T(8,128)S(1)} collective-permute-done((f32[128,384]{1,0:T(8,128)S(1)}, f32[128,384]{1,0:T(8,128)S(1)}, u32[]{:S(2)}, u32[]{:S(2)}) %collective-permute-start.7) | collective-permute-done | bytes 196640 | tf_op jit(solution)/shard_map/ppermute | solution.py:283
  25.0 0.1 broadcast_select_fusion.2
  25.0 1.3 %collective-permute-start.10 = (f32[128,384]{1,0:T(8,128)S(1)}, f32[128,384]{1,0:T(8,128)S(1)}, u32[]{:S(2)}, u32[]{:S(2)}) collective-permute-start(f32[128,384]{1,0:T(8,128)S(1)} %get-tuple-element.24), channel_id=1, source_target_pairs={{16,24},{0,8},{8,16},{17,25},{1,9},{9,17},{18,26},{2,10},{10,18},{... | collective-permute-start | bytes 589832 | tf_op jit(solution)/shard_map/ppermute | solution.py:283
  26.3 1.3 %collective-permute-start.11 = (f32[128,384]{1,0:T(8,128)S(1)}, f32[128,384]{1,0:T(8,128)S(1)}, u32[]{:S(2)}, u32[]{:S(2)}) collective-permute-start(f32[128,384]{1,0:T(8,128)S(1)} %get-tuple-element.23), channel_id=1, source_target_pairs={{16,8},{0,24},{17,9},{1,25},{18,10},{2,26},{19,11},{3,27},{20,12},... | collective-permute-start | bytes 589832 | tf_op jit(solution)/shard_map/ppermute | solution.py:283
  27.6 1.3 %collective-permute-start.12 = (f32[128,384]{1,0:T(8,128)S(1)}, f32[128,384]{1,0:T(8,128)S(1)}, u32[]{:S(2)}, u32[]{:S(2)}) collective-permute-start(f32[128,384]{1,0:T(8,128)S(1)} %get-tuple-element.22), channel_id=1, source_target_pairs={{16,24},{0,16},{17,25},{1,17},{18,26},{2,18},{19,27},{3,19},{20,28... | collective-permute-start | bytes 589832 | tf_op jit(solution)/shard_map/ppermute | solution.py:283
  29.0 1.3 %collective-permute-start.13 = (f32[128,384]{1,0:T(8,128)S(1)}, f32[128,384]{1,0:T(8,128)S(1)}, u32[]{:S(2)}, u32[]{:S(2)}) collective-permute-start(f32[128,384]{1,0:T(8,128)S(1)} %get-tuple-element.21), channel_id=1, source_target_pairs={{16,8},{8,24},{17,9},{9,25},{18,10},{10,26},{19,11},{11,27},{20,12... | collective-permute-start | bytes 589832 | tf_op jit(solution)/shard_map/ppermute | solution.py:283
  30.3 6.4 %coefficients.1 = (f32[768,384]{1,0:T(8,128)S(1)}, bf16[768,768]{1,0:T(8,128)(2,1)S(1)}, bf16[768,768]{1,0:T(8,128)(2,1)S(1)}) custom-call(s32[1]{0:T(128)} %bitcast.me_ref, s32[8]{0:T(128)S(1)} %broadcast_xor_fusion.ids_ref, s32[1,512]{1,0:T(1,128)S(1)} %bitcast.3, f32[512,512]{1,0:T(8,128)S(1)} %copy-done.2, f32[768,384]{1,0:T(8,128)S(1)} %copy-done.1, ...), custom_call_target="tpu_custom_call" | custom-call | tf_op jit(solution)/shard_map/coefficients/pallas_call | solution.py:294
  36.8 3.9 %collective-permute-done.11.refs_9_ = f32[128,384]{1,0:T(8,128)S(1)} collective-permute-done((f32[128,384]{1,0:T(8,128)S(1)}, f32[128,384]{1,0:T(8,128)S(1)}, u32[]{:S(2)}, u32[]{:S(2)}) %collective-permute-start.11) | collective-permute-done | bytes 196640 | tf_op jit(solution)/shard_map/ppermute | solution.py:283
  40.6 3.4 %collective-permute-done.12.refs_10_ = f32[128,384]{1,0:T(8,128)S(1)} collective-permute-done((f32[128,384]{1,0:T(8,128)S(1)}, f32[128,384]{1,0:T(8,128)S(1)}, u32[]{:S(2)}, u32[]{:S(2)}) %collective-permute-start.12) | collective-permute-done | bytes 196640 | tf_op jit(solution)/shard_map/ppermute | solution.py:283
  44.0 3.5 %collective-permute-done.13.refs_11_ = f32[128,384]{1,0:T(8,128)S(1)} collective-permute-done((f32[128,384]{1,0:T(8,128)S(1)}, f32[128,384]{1,0:T(8,128)S(1)}, u32[]{:S(2)}, u32[]{:S(2)}) %collective-permute-start.13) | collective-permute-done | bytes 196640 | tf_op jit(solution)/shard_map/ppermute | solution.py:283
  47.5 3.2 %update.1 = f32[768,384]{1,0:T(8,128)} custom-call(s32[1]{0:T(128)} %bitcast.me_ref, f32[768,384]{1,0:T(8,128)S(1)} %get-tuple-element.13.base_ref, bf16[768,768]{1,0:T(8,128)(2,1)S(1)} %get-tuple-element.14.high_ref, bf16[768,768]{1,0:T(8,128)(2,1)S(1)} %get-tuple-element.15.low_ref, f32[128,384]{1,0:T(8,128)S(1)} %get-tuple-element.16.refs_0_, ...), custom_call_target="tpu_custom_call" | custom-call | tf_op jit(solution)/shard_map/update/pallas_call | solution.py:314
  (24 shorter events, 0.1 us)
Async XLA Ops:
  0.0 1.3 %copy-start = (f32[768,384]{1,0:T(8,128)S(1)}, f32[768,384]{1,0:T(8,128)}, u32[]{:S(2)}) copy-start(f32[768,384]{1,0:T(8,128)} %matrix_ref.3) | copy-start | bytes 3538948
  1.3 0.7 %copy-start.4 = (s32[512]{0:T(512)S(1)}, s32[512]{0:T(512)}, u32[]{:S(2)}) copy-start(s32[512]{0:T(512)} %param.8) | copy-start | bytes 6148
  2.0 28.3 %copy-start.2 = (f32[512,512]{1,0:T(8,128)S(1)}, f32[512,512]{1,0:T(8,128)}, u32[]{:S(2)}) copy-start(f32[512,512]{1,0:T(8,128)} %inverse_ref.1) | copy-start | bytes 3145732
  3.0 27.2 %copy-start.6 = (s32[8]{0:T(128)S(1)}, s32[8]{0:T(128)}, u32[]{:S(2)}) copy-start(s32[8]{0:T(128)} %constant.12.clone) | copy-start | bytes 100
  3.1 27.2 %copy-start.1 = (f32[768,384]{1,0:T(8,128)S(1)}, f32[768,384]{1,0:T(8,128)}, u32[]{:S(2)}) copy-start(f32[768,384]{1,0:T(8,128)} %matrix_ref.3) | copy-start | bytes 3538948
  3.1 27.2 %copy-start.5 = (s32[512]{0:T(512)S(1)}, s32[512]{0:T(512)}, u32[]{:S(2)}) copy-start(s32[512]{0:T(512)} %param.8) | copy-start | bytes 6148
  3.1 6.6 %collective-permute-start.8 = (f32[128,384]{1,0:T(8,128)S(1)}, f32[128,384]{1,0:T(8,128)S(1)}, u32[]{:S(2)}, u32[]{:S(2)}) collective-permute-start(f32[128,384]{1,0:T(8,128)S(1)} %get-tuple-element.17.refs_1_), channel_id=1, source_target_pairs={{0,16},{24,8},{16,0},{1,17},{25,9},{17,1},{2,18},{26,10},{18,2},{3... | collective-permute-start | bytes 589832 | tf_op jit(solution)/shard_map/ppermute | solution.py:283
  5.5 14.2 %collective-permute-start = (f32[64,768]{1,0:T(8,128)}, f32[64,768]{1,0:T(8,128)}, u32[]{:S(2)}, u32[]{:S(2)}) collective-permute-start(f32[64,768]{1,0:T(8,128)} %refs_0_.1), channel_id=1, source_target_pairs={{0,4},{1,5},{2,6},{3,7},{4,0},{5,1},{6,2},{7,3},{8,12},{9,13},{10,... | collective-permute-start | bytes 589832 | tf_op jit(solution)/shard_map/ppermute | solution.py:236
  6.0 15.5 %collective-permute-start.1 = (f32[64,768]{1,0:T(8,128)}, f32[64,768]{1,0:T(8,128)}, u32[]{:S(2)}, u32[]{:S(2)}) collective-permute-start(f32[64,768]{1,0:T(8,128)} %refs_0_.1), channel_id=1, source_target_pairs={{0,2},{1,3},{2,0},{3,1},{4,6},{5,7},{6,4},{7,5},{8,10},{9,11},{10,... | collective-permute-start | bytes 589832 | tf_op jit(solution)/shard_map/ppermute | solution.py:236
  7.5 14.1 %collective-permute-start.2 = (f32[64,768]{1,0:T(8,128)}, f32[64,768]{1,0:T(8,128)}, u32[]{:S(2)}, u32[]{:S(2)}) collective-permute-start(f32[64,768]{1,0:T(8,128)} %refs_0_.1), channel_id=1, source_target_pairs={{0,6},{1,7},{2,4},{3,5},{4,2},{5,3},{6,0},{7,1},{8,14},{9,15},{10,... | collective-permute-start | bytes 589832 | tf_op jit(solution)/shard_map/ppermute | solution.py:236
  9.0 16.0 %collective-permute-start.3 = (f32[64,768]{1,0:T(8,128)}, f32[64,768]{1,0:T(8,128)}, u32[]{:S(2)}, u32[]{:S(2)}) collective-permute-start(f32[64,768]{1,0:T(8,128)} %refs_0_.1), channel_id=1, source_target_pairs={{0,1},{1,0},{2,3},{3,2},{4,5},{5,4},{6,7},{7,6},{8,9},{9,8},{10,11... | collective-permute-start | bytes 589832 | tf_op jit(solution)/shard_map/ppermute | solution.py:236
  9.0 21.3 %copy-start.3 = (f32[64,768]{1,0:T(8,128)S(1)}, f32[64,768]{1,0:T(8,128)}, u32[]{:S(2)}) copy-start(f32[64,768]{1,0:T(8,128)} %refs_0_.1) | copy-start | bytes 589828
  9.7 15.3 %collective-permute-start.7 = (f32[128,384]{1,0:T(8,128)S(1)}, f32[128,384]{1,0:T(8,128)S(1)}, u32[]{:S(2)}, u32[]{:S(2)}) collective-permute-start(f32[128,384]{1,0:T(8,128)S(1)} %get-tuple-element.16.refs_0_), channel_id=1, source_target_pairs={{0,16},{24,0},{16,8},{1,17},{25,1},{17,9},{2,18},{26,2},{18,10},{3... | collective-permute-start | bytes 589832 | tf_op jit(solution)/shard_map/ppermute | solution.py:283
  19.7 17.1 %collective-permute-start.9 = (f32[128,384]{1,0:T(8,128)S(1)}, f32[128,384]{1,0:T(8,128)S(1)}, u32[]{:S(2)}, u32[]{:S(2)}) collective-permute-start(f32[128,384]{1,0:T(8,128)S(1)} %get-tuple-element.16.refs_0_), channel_id=1, source_target_pairs={{24,16},{8,0},{16,24},{25,17},{9,1},{17,25},{26,18},{10,2},{18,26}... | collective-permute-start | bytes 589832 | tf_op jit(solution)/shard_map/ppermute | solution.py:283
  21.6 4.7 %collective-permute-start.4 = (f32[64,768]{1,0:T(8,128)}, f32[64,768]{1,0:T(8,128)S(1)}, u32[]{:S(2)}, u32[]{:S(2)}) collective-permute-start(f32[64,768]{1,0:T(8,128)} %collective-permute-done.refs_1_), channel_id=1, source_target_pairs={{0,1},{1,0},{2,3},{3,2},{4,5},{5,4},{6,7},{7,6},{8,9},{9,8},{10,11... | collective-permute-start | bytes 589832 | tf_op jit(solution)/shard_map/ppermute | solution.py:236
  21.7 5.9 %collective-permute-start.5 = (f32[64,768]{1,0:T(8,128)}, f32[64,768]{1,0:T(8,128)S(1)}, u32[]{:S(2)}, u32[]{:S(2)}) collective-permute-start(f32[64,768]{1,0:T(8,128)} %collective-permute-done.1.refs_2_), channel_id=1, source_target_pairs={{0,1},{1,0},{2,3},{3,2},{4,5},{5,4},{6,7},{7,6},{8,9},{9,8},{10,11... | collective-permute-start | bytes 589832 | tf_op jit(solution)/shard_map/ppermute | solution.py:236
  25.0 4.0 %collective-permute-start.6 = (f32[64,768]{1,0:T(8,128)}, f32[64,768]{1,0:T(8,128)S(1)}, u32[]{:S(2)}, u32[]{:S(2)}) collective-permute-start(f32[64,768]{1,0:T(8,128)} %collective-permute-done.2.refs_3_), channel_id=1, source_target_pairs={{0,1},{1,0},{2,3},{3,2},{4,5},{5,4},{6,7},{7,6},{8,9},{9,8},{10,11... | collective-permute-start | bytes 589832 | tf_op jit(solution)/shard_map/ppermute | solution.py:236
  25.0 11.7 %collective-permute-start.10 = (f32[128,384]{1,0:T(8,128)S(1)}, f32[128,384]{1,0:T(8,128)S(1)}, u32[]{:S(2)}, u32[]{:S(2)}) collective-permute-start(f32[128,384]{1,0:T(8,128)S(1)} %get-tuple-element.24), channel_id=1, source_target_pairs={{16,24},{0,8},{8,16},{17,25},{1,9},{9,17},{18,26},{2,10},{10,18},{... | collective-permute-start | bytes 589832 | tf_op jit(solution)/shard_map/ppermute | solution.py:283
  26.3 14.3 %collective-permute-start.11 = (f32[128,384]{1,0:T(8,128)S(1)}, f32[128,384]{1,0:T(8,128)S(1)}, u32[]{:S(2)}, u32[]{:S(2)}) collective-permute-start(f32[128,384]{1,0:T(8,128)S(1)} %get-tuple-element.23), channel_id=1, source_target_pairs={{16,8},{0,24},{17,9},{1,25},{18,10},{2,26},{19,11},{3,27},{20,12},... | collective-permute-start | bytes 589832 | tf_op jit(solution)/shard_map/ppermute | solution.py:283
  27.6 16.4 %collective-permute-start.12 = (f32[128,384]{1,0:T(8,128)S(1)}, f32[128,384]{1,0:T(8,128)S(1)}, u32[]{:S(2)}, u32[]{:S(2)}) collective-permute-start(f32[128,384]{1,0:T(8,128)S(1)} %get-tuple-element.22), channel_id=1, source_target_pairs={{16,24},{0,16},{17,25},{1,17},{18,26},{2,18},{19,27},{3,19},{20,28... | collective-permute-start | bytes 589832 | tf_op jit(solution)/shard_map/ppermute | solution.py:283
  29.0 18.6 %collective-permute-start.13 = (f32[128,384]{1,0:T(8,128)S(1)}, f32[128,384]{1,0:T(8,128)S(1)}, u32[]{:S(2)}, u32[]{:S(2)}) collective-permute-start(f32[128,384]{1,0:T(8,128)S(1)} %get-tuple-element.21), channel_id=1, source_target_pairs={{16,8},{8,24},{17,9},{9,25},{18,10},{10,26},{19,11},{11,27},{20,12... | collective-permute-start | bytes 589832 | tf_op jit(solution)/shard_map/ppermute | solution.py:283

commit v3 on v2

--- a/solution.py
+++ b/solution.py
@@ -11,7 +11,9 @@
 BF16 = jnp.bfloat16
 VMEM = pl.BlockSpec(memory_space=pltpu.VMEM)
 SMEM = pl.BlockSpec(memory_space=pltpu.SMEM)
+ANY = pl.BlockSpec(memory_space=pl.ANY)
 HBM = pl.BlockSpec(memory_space=pltpu.HBM)
+LONG = pl.CostEstimate(flops=40_000_000_000, transcendentals=0, bytes_accessed=100_000_000)
 PARAMS = pltpu.CompilerParams(vmem_limit_bytes=20 * 1024 * 1024)
 
 
@@ -104,8 +106,8 @@
     return rounds
 
 
-def pick_kernel(count, order, me_ref, pivot_ref, matrix_ref, *refs):
-    outs, (rows_ref, pivot_v, sem) = refs[:-3], refs[-3:]
+def pick_kernel(count, order, me_ref, pivot_ref, matrix_ref, panel_ref, *refs):
+    outs, (panel_out, rows_ref, pivot_v, sem) = refs[:-4], refs[-4:]
     rows, cols = matrix_ref.shape
     width = pivot_ref.shape[1]
     slot = width // count
@@ -113,9 +115,11 @@
     point = pltpu.make_async_copy(pivot_ref, pivot_v, sem.at[0])
     head = pltpu.make_async_copy(matrix_ref.at[:width], rows_ref.at[:width], sem.at[1])
     tail = pltpu.make_async_copy(matrix_ref.at[width:], rows_ref.at[width:], sem.at[2])
+    panel = pltpu.make_async_copy(panel_ref, panel_out, sem.at[3])
     point.start()
     head.start()
     tail.start()
+    panel.start()
     point.wait()
     pivot = pivot_v[...]
     kind, place = classify(pivot, count, rows)
@@ -144,16 +148,15 @@
         for out in outs:
             out[...] = got
 
-
-def coefficient_kernel(count, me_ref, ids_ref, pivot_ref, inverse_ref, matrix_ref, *refs):
-    shards = refs[:-8]
-    base_ref, high_ref, low_ref, pivot_v, inv_ref, pan_ref, rows_ref, sem = refs[-8:]
+    panel.wait()
+
+
+def prepare_kernel(count, me_ref, pivot_ref, inverse_ref, matrix_ref, *refs):
+    high_ref, low_ref, land_ref, base_ref, pivot_v, inv_ref, rows_ref, sem = refs[-8:]
     rows, cols = matrix_ref.shape
     width = pivot_ref.shape[1]
     slot = width // count
     stay = width // 2
-    depth = shards[0].shape[0]
-    total = stay + width
     me = me_ref[0]
     copies = [
         pltpu.make_async_copy(pivot_ref, pivot_v, sem.at[0]),
@@ -162,41 +165,32 @@
     ]
     for copy in copies:
         copy.start()
-    for k, shard in enumerate(shards):
-        pan_ref[pl.ds(pl.multiple_of(ids_ref[k] * depth, depth), depth), :] = shard[...]
     copies[0].wait()
     pivot = pivot_v[...]
     kind, place = classify(pivot, count, rows)
-    spread = one_hot(jnp.where(kind == 0, place, stay + kind * slot + place), total)
-
-    local_row = jnp.where((kind == me) & (kind != 0), pivot - me * rows, -1)
-    landing = (lax.broadcasted_iota(jnp.int32, (rows, width), 0) == local_row).astype(BF16)
-    mine = one_hot(jnp.where((kind == me) & (kind != 0), place, -1), slot)
-    land = mm_nt(landing, mine)
+    spread = one_hot(jnp.where(kind == 0, place, stay + (kind - 1) * slot + place), high_ref.shape[1])
+    mine = (kind == me) & (kind != 0)
+    landing = lax.broadcasted_iota(jnp.int32, (rows, width), 0) == jnp.where(mine, pivot - me * rows, -1)
+    land = mm_nt(landing.astype(BF16), one_hot(jnp.where(mine, place, -1), slot))
+    land_ref[...] = land.astype(BF16)
     taken = jnp.sum(land, axis=1, keepdims=True)
     copies[1].wait()
     inv_high, inv_low = halves(inv_ref[...])
-    col_high = mm_nt(inv_high, spread).astype(BF16)
-    col_low = mm_nt(inv_low, spread).astype(BF16)
+    high_ref[...] = mm_nt(inv_high, spread).astype(BF16)
+    low_ref[...] = mm_nt(inv_low, spread).astype(BF16)
     copies[2].wait()
     base_ref[...] = jnp.where(taken > 0.5, 0.0, rows_ref[...])
 
-    pan_high, pan_low = halves(pan_ref[...])
-    value = mm_tn(pan_low, col_high) + mm_tn(pan_high, col_low) + mm_tn(pan_high, col_high)
-    high, low = halves(-value)
-    high_ref[...] = high
-    low_ref[...] = low
-    high_ref[:, stay : stay + slot] = land.astype(BF16)
-    low_ref[:, stay : stay + slot] = jnp.zeros((rows, slot), BF16)
-
-    @pl.when(me == 0)
-    def _():
-        high_ref[:width, :] = col_high
-        low_ref[:width, :] = col_low
-        base_ref[:width, :] = jnp.zeros((width, cols), F32)
-
-
-def update_kernel(count, places, me_ref, base_ref, high_ref, low_ref, *refs):
+
+def turn_kernel(near_ref, far_ref, high_ref, low_ref):
+    half = near_ref.shape[0]
+    for k, part in enumerate((near_ref, far_ref)):
+        high, low = halves(-part[...])
+        high_ref[:, k * half : (k + 1) * half] = high.T
+        low_ref[:, k * half : (k + 1) * half] = low.T
+
+
+def upper_kernel(count, places, me_ref, high_ref, low_ref, *refs):
     arrays, (out_ref, row_high, row_low) = refs[:-3], refs[-3:]
     slot = arrays[0].shape[0]
     me = me_ref[0]
@@ -206,37 +200,79 @@
         def _(r=r):
             for block, k in enumerate(places[r]):
                 part = pl.ds(block * slot, slot)
-                if k is None:
-                    row_high[part, :] = jnp.zeros(arrays[0].shape, BF16)
-                    row_low[part, :] = jnp.zeros(arrays[0].shape, BF16)
-                else:
-                    row_high[part, :], row_low[part, :] = halves(arrays[k][...])
+                row_high[part, :], row_low[part, :] = halves(arrays[k][...])
 
     high = high_ref[...]
-    part = mm(low_ref[...], row_high[...]) + mm(high, row_low[...]) + mm(high, row_high[...])
-    out_ref[...] = base_ref[...] + part
-
-
-def gather_shards(shard, count):
-    held, masks = [shard], [0]
-    bits = []
+    out_ref[...] = mm(low_ref[...], row_high[...]) + mm(high, row_low[...]) + mm(high, row_high[...])
+
+
+def update_kernel(places, me_ref, ids_ref, base_ref, land_ref, high_ref, low_ref, upper_ref, *refs):
+    arrays, (out_ref, up_high, up_low, row_high, row_low) = refs[:-5], refs[-5:]
+    width = upper_ref.shape[0]
+    me = me_ref[0]
+    depth = width // ids_ref.shape[0]
+    for k in range(ids_ref.shape[0]):
+        source = pl.multiple_of(ids_ref[k] * depth, depth)
+        part = pl.ds(k * depth, depth)
+        up_high[part, :], up_low[part, :] = halves(upper_ref[pl.ds(source, depth), :])
+    for r, k in enumerate(places):
+
+        @pl.when(me == r)
+        def _(k=k):
+            if k is None:
+                row_high[...] = jnp.zeros(row_high.shape, BF16)
+                row_low[...] = jnp.zeros(row_low.shape, BF16)
+            else:
+                row_high[...], row_low[...] = halves(arrays[k][...])
+
+    high, land = high_ref[...], land_ref[...]
+    part = mm(low_ref[...], up_high[...]) + mm(high, up_low[...]) + mm(high, up_high[...])
+    out_ref[...] = base_ref[...] + (mm(land, row_low[...]) + mm(land, row_high[...]) + part)
+
+    @pl.when(me == 0)
+    def _():
+        out_ref[:width, :] = upper_ref[...]
+
+
+def join_kernel(first, second, *refs):
+    out, sem = refs[-2:]
+    rows = first.shape[0]
+    copies = [
+        pltpu.make_async_copy(first, out.at[:rows], sem.at[0]),
+        pltpu.make_async_copy(second, out.at[rows:], sem.at[1]),
+    ]
+    for copy in copies:
+        copy.start()
+    for copy in copies:
+        copy.wait()
+
+
+def join(first, second, afters):
+    rows, cols = first.shape
+    return pl.pallas_call(
+        join_kernel,
+        out_shape=jax.ShapeDtypeStruct((2 * rows, cols), first.dtype),
+        in_specs=[VMEM, VMEM] + [ANY] * len(afters),
+        out_specs=VMEM,
+        scratch_shapes=[pltpu.SemaphoreType.DMA((2,))],
+        compiler_params=PARAMS,
+        name="join",
+    )(first, second, *afters)
+
+
+def gather_shards(shard, count, afters):
+    held, masks = shard, [0]
     bit = 1
-    while bit < count:
-        bits.append(bit)
+    while 2 * bit < count:
         bit *= 2
-    while bits:
-        group = [bits.pop()]
-        if bits and bits[-1] > 1:
-            group.append(bits.pop())
-        steps = [group[0]] if len(group) == 1 else [group[0], group[1], group[0] | group[1]]
-        new, new_masks = [], []
-        for step in steps:
-            pairs = [(i, i ^ step) for i in range(count)]
-            for piece, mask in zip(held, masks):
-                new.append(lax.ppermute(piece, "col", pairs))
-                new_masks.append(mask ^ step)
-        held, masks = held + new, masks + new_masks
-    return held, masks
+    while bit:
+        other = lax.ppermute(held, "col", [(i, i ^ bit) for i in range(count)])
+        masks += [mask ^ bit for mask in masks]
+        if bit > 1:
+            held = join(held, other, afters[0])
+            afters = afters[1:] or afters
+        bit //= 2
+    return held, other, masks
 
 
 def local(row_count, col_count, matrix, panel_t, inverse_lower, pivot_rows):
@@ -252,19 +288,23 @@
 
     rounds = plan(row_count)
     order = [item for moves in rounds for s, t, item in moves if s == 0]
-    own = pl.pallas_call(
+    matrix = pltpu.with_memory_space_constraint(matrix, pltpu.HBM)
+    pivot = pltpu.with_memory_space_constraint(pivot, pltpu.HBM)
+    panel_t = pltpu.with_memory_space_constraint(panel_t, pltpu.HBM)
+    inverse_lower = pltpu.with_memory_space_constraint(inverse_lower, pltpu.HBM)
+    *own, panel = pl.pallas_call(
         functools.partial(pick_kernel, row_count, order),
-        out_shape=(item_shape,) * len(order),
-        in_specs=[SMEM, HBM, HBM],
-        out_specs=(VMEM,) * len(order),
+        out_shape=(item_shape,) * len(order) + (jax.ShapeDtypeStruct(panel_t.shape, F32),),
+        in_specs=[SMEM, HBM, HBM, HBM],
+        out_specs=(VMEM,) * (len(order) + 1),
         scratch_shapes=[
             pltpu.VMEM((rows, cols), F32),
             pltpu.VMEM((1, width), jnp.int32),
-            pltpu.SemaphoreType.DMA((3,)),
+            pltpu.SemaphoreType.DMA((4,)),
         ],
         compiler_params=PARAMS,
         name="pick",
-    )(here, pivot, matrix)
+    )(here, pivot, matrix, panel_t)
 
     arrays = list(own)
     found = [{} for _ in range(row_count)]
@@ -281,45 +321,64 @@
         for s, t, item in moves:
             found[t][item] = len(arrays)
         arrays.append(lax.ppermute(operand, "row", [(s, t) for s, t, item in moves]))
-    blocks = [("stay", c) for c in range(row_count // 2)]
-    places = [
-        [found[r].get(item) for item in blocks + [("moved", r)] + [("pick", p) for p in range(1, row_count)]]
-        for r in range(row_count)
-    ]
-
-    shards, masks = gather_shards(panel_t, col_count)
-    ids = column ^ jnp.array(masks, jnp.int32)
-
-    total = stay + width
-    base, high, low = pl.pallas_call(
-        functools.partial(coefficient_kernel, row_count),
+    received = arrays[len(own) :]
+    blocks = [("stay", c) for c in range(row_count // 2)] + [("pick", p) for p in range(1, row_count)]
+    places = [[found[r][item] for item in blocks] for r in range(row_count)]
+    landed = [found[r].get(("moved", r)) for r in range(row_count)]
+
+    picked_rows = len(blocks) * slot
+    inv_high, inv_low, land, base = pl.pallas_call(
+        functools.partial(prepare_kernel, row_count),
         out_shape=(
+            jax.ShapeDtypeStruct((width, picked_rows), BF16),
+            jax.ShapeDtypeStruct((width, picked_rows), BF16),
+            jax.ShapeDtypeStruct((rows, slot), BF16),
             jax.ShapeDtypeStruct((rows, cols), F32),
-            jax.ShapeDtypeStruct((rows, total), BF16),
-            jax.ShapeDtypeStruct((rows, total), BF16),
         ),
-        in_specs=[SMEM, SMEM, HBM, HBM, HBM] + [VMEM] * len(shards),
-        out_specs=(VMEM,) * 3,
+        in_specs=[SMEM, HBM, HBM, HBM] + [ANY] * 2,
+        out_specs=(VMEM,) * 4,
         scratch_shapes=[
             pltpu.VMEM((1, width), jnp.int32),
             pltpu.VMEM((width, width), F32),
-            pltpu.VMEM((width, rows), F32),
             pltpu.VMEM((rows, cols), F32),
             pltpu.SemaphoreType.DMA((3,)),
         ],
         compiler_params=PARAMS,
-        name="coefficients",
-    )(here, ids, pivot, inverse_lower, matrix, *shards)
+        cost_estimate=LONG,
+        name="prepare",
+    )(here, pivot, inverse_lower, matrix, *received[1:3])
+
+    near, far, masks = gather_shards(panel, col_count, [received[:1], []])
+    ids = column ^ jnp.array(masks, jnp.int32)
+
+    upper = pl.pallas_call(
+        functools.partial(upper_kernel, row_count, places),
+        out_shape=jax.ShapeDtypeStruct((width, cols), F32),
+        in_specs=[SMEM] + [VMEM] * (2 + len(arrays)),
+        out_specs=VMEM,
+        scratch_shapes=[pltpu.VMEM((picked_rows, cols), BF16)] * 2,
+        compiler_params=PARAMS,
+        name="upper",
+    )(here, inv_high, inv_low, *arrays)
+
+    pan_high, pan_low = pl.pallas_call(
+        turn_kernel,
+        out_shape=(jax.ShapeDtypeStruct((rows, width), BF16),) * 2,
+        in_specs=[VMEM, VMEM],
+        out_specs=(VMEM, VMEM),
+        compiler_params=PARAMS,
+        name="turn",
+    )(near, far)
 
     return pl.pallas_call(
-        functools.partial(update_kernel, row_count, places),
+        functools.partial(update_kernel, landed),
         out_shape=jax.ShapeDtypeStruct((rows, cols), F32),
-        in_specs=[SMEM] + [VMEM] * (3 + len(arrays)),
+        in_specs=[SMEM, SMEM] + [VMEM] * (5 + len(arrays)),
         out_specs=VMEM,
-        scratch_shapes=[pltpu.VMEM((total, cols), BF16), pltpu.VMEM((total, cols), BF16)],
+        scratch_shapes=[pltpu.VMEM((width, cols), BF16)] * 2 + [pltpu.VMEM((slot, cols), BF16)] * 2,
         compiler_params=PARAMS,
         name="update",
-    )(here, base, high, low, *arrays)
+    )(here, ids, base, land, pan_high, pan_low, upper, *arrays)
 
 
 def solution(mesh):

time: 51.1 us -> 42.3 us (0.83)
  starting transfers between devices: 23.5 us -> 16.5 us
  local copies, waits for them, and re-layouts: 1.98 us -> 0.01 us
    ppermute x7 -> x3, waiting for transfers between devices: 0.02 us -> 5.52 us  [gather_shards(): other = lax.ppermute(held, 'col', [(i, i ^ bit) for i in range(count)])]
    ppermute x7, waiting for transfers between devices: 14.2 us -> 8.69 us  [local(): lax.ppermute(operand, 'row', [(s, t) for s, t, item in moves])]
    ppermute x7, starting transfers between devices: 19.4 us -> 14.3 us  [local(): lax.ppermute(operand, 'row', [(s, t) for s, t, item in moves])]
    unnamed x14 -> x2, local copies, waits for them, and re-layouts: 1.98 us -> 0.01 us
    ppermute x7 -> x3, starting transfers between devices: 4.12 us -> 2.19 us  [gather_shards(): other = lax.ppermute(held, 'col', [(i, i ^ bit) for i in range(count)])]
    pallas_call x1, Pallas kernels: 1.08 us -> 1.92 us  [local(): pl.pallas_call(functools.partial(pick_kernel, row_count, order), out_shap...]
    pallas_call x2 -> x6, Pallas kernels: 9.64 us -> 9.22 us  [the longest x1 3.44 us: local(): pl.pallas_call(functools.partial(update_kernel, landed), out_shape=jax.Sh...]
  transfers between devices with their start and end apart: 14 -> 10, of which waited for: 5 -> 4; matrix products, arithmetic and copies ran while one was open for 0% -> 0% of each run, Pallas kernels for 13% -> 13%
where the time goes in v3:
time: 42.3 us; the launch traced here: 42.1 us
  starting transfers between devices  16.5 us (39%)
  waiting for transfers between devices  14.2 us (34%)
  Pallas kernels  11.1 us (26%)
    ppermute x7, starting transfers between devices, local(): lax.ppermute(operand, 'row', [(s, t) for s, t, item in moves])  14.3 us
    ppermute x7, waiting for transfers between devices, local(): lax.ppermute(operand, 'row', [(s, t) for s, t, item in moves])  8.69 us
    ppermute x3, waiting for transfers between devices, gather_shards(): other = lax.ppermute(held, 'col', [(i, i ^ bit) for i in range(count)])  5.52 us
    pallas_call x1, Pallas kernels, local(): pl.pallas_call(functools.partial(update_kernel, landed), out_shape=jax.Sh...  3.44 us
    pallas_call x1, Pallas kernels, local(): pl.pallas_call(functools.partial(prepare_kernel, row_count), out_shape=(j...  2.96 us
    ppermute x3, starting transfers between devices, gather_shards(): other = lax.ppermute(held, 'col', [(i, i ^ bit) for i in range(count)])  2.19 us
    pallas_call x1, Pallas kernels, local(): pl.pallas_call(functools.partial(pick_kernel, row_count, order), out_shap...  1.92 us
    pallas_call x1, Pallas kernels, local(): pl.pallas_call(functools.partial(upper_kernel, row_count, places), out_sh...  1.45 us
  transfers between devices with their start and end apart: 10, of which 4 were waited for; matrix products, arithmetic and copies ran while one was open for 0% of the time, Pallas kernels for 13%

profile of v3, /device:TPU:28, one launch (start us, length us, event | category | flops | bytes accessed | tf_op | source)
XLA Modules:
  0.0 42.1 jit_solution(9229396841533595343)
XLA Ops:
  0.0 1.9 %pick.1 = (f32[128,384]{1,0:T(8,128)S(1)}, f32[128,384]{1,0:T(8,128)S(1)}, f32[128,384]{1,0:T(8,128)S(1)}, f32[128,384]{1,0:T(8,128)S(1)}, f32[128,384]{1,0:T(8,128)S(1)}, /*index=5*/f32[64,768]{1,0:T(8,128)S(1)}) custom-call(s32[1]{0:T(128)} %bitcast.me_ref, s32[1,512]{1,0:T(1,128)} %bitcast.2, f32[768,384]{1,0:T(8,128)} %matrix_ref.3, f32[64,768]{1,0:T(8,128)} %panel_ref.1), custom_call_target="tpu_custom_call" | custom-call | tf_op jit(solution)/shard_map/pick/pallas_call | solution.py:295
  1.9 2.7 %collective-permute-start.3 = (f32[128,384]{1,0:T(8,128)S(1)}, f32[128,384]{1,0:T(8,128)S(1)}, u32[]{:S(2)}, u32[]{:S(2)}) collective-permute-start(f32[128,384]{1,0:T(8,128)S(1)} %get-tuple-element.18.refs_0_), channel_id=1, source_target_pairs={{0,16},{24,0},{16,8},{1,17},{25,1},{17,9},{2,18},{26,2},{18,10},{3... | collective-permute-start | bytes 589832 | tf_op jit(solution)/shard_map/ppermute | solution.py:323
  4.7 2.0 %collective-permute-start.1 = (f32[128,384]{1,0:T(8,128)S(1)}, f32[128,384]{1,0:T(8,128)S(1)}, u32[]{:S(2)}, u32[]{:S(2)}) collective-permute-start(f32[128,384]{1,0:T(8,128)S(1)} %get-tuple-element.18.refs_0_), channel_id=1, source_target_pairs={{24,16},{8,0},{16,24},{25,17},{9,1},{17,25},{26,18},{10,2},{18,26}... | collective-permute-start | bytes 589832 | tf_op jit(solution)/shard_map/ppermute | solution.py:323
  6.7 0.6 %collective-permute-start.2 = (f32[64,768]{1,0:T(8,128)S(1)}, f32[64,768]{1,0:T(8,128)S(1)}, u32[]{:S(2)}, u32[]{:S(2)}) collective-permute-start(f32[64,768]{1,0:T(8,128)S(1)} %get-tuple-element.21.first), channel_id=1, source_target_pairs={{0,4},{1,5},{2,6},{3,7},{4,0},{5,1},{6,2},{7,3},{8,12},{9,13},{10,... | collective-permute-start | bytes 589832 | tf_op jit(solution)/shard_map/ppermute | solution.py:269
  7.2 4.4 %collective-permute-start = (f32[128,384]{1,0:T(8,128)S(1)}, f32[128,384]{1,0:T(8,128)S(1)}, u32[]{:S(2)}, u32[]{:S(2)}) collective-permute-start(f32[128,384]{1,0:T(8,128)S(1)} %get-tuple-element.17.refs_1_), channel_id=1, source_target_pairs={{0,16},{24,8},{16,0},{1,17},{25,9},{17,1},{2,18},{26,10},{18,2},{3... | collective-permute-start | bytes 589832 | tf_op jit(solution)/shard_map/ppermute | solution.py:323
  11.7 1.4 %collective-permute-done.2.second = f32[64,768]{1,0:T(8,128)S(1)} collective-permute-done((f32[64,768]{1,0:T(8,128)S(1)}, f32[64,768]{1,0:T(8,128)S(1)}, u32[]{:S(2)}, u32[]{:S(2)}) %collective-permute-start.2) | collective-permute-done | bytes 196640 | tf_op jit(solution)/shard_map/ppermute | solution.py:269
  13.0 0.0 collective-permute-done.3.refs_0_.refs_5_
  13.0 0.5 %join.2.first = f32[128,768]{1,0:T(8,128)S(1)} custom-call(f32[64,768]{1,0:T(8,128)S(1)} %get-tuple-element.21.first, f32[64,768]{1,0:T(8,128)S(1)} %collective-permute-done.2.second, f32[128,384]{1,0:T(8,128)S(1)} %collective-permute-done.3.refs_0_.refs_5_), custom_call_target="tpu_custom_call" | custom-call | tf_op jit(solution)/shard_map/join/pallas_call | solution.py:252
  13.6 1.6 %collective-permute-start.4 = (f32[128,768]{1,0:T(8,128)S(1)}, f32[128,768]{1,0:T(8,128)S(1)}, u32[]{:S(2)}, u32[]{:S(2)}) collective-permute-start(f32[128,768]{1,0:T(8,128)S(1)} %join.2.first), channel_id=1, source_target_pairs={{0,2},{1,3},{2,0},{3,1},{4,6},{5,7},{6,4},{7,5},{8,10},{9,11},{10,... | collective-permute-start | bytes 1179656 | tf_op jit(solution)/shard_map/ppermute | solution.py:269
  15.2 1.3 %collective-permute-start.7 = (f32[128,384]{1,0:T(8,128)S(1)}, f32[128,384]{1,0:T(8,128)S(1)}, u32[]{:S(2)}, u32[]{:S(2)}) collective-permute-start(f32[128,384]{1,0:T(8,128)S(1)} %get-tuple-element.31), channel_id=1, source_target_pairs={{16,8},{0,24},{17,9},{1,25},{18,10},{2,26},{19,11},{3,27},{20,12},... | collective-permute-start | bytes 589832 | tf_op jit(solution)/shard_map/ppermute | solution.py:323
  16.5 1.3 %collective-permute-start.6 = (f32[128,384]{1,0:T(8,128)S(1)}, f32[128,384]{1,0:T(8,128)S(1)}, u32[]{:S(2)}, u32[]{:S(2)}) collective-permute-start(f32[128,384]{1,0:T(8,128)S(1)} %get-tuple-element.32), channel_id=1, source_target_pairs={{16,24},{0,8},{8,16},{17,25},{1,9},{9,17},{18,26},{2,10},{10,18},{... | collective-permute-start | bytes 589832 | tf_op jit(solution)/shard_map/ppermute | solution.py:323
  17.8 0.0 collective-permute-done.refs_0_.refs_6_
  17.8 1.3 %collective-permute-start.9 = (f32[128,384]{1,0:T(8,128)S(1)}, f32[128,384]{1,0:T(8,128)S(1)}, u32[]{:S(2)}, u32[]{:S(2)}) collective-permute-start(f32[128,384]{1,0:T(8,128)S(1)} %get-tuple-element.29), channel_id=1, source_target_pairs={{16,8},{8,24},{17,9},{9,25},{18,10},{10,26},{19,11},{11,27},{20,12... | collective-permute-start | bytes 589832 | tf_op jit(solution)/shard_map/ppermute | solution.py:323
  19.1 4.1 %collective-permute-done.4.second = f32[128,768]{1,0:T(8,128)S(1)} collective-permute-done((f32[128,768]{1,0:T(8,128)S(1)}, f32[128,768]{1,0:T(8,128)S(1)}, u32[]{:S(2)}, u32[]{:S(2)}) %collective-permute-start.4) | collective-permute-done | bytes 393248 | tf_op jit(solution)/shard_map/ppermute | solution.py:269
  23.2 1.3 %collective-permute-start.8 = (f32[128,384]{1,0:T(8,128)S(1)}, f32[128,384]{1,0:T(8,128)S(1)}, u32[]{:S(2)}, u32[]{:S(2)}) collective-permute-start(f32[128,384]{1,0:T(8,128)S(1)} %get-tuple-element.30), channel_id=1, source_target_pairs={{16,24},{0,16},{17,25},{1,17},{18,26},{2,18},{19,27},{3,19},{20,28... | collective-permute-start | bytes 589832 | tf_op jit(solution)/shard_map/ppermute | solution.py:323
  24.5 0.4 join.3.near_ref
  24.9 0.0 collective-permute-done.1.refs_1_.refs_7_
  24.9 0.1 collective-permute-start.5
  25.0 3.0 %prepare.1 = (bf16[512,640]{1,0:T(8,128)(2,1)S(1)}, bf16[512,640]{1,0:T(8,128)(2,1)S(1)}, bf16[768,128]{1,0:T(8,128)(2,1)S(1)}, f32[768,384]{1,0:T(8,128)S(1)}) custom-call(s32[1]{0:T(128)} %bitcast.me_ref, s32[1,512]{1,0:T(1,128)} %bitcast.3, f32[512,512]{1,0:T(8,128)} %inverse_ref.1, f32[768,384]{1,0:T(8,128)} %matrix_ref.3, ...), custom_call_target="tpu_custom_call" | custom-call | flops 40000000000 | bytes 100000000 | tf_op jit(solution)/shard_map/prepare/pallas_call | solution.py:330
  28.0 4.2 %collective-permute-done.6.refs_8_ = f32[128,384]{1,0:T(8,128)S(1)} collective-permute-done((f32[128,384]{1,0:T(8,128)S(1)}, f32[128,384]{1,0:T(8,128)S(1)}, u32[]{:S(2)}, u32[]{:S(2)}) %collective-permute-start.6) | collective-permute-done | bytes 196640 | tf_op jit(solution)/shard_map/ppermute | solution.py:323
  32.2 4.4 %collective-permute-done.9.refs_11_ = f32[128,384]{1,0:T(8,128)S(1)} collective-permute-done((f32[128,384]{1,0:T(8,128)S(1)}, f32[128,384]{1,0:T(8,128)S(1)}, u32[]{:S(2)}, u32[]{:S(2)}) %collective-permute-start.9) | collective-permute-done | bytes 196640 | tf_op jit(solution)/shard_map/ppermute | solution.py:323
  36.7 1.5 %upper.1.upper_ref = f32[512,384]{1,0:T(8,128)S(1)} custom-call(s32[1]{0:T(128)} %bitcast.me_ref, bf16[512,640]{1,0:T(8,128)(2,1)S(1)} %get-tuple-element.24.high_ref, bf16[512,640]{1,0:T(8,128)(2,1)S(1)} %get-tuple-element.25.low_ref, f32[128,384]{1,0:T(8,128)S(1)} %get-tuple-element.18.refs_0_, f32[128,384]{1,0:T(8,128)S(1)} %get-tuple-element.17.refs_1_, ...), custom_call_target="tpu_custom_call" | custom-call | tf_op jit(solution)/shard_map/upper/pallas_call | solution.py:354
  38.1 0.5 %turn.1 = (bf16[768,512]{1,0:T(8,128)(2,1)S(1)}, bf16[768,512]{1,0:T(8,128)(2,1)S(1)}) custom-call(f32[256,768]{1,0:T(8,128)S(1)} %join.3.near_ref, f32[256,768]{1,0:T(8,128)S(1)} %collective-permute-done.5.far_ref), custom_call_target="tpu_custom_call" | custom-call | tf_op jit(solution)/shard_map/turn/pallas_call | solution.py:364
  38.6 3.4 %update.1 = f32[768,384]{1,0:T(8,128)} custom-call(s32[1]{0:T(128)} %bitcast.me_ref, s32[8]{0:T(128)S(1)} %broadcast_xor_fusion.ids_ref, f32[768,384]{1,0:T(8,128)S(1)} %get-tuple-element.19.base_ref, bf16[768,128]{1,0:T(8,128)(2,1)S(1)} %get-tuple-element.20.land_ref, bf16[768,512]{1,0:T(8,128)(2,1)S(1)} %get-tuple-element.22.high_ref, ...), custom_call_target="tpu_custom_call" | custom-call | tf_op jit(solution)/shard_map/update/pallas_call | solution.py:373
  (8 shorter events, 0.1 us)
Async XLA Ops:
  0.0 11.6 %copy-start = (s32[8]{0:T(128)S(1)}, s32[8]{0:T(128)}, u32[]{:S(2)}) copy-start(s32[8]{0:T(128)} %constant.12.clone) | copy-start | bytes 100
  1.9 11.1 %collective-permute-start.3 = (f32[128,384]{1,0:T(8,128)S(1)}, f32[128,384]{1,0:T(8,128)S(1)}, u32[]{:S(2)}, u32[]{:S(2)}) collective-permute-start(f32[128,384]{1,0:T(8,128)S(1)} %get-tuple-element.18.refs_0_), channel_id=1, source_target_pairs={{0,16},{24,0},{16,8},{1,17},{25,1},{17,9},{2,18},{26,2},{18,10},{3... | collective-permute-start | bytes 589832 | tf_op jit(solution)/shard_map/ppermute | solution.py:323
  4.7 20.3 %collective-permute-start.1 = (f32[128,384]{1,0:T(8,128)S(1)}, f32[128,384]{1,0:T(8,128)S(1)}, u32[]{:S(2)}, u32[]{:S(2)}) collective-permute-start(f32[128,384]{1,0:T(8,128)S(1)} %get-tuple-element.18.refs_0_), channel_id=1, source_target_pairs={{24,16},{8,0},{16,24},{25,17},{9,1},{17,25},{26,18},{10,2},{18,26}... | collective-permute-start | bytes 589832 | tf_op jit(solution)/shard_map/ppermute | solution.py:323
  6.7 6.4 %collective-permute-start.2 = (f32[64,768]{1,0:T(8,128)S(1)}, f32[64,768]{1,0:T(8,128)S(1)}, u32[]{:S(2)}, u32[]{:S(2)}) collective-permute-start(f32[64,768]{1,0:T(8,128)S(1)} %get-tuple-element.21.first), channel_id=1, source_target_pairs={{0,4},{1,5},{2,6},{3,7},{4,0},{5,1},{6,2},{7,3},{8,12},{9,13},{10,... | collective-permute-start | bytes 589832 | tf_op jit(solution)/shard_map/ppermute | solution.py:269
  7.2 10.5 %collective-permute-start = (f32[128,384]{1,0:T(8,128)S(1)}, f32[128,384]{1,0:T(8,128)S(1)}, u32[]{:S(2)}, u32[]{:S(2)}) collective-permute-start(f32[128,384]{1,0:T(8,128)S(1)} %get-tuple-element.17.refs_1_), channel_id=1, source_target_pairs={{0,16},{24,8},{16,0},{1,17},{25,9},{17,1},{2,18},{26,10},{18,2},{3... | collective-permute-start | bytes 589832 | tf_op jit(solution)/shard_map/ppermute | solution.py:323
  13.6 9.7 %collective-permute-start.4 = (f32[128,768]{1,0:T(8,128)S(1)}, f32[128,768]{1,0:T(8,128)S(1)}, u32[]{:S(2)}, u32[]{:S(2)}) collective-permute-start(f32[128,768]{1,0:T(8,128)S(1)} %join.2.first), channel_id=1, source_target_pairs={{0,2},{1,3},{2,0},{3,1},{4,6},{5,7},{6,4},{7,5},{8,10},{9,11},{10,... | collective-permute-start | bytes 1179656 | tf_op jit(solution)/shard_map/ppermute | solution.py:269
  15.2 12.8 %collective-permute-start.7 = (f32[128,384]{1,0:T(8,128)S(1)}, f32[128,384]{1,0:T(8,128)S(1)}, u32[]{:S(2)}, u32[]{:S(2)}) collective-permute-start(f32[128,384]{1,0:T(8,128)S(1)} %get-tuple-element.31), channel_id=1, source_target_pairs={{16,8},{0,24},{17,9},{1,25},{18,10},{2,26},{19,11},{3,27},{20,12},... | collective-permute-start | bytes 589832 | tf_op jit(solution)/shard_map/ppermute | solution.py:323
  16.5 15.8 %collective-permute-start.6 = (f32[128,384]{1,0:T(8,128)S(1)}, f32[128,384]{1,0:T(8,128)S(1)}, u32[]{:S(2)}, u32[]{:S(2)}) collective-permute-start(f32[128,384]{1,0:T(8,128)S(1)} %get-tuple-element.32), channel_id=1, source_target_pairs={{16,24},{0,8},{8,16},{17,25},{1,9},{9,17},{18,26},{2,10},{10,18},{... | collective-permute-start | bytes 589832 | tf_op jit(solution)/shard_map/ppermute | solution.py:323
  17.8 18.9 %collective-permute-start.9 = (f32[128,384]{1,0:T(8,128)S(1)}, f32[128,384]{1,0:T(8,128)S(1)}, u32[]{:S(2)}, u32[]{:S(2)}) collective-permute-start(f32[128,384]{1,0:T(8,128)S(1)} %get-tuple-element.29), channel_id=1, source_target_pairs={{16,8},{8,24},{17,9},{9,25},{18,10},{10,26},{19,11},{11,27},{20,12... | collective-permute-start | bytes 589832 | tf_op jit(solution)/shard_map/ppermute | solution.py:323
  23.2 13.4 %collective-permute-start.8 = (f32[128,384]{1,0:T(8,128)S(1)}, f32[128,384]{1,0:T(8,128)S(1)}, u32[]{:S(2)}, u32[]{:S(2)}) collective-permute-start(f32[128,384]{1,0:T(8,128)S(1)} %get-tuple-element.30), channel_id=1, source_target_pairs={{16,24},{0,16},{17,25},{1,17},{18,26},{2,18},{19,27},{3,19},{20,28... | collective-permute-start | bytes 589832 | tf_op jit(solution)/shard_map/ppermute | solution.py:323
  24.9 13.2 %collective-permute-start.5 = (f32[256,768]{1,0:T(8,128)S(1)}, f32[256,768]{1,0:T(8,128)S(1)}, u32[]{:S(2)}, u32[]{:S(2)}) collective-permute-start(f32[256,768]{1,0:T(8,128)S(1)} %join.3.near_ref), channel_id=1, source_target_pairs={{0,1},{1,0},{2,3},{3,2},{4,5},{5,4},{6,7},{7,6},{8,9},{9,8},{10,11... | collective-permute-start | bytes 2359304 | tf_op jit(solution)/shard_map/ppermute | solution.py:269

commit v4 on v3

--- a/solution.py
+++ b/solution.py
@@ -71,27 +71,23 @@
 def plan(count):
     middle, chunks = count // 2, count // 2
     first = [(0, middle, ("stay", c)) for c in range(chunks)]
-    relays, down, late = [], [], []
+    relays = []
     for c in range(chunks):
         for k in range(1, count):
             if middle + k < count:
                 relays.append((middle + k - 1, middle + k, ("stay", c)))
             if middle - k > 0:
                 relays.append((middle - k + 1, middle - k, ("stay", c)))
-    for gap in range(count - 1, 0, -1):
-        down += [(r, r - gap, ("pick", r)) for r in range(count - 1, gap - 1, -1) if r > 0]
-    for gap in range(1, count):
-        down += [(r, r + gap, ("pick", r)) for r in range(middle, count - gap)]
-    for s in [1] + list(range(count - 1, 1, -1)):
-        late.append((0, s, ("moved", s)))
-    for gap in range(1, count):
-        late += [(r, r + gap, ("pick", r)) for r in range(1, min(middle, count - gap))]
+    early = [(s, t, ("pick", s)) for t in range(1, count) for s in range(middle, count) if s != t]
+    late = [(0, t, ("moved", t)) for t in range(1, count)]
+    late += [(s, t, ("pick", s)) for t in range(count - 1, 0, -1) for s in range(1, middle) if s != t]
+    late += [(s, 0, ("pick", s)) for s in range(middle, count)]
+    early += [(s, 0, ("pick", s)) for s in range(1, middle)]
     ready = {(0, ("stay", c)): 0 for c in range(chunks)}
     rounds = []
-    while first or relays or down or late:
+    while first or relays or early or late:
         now, senders, targets = [], set(), set()
-        waiting = len(rounds) <= chunks
-        for queue in (first, relays, down, [] if waiting else late):
+        for queue in (first, relays, early, [] if len(rounds) < chunks else late):
             for move in list(queue):
                 s, t, item = move
                 known = item[0] != "stay" or ready.get((s, item), len(rounds) + 1) <= len(rounds)
@@ -168,7 +164,9 @@
     copies[0].wait()
     pivot = pivot_v[...]
     kind, place = classify(pivot, count, rows)
-    spread = one_hot(jnp.where(kind == 0, place, stay + (kind - 1) * slot + place), high_ref.shape[1])
+    total = high_ref.shape[1]
+    stayed = jnp.where(place < stay - slot, place, place + total - stay)
+    spread = one_hot(jnp.where(kind == 0, stayed, stay + (kind - 2) * slot + place), total)
     mine = (kind == me) & (kind != 0)
     landing = lax.broadcasted_iota(jnp.int32, (rows, width), 0) == jnp.where(mine, pivot - me * rows, -1)
     land = mm_nt(landing.astype(BF16), one_hot(jnp.where(mine, place, -1), slot))
@@ -182,16 +180,33 @@
     base_ref[...] = jnp.where(taken > 0.5, 0.0, rows_ref[...])
 
 
-def turn_kernel(near_ref, far_ref, high_ref, low_ref):
+def turn_kernel(me_ref, ids_ref, near_ref, far_ref, inv_high, inv_low, *refs):
+    high_ref, low_ref, end_high, end_low, order_high, order_low = refs
     half = near_ref.shape[0]
+    width, slot = order_high.shape
     for k, part in enumerate((near_ref, far_ref)):
         high, low = halves(-part[...])
         high_ref[:, k * half : (k + 1) * half] = high.T
         low_ref[:, k * half : (k + 1) * half] = low.T
-
-
-def upper_kernel(count, places, me_ref, high_ref, low_ref, *refs):
-    arrays, (out_ref, row_high, row_low) = refs[:-3], refs[-3:]
+    first = inv_high.shape[1] - slot
+    depth = width // ids_ref.shape[0]
+    for k in range(ids_ref.shape[0]):
+        source = pl.ds(pl.multiple_of(ids_ref[k] * depth, depth), depth)
+        part = pl.ds(k * depth, depth)
+        order_high[part, :] = inv_high[source, first:].astype(F32)
+        order_low[part, :] = inv_low[source, first:].astype(F32)
+    pan_high, last_high = high_ref[...], order_high[...].astype(BF16)
+    value = mm(low_ref[...], last_high) + mm(pan_high, order_low[...].astype(BF16)) + mm(pan_high, last_high)
+    end_high[...], end_low[...] = halves(value)
+
+    @pl.when(me_ref[0] == 0)
+    def _():
+        end_high[:width, :] = inv_high[:, first:]
+        end_low[:width, :] = inv_low[:, first:]
+
+
+def upper_kernel(count, places, landed, me_ref, high_ref, low_ref, land_ref, base_ref, *refs):
+    arrays, (out_ref, rows_out, row_high, row_low, new_high, new_low) = refs[:-6], refs[-6:]
     slot = arrays[0].shape[0]
     me = me_ref[0]
     for r in range(count):
@@ -201,37 +216,45 @@
             for block, k in enumerate(places[r]):
                 part = pl.ds(block * slot, slot)
                 row_high[part, :], row_low[part, :] = halves(arrays[k][...])
-
-    high = high_ref[...]
-    out_ref[...] = mm(low_ref[...], row_high[...]) + mm(high, row_low[...]) + mm(high, row_high[...])
-
-
-def update_kernel(places, me_ref, ids_ref, base_ref, land_ref, high_ref, low_ref, upper_ref, *refs):
-    arrays, (out_ref, up_high, up_low, row_high, row_low) = refs[:-5], refs[-5:]
+            if landed[r] is None:
+                new_high[...] = jnp.zeros(new_high.shape, BF16)
+                new_low[...] = jnp.zeros(new_low.shape, BF16)
+            else:
+                new_high[...], new_low[...] = halves(arrays[landed[r]][...])
+
+    depth = row_high.shape[0]
+    high, land = high_ref[:, :depth], land_ref[...]
+    out_ref[...] = mm(low_ref[:, :depth], row_high[...]) + mm(high, row_low[...]) + mm(high, row_high[...])
+    rows_out[...] = base_ref[...] + (mm(land, new_low[...]) + mm(land, new_high[...]))
+
+
+def update_kernel(me_ref, ids_ref, rows_ref, high_ref, low_ref, upper_ref, out_ref, up_high, up_low):
     width = upper_ref.shape[0]
-    me = me_ref[0]
     depth = width // ids_ref.shape[0]
     for k in range(ids_ref.shape[0]):
         source = pl.multiple_of(ids_ref[k] * depth, depth)
         part = pl.ds(k * depth, depth)
         up_high[part, :], up_low[part, :] = halves(upper_ref[pl.ds(source, depth), :])
-    for r, k in enumerate(places):
-
-        @pl.when(me == r)
-        def _(k=k):
-            if k is None:
-                row_high[...] = jnp.zeros(row_high.shape, BF16)
-                row_low[...] = jnp.zeros(row_low.shape, BF16)
-            else:
-                row_high[...], row_low[...] = halves(arrays[k][...])
-
-    high, land = high_ref[...], land_ref[...]
+    high = high_ref[...]
     part = mm(low_ref[...], up_high[...]) + mm(high, up_low[...]) + mm(high, up_high[...])
-    out_ref[...] = base_ref[...] + (mm(land, row_low[...]) + mm(land, row_high[...]) + part)
-
-    @pl.when(me == 0)
+    out_ref[...] = rows_ref[...] + part
+
+    @pl.when(me_ref[0] == 0)
     def _():
         out_ref[:width, :] = upper_ref[...]
+
+
+def finish_kernel(places, me_ref, part_ref, high_ref, low_ref, *refs):
+    arrays, (out_ref, row_high, row_low) = refs[:-3], refs[-3:]
+    for r, k in enumerate(places):
+
+        @pl.when(me_ref[0] == r)
+        def _(k=k):
+            row_high[...], row_low[...] = halves(arrays[k][...])
+
+    high = high_ref[...]
+    value = mm(low_ref[...], row_high[...]) + mm(high, row_low[...]) + mm(high, row_high[...])
+    out_ref[...] = part_ref[...] + value
 
 
 def join_kernel(first, second, *refs):
@@ -312,21 +335,26 @@
         found[0][item] = k
     for r in range(1, row_count):
         found[r]["pick", r] = 0
+    operands, chunks = [], row_count // 2
     for moves in rounds:
         leaving = [item for s, t, item in moves if s == 0]
         operand = own[order.index(leaving[0])] if leaving else own[0]
+        if len(operands) > chunks + 1 and all(item[0] == "stay" for s, t, item in moves):
+            operand = arrays[len(own) + chunks]
         for s, t, item in moves:
             if s != 0 and item[0] == "stay":
                 operand = jnp.where(me == s, arrays[found[s][item]], operand)
         for s, t, item in moves:
             found[t][item] = len(arrays)
+        operands.append(operand)
         arrays.append(lax.ppermute(operand, "row", [(s, t) for s, t, item in moves]))
     received = arrays[len(own) :]
-    blocks = [("stay", c) for c in range(row_count // 2)] + [("pick", p) for p in range(1, row_count)]
+    blocks = [("stay", c) for c in range(chunks - 1)] + [("pick", p) for p in range(1, row_count)]
     places = [[found[r][item] for item in blocks] for r in range(row_count)]
     landed = [found[r].get(("moved", r)) for r in range(row_count)]
-
-    picked_rows = len(blocks) * slot
+    last = [found[r]["stay", chunks - 1] for r in range(row_count)]
+
+    picked_rows = (len(blocks) + 1) * slot
     inv_high, inv_low, land, base = pl.pallas_call(
         functools.partial(prepare_kernel, row_count),
         out_shape=(
@@ -348,37 +376,54 @@
         name="prepare",
     )(here, pivot, inverse_lower, matrix, *received[1:3])
 
-    near, far, masks = gather_shards(panel, col_count, [received[:1], []])
+    near, far, masks = gather_shards(panel, col_count, [operands[3:5], []])
     ids = column ^ jnp.array(masks, jnp.int32)
 
-    upper = pl.pallas_call(
-        functools.partial(upper_kernel, row_count, places),
-        out_shape=jax.ShapeDtypeStruct((width, cols), F32),
-        in_specs=[SMEM] + [VMEM] * (2 + len(arrays)),
+    def used(*tables):
+        names = sorted({k for table in tables for k in jax.tree.leaves(table)})
+        return [arrays[k] for k in names], [jax.tree.map(names.index, table) for table in tables]
+
+    here_arrays, (places, landed) = used(places, landed)
+    upper, with_landed = pl.pallas_call(
+        functools.partial(upper_kernel, row_count, places, landed),
+        out_shape=(jax.ShapeDtypeStruct((width, cols), F32), jax.ShapeDtypeStruct((rows, cols), F32)),
+        in_specs=[SMEM] + [VMEM] * (4 + len(here_arrays)),
+        out_specs=(VMEM, VMEM),
+        scratch_shapes=[pltpu.VMEM((picked_rows - slot, cols), BF16)] * 2 + [pltpu.VMEM((slot, cols), BF16)] * 2,
+        compiler_params=PARAMS,
+        name="upper",
+    )(here, inv_high, inv_low, land, base, *here_arrays)
+
+    pan_high, pan_low, end_high, end_low = pl.pallas_call(
+        turn_kernel,
+        out_shape=(jax.ShapeDtypeStruct((rows, width), BF16),) * 2 + (jax.ShapeDtypeStruct((rows, slot), BF16),) * 2,
+        in_specs=[SMEM, SMEM] + [VMEM] * 4,
+        out_specs=(VMEM,) * 4,
+        scratch_shapes=[pltpu.VMEM((width, slot), F32)] * 2,
+        compiler_params=PARAMS,
+        name="turn",
+    )(here, ids, near, far, inv_high, inv_low)
+
+    part = pl.pallas_call(
+        update_kernel,
+        out_shape=jax.ShapeDtypeStruct((rows, cols), F32),
+        in_specs=[SMEM, SMEM] + [VMEM] * 4,
         out_specs=VMEM,
-        scratch_shapes=[pltpu.VMEM((picked_rows, cols), BF16)] * 2,
-        compiler_params=PARAMS,
-        name="upper",
-    )(here, inv_high, inv_low, *arrays)
-
-    pan_high, pan_low = pl.pallas_call(
-        turn_kernel,
-        out_shape=(jax.ShapeDtypeStruct((rows, width), BF16),) * 2,
-        in_specs=[VMEM, VMEM],
-        out_specs=(VMEM, VMEM),
-        compiler_params=PARAMS,
-        name="turn",
-    )(near, far)
-
+        scratch_shapes=[pltpu.VMEM((width, cols), BF16)] * 2,
+        compiler_params=PARAMS,
+        name="update",
+    )(here, ids, with_landed, pan_high, pan_low, upper)
+
+    last_arrays, (last,) = used(last)
     return pl.pallas_call(
-        functools.partial(update_kernel, landed),
+        functools.partial(finish_kernel, last),
         out_shape=jax.ShapeDtypeStruct((rows, cols), F32),
-        in_specs=[SMEM, SMEM] + [VMEM] * (5 + len(arrays)),
+        in_specs=[SMEM] + [VMEM] * (3 + len(last_arrays)),
         out_specs=VMEM,
-        scratch_shapes=[pltpu.VMEM((width, cols), BF16)] * 2 + [pltpu.VMEM((slot, cols), BF16)] * 2,
-        compiler_params=PARAMS,
-        name="update",
-    )(here, ids, base, land, pan_high, pan_low, upper, *arrays)
+        scratch_shapes=[pltpu.VMEM((slot, cols), BF16)] * 2,
+        compiler_params=PARAMS,
+        name="finish",
+    )(here, part, end_high, end_low, *last_arrays)
 
 
 def solution(mesh):

time: 42.3 us -> 39.7 us (0.939)
  the two profiles are of different devices: /device:TPU:28 before, /device:TPU:16 now
where the time goes in v4:
time: 39.7 us; the launch traced here: 39.5 us
  starting transfers between devices  18.8 us (47%)
  Pallas kernels  12.3 us (31%)
  waiting for transfers between devices  8.1 us (20%)
    ppermute x7, starting transfers between devices, local(): lax.ppermute(operand, 'row', [(s, t) for s, t, item in moves])  15.7 us
    ppermute x7, waiting for transfers between devices, local(): lax.ppermute(operand, 'row', [(s, t) for s, t, item in moves])  6.92 us
    ppermute x3, starting transfers between devices, gather_shards(): other = lax.ppermute(held, 'col', [(i, i ^ bit) for i in range(count)])  3.15 us
    pallas_call x1, Pallas kernels, local(): pl.pallas_call(functools.partial(prepare_kernel, row_count), out_shape=(j...  2.95 us
    pallas_call x1, Pallas kernels, local(): pl.pallas_call(update_kernel, out_shape=jax.ShapeDtypeStruct((rows, cols)...  2.03 us
    pallas_call x1, Pallas kernels, local(): pl.pallas_call(functools.partial(pick_kernel, row_count, order), out_shap...  1.91 us
    pallas_call x1, Pallas kernels, local(): pl.pallas_call(functools.partial(finish_kernel, last), out_shape=jax.Shap...  1.7 us
    pallas_call x1, Pallas kernels, local(): pl.pallas_call(functools.partial(upper_kernel, row_count, places, landed)...  1.46 us
  transfers between devices with their start and end apart: 10, of which 3 were waited for; matrix products, arithmetic and copies ran while one was open for 0% of the time, Pallas kernels for 22%

profile of v4, /device:TPU:16, one launch (start us, length us, event | category | flops | bytes accessed | tf_op | source)
XLA Modules:
  0.0 39.5 jit_solution(6128374844813700473)
XLA Ops:
  0.0 1.9 %pick.1 = (f32[128,384]{1,0:T(8,128)S(1)}, f32[128,384]{1,0:T(8,128)S(1)}, f32[128,384]{1,0:T(8,128)S(1)}, f32[128,384]{1,0:T(8,128)S(1)}, f32[128,384]{1,0:T(8,128)S(1)}, /*index=5*/f32[64,768]{1,0:T(8,128)S(1)}) custom-call(s32[1]{0:T(128)} %bitcast.me_ref, s32[1,512]{1,0:T(1,128)} %bitcast.2, f32[768,384]{1,0:T(8,128)} %matrix_ref.3, f32[64,768]{1,0:T(8,128)} %panel_ref.1), custom_call_target="tpu_custom_call" | custom-call | tf_op jit(solution)/shard_map/pick/pallas_call | solution.py:318
  1.9 0.0 copy-start
  1.9 2.4 %collective-permute-start.2 = (f32[128,384]{1,0:T(8,128)S(1)}, f32[128,384]{1,0:T(8,128)S(1)}, u32[]{:S(2)}, u32[]{:S(2)}) collective-permute-start(f32[128,384]{1,0:T(8,128)S(1)} %get-tuple-element.27.refs_0_), channel_id=1, source_target_pairs={{0,16},{16,8},{8,0},{1,17},{17,9},{9,1},{2,18},{18,10},{10,2},{3,1... | collective-permute-start | bytes 589832 | tf_op jit(solution)/shard_map/ppermute | solution.py:350
  4.3 1.9 %collective-permute-start = (f32[128,384]{1,0:T(8,128)S(1)}, f32[128,384]{1,0:T(8,128)S(1)}, u32[]{:S(2)}, u32[]{:S(2)}) collective-permute-start(f32[128,384]{1,0:T(8,128)S(1)} %get-tuple-element.21.refs_0_), channel_id=1, source_target_pairs={{0,16},{24,8},{16,24},{1,17},{25,9},{17,25},{2,18},{26,10},{18,26}... | collective-permute-start | bytes 589832 | tf_op jit(solution)/shard_map/ppermute | solution.py:350
  6.2 3.0 %collective-permute-start.1 = (f32[128,384]{1,0:T(8,128)S(1)}, f32[128,384]{1,0:T(8,128)S(1)}, u32[]{:S(2)}, u32[]{:S(2)}) collective-permute-start(f32[128,384]{1,0:T(8,128)S(1)} %get-tuple-element.22), channel_id=1, source_target_pairs={{24,16},{0,8},{8,24},{16,0},{25,17},{1,9},{9,25},{17,1},{26,18},{2... | collective-permute-start | bytes 589832 | tf_op jit(solution)/shard_map/ppermute | solution.py:350
  9.2 1.5 %collective-permute-start.5 = (f32[64,768]{1,0:T(8,128)S(1)}, f32[64,768]{1,0:T(8,128)S(1)}, u32[]{:S(2)}, u32[]{:S(2)}) collective-permute-start(f32[64,768]{1,0:T(8,128)S(1)} %get-tuple-element.31.first), channel_id=1, source_target_pairs={{0,4},{1,5},{2,6},{3,7},{4,0},{5,1},{6,2},{7,3},{8,12},{9,13},{10,... | collective-permute-start | bytes 589832 | tf_op jit(solution)/shard_map/ppermute | solution.py:292
  10.7 3.1 %collective-permute-done.2.refs_1_ = f32[128,384]{1,0:T(8,128)S(1)} collective-permute-done((f32[128,384]{1,0:T(8,128)S(1)}, f32[128,384]{1,0:T(8,128)S(1)}, u32[]{:S(2)}, u32[]{:S(2)}) %collective-permute-start.2) | collective-permute-done | bytes 196640 | tf_op jit(solution)/shard_map/ppermute | solution.py:350
  13.8 1.2 %collective-permute-done.5.second = f32[64,768]{1,0:T(8,128)S(1)} collective-permute-done((f32[64,768]{1,0:T(8,128)S(1)}, f32[64,768]{1,0:T(8,128)S(1)}, u32[]{:S(2)}, u32[]{:S(2)}) %collective-permute-start.5) | collective-permute-done | bytes 196640 | tf_op jit(solution)/shard_map/ppermute | solution.py:292
  15.0 0.5 %join.2.first = f32[128,768]{1,0:T(8,128)S(1)} custom-call(f32[64,768]{1,0:T(8,128)S(1)} %get-tuple-element.31.first, f32[64,768]{1,0:T(8,128)S(1)} %collective-permute-done.5.second, f32[128,384]{1,0:T(8,128)S(1)} %get-tuple-element.38.refs_0_, f32[128,384]{1,0:T(8,128)S(1)} %get-tuple-element.37.refs_1_), custom_call_target="tpu_custom_call" | custom-call | tf_op jit(solution)/shard_map/join/pallas_call | solution.py:275
  15.5 1.6 %collective-permute-start.6 = (f32[128,768]{1,0:T(8,128)S(1)}, f32[128,768]{1,0:T(8,128)S(1)}, u32[]{:S(2)}, u32[]{:S(2)}) collective-permute-start(f32[128,768]{1,0:T(8,128)S(1)} %join.2.first), channel_id=1, source_target_pairs={{0,2},{1,3},{2,0},{3,1},{4,6},{5,7},{6,4},{7,5},{8,10},{9,11},{10,... | collective-permute-start | bytes 1179656 | tf_op jit(solution)/shard_map/ppermute | solution.py:292
  17.1 1.9 %collective-permute-start.3 = (f32[128,384]{1,0:T(8,128)S(1)}, f32[128,384]{1,0:T(8,128)S(1)}, u32[]{:S(2)}, u32[]{:S(2)}) collective-permute-start(f32[128,384]{1,0:T(8,128)S(1)} %get-tuple-element.38.refs_0_), channel_id=1, source_target_pairs={{16,24},{0,16},{24,0},{17,25},{1,17},{25,1},{18,26},{2,18},{26,2},... | collective-permute-start | bytes 589832 | tf_op jit(solution)/shard_map/ppermute | solution.py:350
  19.0 1.9 %collective-permute-start.4 = (f32[128,384]{1,0:T(8,128)S(1)}, f32[128,384]{1,0:T(8,128)S(1)}, u32[]{:S(2)}, u32[]{:S(2)}) collective-permute-start(f32[128,384]{1,0:T(8,128)S(1)} %get-tuple-element.37.refs_1_), channel_id=1, source_target_pairs={{16,8},{0,24},{8,16},{17,9},{1,25},{9,17},{18,10},{2,26},{10,18},{... | collective-permute-start | bytes 589832 | tf_op jit(solution)/shard_map/ppermute | solution.py:350
  20.9 0.0 collective-permute-done.refs_0_.refs_2_.refs_1_
  20.9 0.0 collective-permute-done.1.refs_1_.refs_3_
  21.0 3.1 %collective-permute-start.8 = (f32[128,384]{1,0:T(8,128)S(1)}, f32[128,384]{1,0:T(8,128)S(1)}, u32[]{:S(2)}, u32[]{:S(2)}) collective-permute-start(f32[128,384]{1,0:T(8,128)S(1)} %broadcast_select_fusion), channel_id=1, source_target_pairs={{16,24},{17,25},{18,26},{19,27},{20,28},{21,29},{22,30},{23,31}} | collective-permute-start | bytes 589832 | tf_op jit(solution)/shard_map/ppermute | solution.py:350
  24.1 1.5 %collective-permute-start.9 = (f32[128,384]{1,0:T(8,128)S(1)}, f32[128,384]{1,0:T(8,128)S(1)}, u32[]{:S(2)}, u32[]{:S(2)}) collective-permute-start(f32[128,384]{1,0:T(8,128)S(1)} %broadcast_select_fusion), channel_id=1, source_target_pairs={{16,8},{17,9},{18,10},{19,11},{20,12},{21,13},{22,14},{23,15}} | collective-permute-start | bytes 589832 | tf_op jit(solution)/shard_map/ppermute | solution.py:350
  25.6 0.4 %join.3.near_ref = f32[256,768]{1,0:T(8,128)S(1)} custom-call(f32[128,768]{1,0:T(8,128)S(1)} %join.2.first, f32[128,768]{1,0:T(8,128)S(1)} %collective-permute-done.6.second), custom_call_target="tpu_custom_call" | custom-call | tf_op jit(solution)/shard_map/join/pallas_call | solution.py:275
  26.0 0.1 collective-permute-start.7
  26.1 2.9 %prepare.1 = (bf16[512,640]{1,0:T(8,128)(2,1)S(1)}, bf16[512,640]{1,0:T(8,128)(2,1)S(1)}, bf16[768,128]{1,0:T(8,128)(2,1)S(1)}, f32[768,384]{1,0:T(8,128)S(1)}) custom-call(s32[1]{0:T(128)} %bitcast.me_ref, s32[1,512]{1,0:T(1,128)} %bitcast.3, f32[512,512]{1,0:T(8,128)} %inverse_ref.1, f32[768,384]{1,0:T(8,128)} %matrix_ref.3, ...), custom_call_target="tpu_custom_call" | custom-call | flops 40000000000 | bytes 100000000 | tf_op jit(solution)/shard_map/prepare/pallas_call | solution.py:358
  29.0 3.8 %collective-permute-done.4.refs_5_ = f32[128,384]{1,0:T(8,128)S(1)} collective-permute-done((f32[128,384]{1,0:T(8,128)S(1)}, f32[128,384]{1,0:T(8,128)S(1)}, u32[]{:S(2)}, u32[]{:S(2)}) %collective-permute-start.4) | collective-permute-done | bytes 196640 | tf_op jit(solution)/shard_map/ppermute | solution.py:350
  32.9 1.5 %upper.1 = (f32[512,384]{1,0:T(8,128)S(1)}, f32[768,384]{1,0:T(8,128)S(1)}) custom-call(s32[1]{0:T(128)} %bitcast.me_ref, bf16[512,640]{1,0:T(8,128)(2,1)S(1)} %get-tuple-element.23.high_ref.inv_high, bf16[512,640]{1,0:T(8,128)(2,1)S(1)} %get-tuple-element.24.low_ref.inv_low, bf16[768,128]{1,0:T(8,128)(2,1)S(1)} %get-tuple-element.25.land_ref, ...), custom_call_target="tpu_custom_call" | custom-call | tf_op jit(solution)/shard_map/upper/pallas_call | solution.py:387
  34.3 1.4 %turn.1 = (bf16[768,512]{1,0:T(8,128)(2,1)S(1)}, bf16[768,512]{1,0:T(8,128)(2,1)S(1)}, bf16[768,128]{1,0:T(8,128)(2,1)S(1)}, bf16[768,128]{1,0:T(8,128)(2,1)S(1)}) custom-call(s32[1]{0:T(128)} %bitcast.me_ref, s32[8]{0:T(128)S(1)} %broadcast_xor_fusion.ids_ref, f32[256,768]{1,0:T(8,128)S(1)} %join.3.near_ref, f32[256,768]{1,0:T(8,128)S(1)} %collective-permute-done.7.far_ref, ...), custom_call_target="tpu_custom_call" | custom-call | tf_op jit(solution)/shard_map/turn/pallas_call | solution.py:397
  35.7 2.0 %update.1.part_ref = f32[768,384]{1,0:T(8,128)S(1)} custom-call(s32[1]{0:T(128)} %bitcast.me_ref, s32[8]{0:T(128)S(1)} %broadcast_xor_fusion.ids_ref, f32[768,384]{1,0:T(8,128)S(1)} %get-tuple-element.30.rows_ref, bf16[768,512]{1,0:T(8,128)(2,1)S(1)} %get-tuple-element.32.high_ref, bf16[768,512]{1,0:T(8,128)(2,1)S(1)} %get-tuple-element.33.low_ref, ...), custom_call_target="tpu_custom_call" | custom-call | tf_op jit(solution)/shard_map/update/pallas_call | solution.py:407
  37.8 1.7 %finish.1 = f32[768,384]{1,0:T(8,128)} custom-call(s32[1]{0:T(128)} %bitcast.me_ref, f32[768,384]{1,0:T(8,128)S(1)} %update.1.part_ref, bf16[768,128]{1,0:T(8,128)(2,1)S(1)} %get-tuple-element.35.high_ref, bf16[768,128]{1,0:T(8,128)(2,1)S(1)} %get-tuple-element.36.low_ref, f32[128,384]{1,0:T(8,128)S(1)} %get-tuple-element.21.refs_0_, ...), custom_call_target="tpu_custom_call" | custom-call | tf_op jit(solution)/shard_map/finish/pallas_call | solution.py:418
  (9 shorter events, 0.1 us)
Async XLA Ops:
  1.9 15.1 %copy-start = (s32[8]{0:T(128)S(1)}, s32[8]{0:T(128)}, u32[]{:S(2)}) copy-start(s32[8]{0:T(128)} %constant.12.clone) | copy-start | bytes 100
  1.9 11.9 %collective-permute-start.2 = (f32[128,384]{1,0:T(8,128)S(1)}, f32[128,384]{1,0:T(8,128)S(1)}, u32[]{:S(2)}, u32[]{:S(2)}) collective-permute-start(f32[128,384]{1,0:T(8,128)S(1)} %get-tuple-element.27.refs_0_), channel_id=1, source_target_pairs={{0,16},{16,8},{8,0},{1,17},{17,9},{9,1},{2,18},{18,10},{10,2},{3,1... | collective-permute-start | bytes 589832 | tf_op jit(solution)/shard_map/ppermute | solution.py:350
  4.3 16.6 %collective-permute-start = (f32[128,384]{1,0:T(8,128)S(1)}, f32[128,384]{1,0:T(8,128)S(1)}, u32[]{:S(2)}, u32[]{:S(2)}) collective-permute-start(f32[128,384]{1,0:T(8,128)S(1)} %get-tuple-element.21.refs_0_), channel_id=1, source_target_pairs={{0,16},{24,8},{16,24},{1,17},{25,9},{17,25},{2,18},{26,10},{18,26}... | collective-permute-start | bytes 589832 | tf_op jit(solution)/shard_map/ppermute | solution.py:350
  6.2 14.7 %collective-permute-start.1 = (f32[128,384]{1,0:T(8,128)S(1)}, f32[128,384]{1,0:T(8,128)S(1)}, u32[]{:S(2)}, u32[]{:S(2)}) collective-permute-start(f32[128,384]{1,0:T(8,128)S(1)} %get-tuple-element.22), channel_id=1, source_target_pairs={{24,16},{0,8},{8,24},{16,0},{25,17},{1,9},{9,25},{17,1},{26,18},{2... | collective-permute-start | bytes 589832 | tf_op jit(solution)/shard_map/ppermute | solution.py:350
  9.2 5.8 %collective-permute-start.5 = (f32[64,768]{1,0:T(8,128)S(1)}, f32[64,768]{1,0:T(8,128)S(1)}, u32[]{:S(2)}, u32[]{:S(2)}) collective-permute-start(f32[64,768]{1,0:T(8,128)S(1)} %get-tuple-element.31.first), channel_id=1, source_target_pairs={{0,4},{1,5},{2,6},{3,7},{4,0},{5,1},{6,2},{7,3},{8,12},{9,13},{10,... | collective-permute-start | bytes 589832 | tf_op jit(solution)/shard_map/ppermute | solution.py:292
  15.5 10.1 %collective-permute-start.6 = (f32[128,768]{1,0:T(8,128)S(1)}, f32[128,768]{1,0:T(8,128)S(1)}, u32[]{:S(2)}, u32[]{:S(2)}) collective-permute-start(f32[128,768]{1,0:T(8,128)S(1)} %join.2.first), channel_id=1, source_target_pairs={{0,2},{1,3},{2,0},{3,1},{4,6},{5,7},{6,4},{7,5},{8,10},{9,11},{10,... | collective-permute-start | bytes 1179656 | tf_op jit(solution)/shard_map/ppermute | solution.py:292
  17.1 12.0 %collective-permute-start.3 = (f32[128,384]{1,0:T(8,128)S(1)}, f32[128,384]{1,0:T(8,128)S(1)}, u32[]{:S(2)}, u32[]{:S(2)}) collective-permute-start(f32[128,384]{1,0:T(8,128)S(1)} %get-tuple-element.38.refs_0_), channel_id=1, source_target_pairs={{16,24},{0,16},{24,0},{17,25},{1,17},{25,1},{18,26},{2,18},{26,2},... | collective-permute-start | bytes 589832 | tf_op jit(solution)/shard_map/ppermute | solution.py:350
  19.0 13.9 %collective-permute-start.4 = (f32[128,384]{1,0:T(8,128)S(1)}, f32[128,384]{1,0:T(8,128)S(1)}, u32[]{:S(2)}, u32[]{:S(2)}) collective-permute-start(f32[128,384]{1,0:T(8,128)S(1)} %get-tuple-element.37.refs_1_), channel_id=1, source_target_pairs={{16,8},{0,24},{8,16},{17,9},{1,25},{9,17},{18,10},{2,26},{10,18},{... | collective-permute-start | bytes 589832 | tf_op jit(solution)/shard_map/ppermute | solution.py:350
  21.0 16.8 %collective-permute-start.8 = (f32[128,384]{1,0:T(8,128)S(1)}, f32[128,384]{1,0:T(8,128)S(1)}, u32[]{:S(2)}, u32[]{:S(2)}) collective-permute-start(f32[128,384]{1,0:T(8,128)S(1)} %broadcast_select_fusion), channel_id=1, source_target_pairs={{16,24},{17,25},{18,26},{19,27},{20,28},{21,29},{22,30},{23,31}} | collective-permute-start | bytes 589832 | tf_op jit(solution)/shard_map/ppermute | solution.py:350
  24.1 13.7 %collective-permute-start.9 = (f32[128,384]{1,0:T(8,128)S(1)}, f32[128,384]{1,0:T(8,128)S(1)}, u32[]{:S(2)}, u32[]{:S(2)}) collective-permute-start(f32[128,384]{1,0:T(8,128)S(1)} %broadcast_select_fusion), channel_id=1, source_target_pairs={{16,8},{17,9},{18,10},{19,11},{20,12},{21,13},{22,14},{23,15}} | collective-permute-start | bytes 589832 | tf_op jit(solution)/shard_map/ppermute | solution.py:350
  26.0 8.3 %collective-permute-start.7 = (f32[256,768]{1,0:T(8,128)S(1)}, f32[256,768]{1,0:T(8,128)S(1)}, u32[]{:S(2)}, u32[]{:S(2)}) collective-permute-start(f32[256,768]{1,0:T(8,128)S(1)} %join.3.near_ref), channel_id=1, source_target_pairs={{0,1},{1,0},{2,3},{3,2},{4,5},{5,4},{6,7},{7,6},{8,9},{9,8},{10,11... | collective-permute-start | bytes 2359304 | tf_op jit(solution)/shard_map/ppermute | solution.py:292

commit v5 on v4

--- a/solution.py
+++ b/solution.py
@@ -13,6 +13,7 @@
 SMEM = pl.BlockSpec(memory_space=pltpu.SMEM)
 ANY = pl.BlockSpec(memory_space=pl.ANY)
 HBM = pl.BlockSpec(memory_space=pltpu.HBM)
+SHORT = pl.CostEstimate(flops=1_000_000, transcendentals=0, bytes_accessed=100_000)
 LONG = pl.CostEstimate(flops=40_000_000_000, transcendentals=0, bytes_accessed=100_000_000)
 PARAMS = pltpu.CompilerParams(vmem_limit_bytes=20 * 1024 * 1024)
 
@@ -165,8 +166,9 @@
     pivot = pivot_v[...]
     kind, place = classify(pivot, count, rows)
     total = high_ref.shape[1]
-    stayed = jnp.where(place < stay - slot, place, place + total - stay)
-    spread = one_hot(jnp.where(kind == 0, stayed, stay + (kind - 2) * slot + place), total)
+    middle = count // 2
+    start = jnp.where(kind == 0, (count - middle) * slot, stay + (kind + count - middle - 1) * slot)
+    spread = one_hot(place + jnp.where(kind < middle, start, (kind - middle) * slot), total)
     mine = (kind == me) & (kind != 0)
     landing = lax.broadcasted_iota(jnp.int32, (rows, width), 0) == jnp.where(mine, pivot - me * rows, -1)
     land = mm_nt(landing.astype(BF16), one_hot(jnp.where(mine, place, -1), slot))
@@ -180,15 +182,15 @@
     base_ref[...] = jnp.where(taken > 0.5, 0.0, rows_ref[...])
 
 
-def turn_kernel(me_ref, ids_ref, near_ref, far_ref, inv_high, inv_low, *refs):
+def turn_kernel(me_ref, ids_ref, near_ref, far_ref, inv_high, inv_low, land_ref, *refs):
     high_ref, low_ref, end_high, end_low, order_high, order_low = refs
     half = near_ref.shape[0]
-    width, slot = order_high.shape
+    width, picked_rows = order_high.shape
     for k, part in enumerate((near_ref, far_ref)):
         high, low = halves(-part[...])
         high_ref[:, k * half : (k + 1) * half] = high.T
         low_ref[:, k * half : (k + 1) * half] = low.T
-    first = inv_high.shape[1] - slot
+    first = inv_high.shape[1] - picked_rows
     depth = width // ids_ref.shape[0]
     for k in range(ids_ref.shape[0]):
         source = pl.ds(pl.multiple_of(ids_ref[k] * depth, depth), depth)
@@ -197,35 +199,37 @@
         order_low[part, :] = inv_low[source, first:].astype(F32)
     pan_high, last_high = high_ref[...], order_high[...].astype(BF16)
     value = mm(low_ref[...], last_high) + mm(pan_high, order_low[...].astype(BF16)) + mm(pan_high, last_high)
-    end_high[...], end_low[...] = halves(value)
+    end_high[:, :picked_rows], end_low[:, :picked_rows] = halves(value)
+    end_high[:, picked_rows:] = land_ref[...]
+    end_low[:, picked_rows:] = jnp.zeros(land_ref.shape, BF16)
 
     @pl.when(me_ref[0] == 0)
     def _():
-        end_high[:width, :] = inv_high[:, first:]
-        end_low[:width, :] = inv_low[:, first:]
-
-
-def upper_kernel(count, places, landed, me_ref, high_ref, low_ref, land_ref, base_ref, *refs):
-    arrays, (out_ref, rows_out, row_high, row_low, new_high, new_low) = refs[:-6], refs[-6:]
-    slot = arrays[0].shape[0]
-    me = me_ref[0]
-    for r in range(count):
+        end_high[:width, :picked_rows] = inv_high[:, first:]
+        end_low[:width, :picked_rows] = inv_low[:, first:]
+
+
+def collect(places, me, arrays, row_high, row_low):
+    slot, cols = arrays[0].shape
+    for r in range(len(places)):
 
         @pl.when(me == r)
         def _(r=r):
             for block, k in enumerate(places[r]):
                 part = pl.ds(block * slot, slot)
-                row_high[part, :], row_low[part, :] = halves(arrays[k][...])
-            if landed[r] is None:
-                new_high[...] = jnp.zeros(new_high.shape, BF16)
-                new_low[...] = jnp.zeros(new_low.shape, BF16)
-            else:
-                new_high[...], new_low[...] = halves(arrays[landed[r]][...])
-
+                if k is None:
+                    row_high[part, :] = jnp.zeros((slot, cols), BF16)
+                    row_low[part, :] = jnp.zeros((slot, cols), BF16)
+                else:
+                    row_high[part, :], row_low[part, :] = halves(arrays[k][...])
+
+
+def upper_kernel(places, me_ref, high_ref, low_ref, *refs):
+    arrays, (out_ref, row_high, row_low) = refs[:-3], refs[-3:]
+    collect(places, me_ref[0], arrays, row_high, row_low)
     depth = row_high.shape[0]
-    high, land = high_ref[:, :depth], land_ref[...]
+    high = high_ref[:, :depth]
     out_ref[...] = mm(low_ref[:, :depth], row_high[...]) + mm(high, row_low[...]) + mm(high, row_high[...])
-    rows_out[...] = base_ref[...] + (mm(land, new_low[...]) + mm(land, new_high[...]))
 
 
 def update_kernel(me_ref, ids_ref, rows_ref, high_ref, low_ref, upper_ref, out_ref, up_high, up_low):
@@ -246,12 +250,7 @@
 
 def finish_kernel(places, me_ref, part_ref, high_ref, low_ref, *refs):
     arrays, (out_ref, row_high, row_low) = refs[:-3], refs[-3:]
-    for r, k in enumerate(places):
-
-        @pl.when(me_ref[0] == r)
-        def _(k=k):
-            row_high[...], row_low[...] = halves(arrays[k][...])
-
+    collect(places, me_ref[0], arrays, row_high, row_low)
     high = high_ref[...]
     value = mm(low_ref[...], row_high[...]) + mm(high, row_low[...]) + mm(high, row_high[...])
     out_ref[...] = part_ref[...] + value
@@ -349,12 +348,13 @@
         operands.append(operand)
         arrays.append(lax.ppermute(operand, "row", [(s, t) for s, t, item in moves]))
     received = arrays[len(own) :]
-    blocks = [("stay", c) for c in range(chunks - 1)] + [("pick", p) for p in range(1, row_count)]
+    blocks = [("pick", p) for p in range(chunks, row_count)]
+    late_blocks = [("stay", c) for c in range(chunks)] + [("pick", p) for p in range(1, chunks)]
     places = [[found[r][item] for item in blocks] for r in range(row_count)]
-    landed = [found[r].get(("moved", r)) for r in range(row_count)]
-    last = [found[r]["stay", chunks - 1] for r in range(row_count)]
-
-    picked_rows = (len(blocks) + 1) * slot
+    late = [[found[r].get(item) for item in late_blocks + [("moved", r)]] for r in range(row_count)]
+    late_rows = len(late_blocks) * slot
+
+    picked_rows = len(blocks) * slot + late_rows
     inv_high, inv_low, land, base = pl.pallas_call(
         functools.partial(prepare_kernel, row_count),
         out_shape=(
@@ -363,7 +363,7 @@
             jax.ShapeDtypeStruct((rows, slot), BF16),
             jax.ShapeDtypeStruct((rows, cols), F32),
         ),
-        in_specs=[SMEM, HBM, HBM, HBM] + [ANY] * 2,
+        in_specs=[SMEM, HBM, HBM, HBM],
         out_specs=(VMEM,) * 4,
         scratch_shapes=[
             pltpu.VMEM((1, width), jnp.int32),
@@ -372,37 +372,39 @@
             pltpu.SemaphoreType.DMA((3,)),
         ],
         compiler_params=PARAMS,
-        cost_estimate=LONG,
+        cost_estimate=SHORT,
         name="prepare",
-    )(here, pivot, inverse_lower, matrix, *received[1:3])
-
-    near, far, masks = gather_shards(panel, col_count, [operands[3:5], []])
+    )(here, pivot, inverse_lower, matrix)
+
+    near, far, masks = gather_shards(panel, col_count, [operands[3:5] + [land], []])
     ids = column ^ jnp.array(masks, jnp.int32)
 
     def used(*tables):
         names = sorted({k for table in tables for k in jax.tree.leaves(table)})
         return [arrays[k] for k in names], [jax.tree.map(names.index, table) for table in tables]
 
-    here_arrays, (places, landed) = used(places, landed)
-    upper, with_landed = pl.pallas_call(
-        functools.partial(upper_kernel, row_count, places, landed),
-        out_shape=(jax.ShapeDtypeStruct((width, cols), F32), jax.ShapeDtypeStruct((rows, cols), F32)),
-        in_specs=[SMEM] + [VMEM] * (4 + len(here_arrays)),
-        out_specs=(VMEM, VMEM),
-        scratch_shapes=[pltpu.VMEM((picked_rows - slot, cols), BF16)] * 2 + [pltpu.VMEM((slot, cols), BF16)] * 2,
-        compiler_params=PARAMS,
+    early_arrays, (places,) = used(places)
+    upper = pl.pallas_call(
+        functools.partial(upper_kernel, places),
+        out_shape=jax.ShapeDtypeStruct((width, cols), F32),
+        in_specs=[SMEM] + [VMEM] * (2 + len(early_arrays)),
+        out_specs=VMEM,
+        scratch_shapes=[pltpu.VMEM((picked_rows - late_rows, cols), BF16)] * 2,
+        compiler_params=PARAMS,
+        cost_estimate=LONG,
         name="upper",
-    )(here, inv_high, inv_low, land, base, *here_arrays)
+    )(here, inv_high, inv_low, *early_arrays)
 
     pan_high, pan_low, end_high, end_low = pl.pallas_call(
         turn_kernel,
-        out_shape=(jax.ShapeDtypeStruct((rows, width), BF16),) * 2 + (jax.ShapeDtypeStruct((rows, slot), BF16),) * 2,
-        in_specs=[SMEM, SMEM] + [VMEM] * 4,
+        out_shape=(jax.ShapeDtypeStruct((rows, width), BF16),) * 2
+        + (jax.ShapeDtypeStruct((rows, late_rows + slot), BF16),) * 2,
+        in_specs=[SMEM, SMEM] + [VMEM] * 5,
         out_specs=(VMEM,) * 4,
-        scratch_shapes=[pltpu.VMEM((width, slot), F32)] * 2,
+        scratch_shapes=[pltpu.VMEM((width, late_rows), F32)] * 2,
         compiler_params=PARAMS,
         name="turn",
-    )(here, ids, near, far, inv_high, inv_low)
+    )(here, ids, near, far, inv_high, inv_low, land)
 
     part = pl.pallas_call(
         update_kernel,
@@ -412,18 +414,18 @@
         scratch_shapes=[pltpu.VMEM((width, cols), BF16)] * 2,
         compiler_params=PARAMS,
         name="update",
-    )(here, ids, with_landed, pan_high, pan_low, upper)
-
-    last_arrays, (last,) = used(last)
+    )(here, ids, base, pan_high, pan_low, upper)
+
+    late_arrays, (late,) = used(late)
     return pl.pallas_call(
-        functools.partial(finish_kernel, last),
+        functools.partial(finish_kernel, late),
         out_shape=jax.ShapeDtypeStruct((rows, cols), F32),
-        in_specs=[SMEM] + [VMEM] * (3 + len(last_arrays)),
+        in_specs=[SMEM] + [VMEM] * (3 + len(late_arrays)),
         out_specs=VMEM,
-        scratch_shapes=[pltpu.VMEM((slot, cols), BF16)] * 2,
+        scratch_shapes=[pltpu.VMEM((late_rows + slot, cols), BF16)] * 2,
         compiler_params=PARAMS,
         name="finish",
-    )(here, part, end_high, end_low, *last_arrays)
+    )(here, part, end_high, end_low, *late_arrays)
 
 
 def solution(mesh):

time: 39.7 us -> 36.3 us (0.914)
  the two profiles are of different devices: /device:TPU:16 before, /device:TPU:3 now
where the time goes in v5:
time: 36.3 us; the launch traced here: 36.1 us
  starting transfers between devices  20 us (55%)
  Pallas kernels  13.7 us (38%)
  waiting for transfers between devices  2.12 us (6%)
    ppermute x7, starting transfers between devices, local(): lax.ppermute(operand, 'row', [(s, t) for s, t, item in moves])  14.2 us
    ppermute x3, starting transfers between devices, gather_shards(): other = lax.ppermute(held, 'col', [(i, i ^ bit) for i in range(count)])  5.88 us
    pallas_call x1, Pallas kernels, local(): pl.pallas_call(functools.partial(prepare_kernel, row_count), out_shape=(j...  2.93 us
    pallas_call x1, Pallas kernels, local(): pl.pallas_call(functools.partial(finish_kernel, late), out_shape=jax.Shap...  2.55 us
    pallas_call x1, Pallas kernels, local(): pl.pallas_call(functools.partial(pick_kernel, row_count, order), out_shap...  2.51 us
    pallas_call x1, Pallas kernels, local(): pl.pallas_call(update_kernel, out_shape=jax.ShapeDtypeStruct((rows, cols)...  2.06 us
    pallas_call x1, Pallas kernels, local(): pl.pallas_call(turn_kernel, out_shape=(jax.ShapeDtypeStruct((rows, width)...  2.04 us
    ppermute x3, waiting for transfers between devices, gather_shards(): other = lax.ppermute(held, 'col', [(i, i ^ bit) for i in range(count)])  1.27 us
  transfers between devices with their start and end apart: 10, of which 2 were waited for; matrix products, arithmetic and copies ran while one was open for 0% of the time, Pallas kernels for 24%

profile of v5, /device:TPU:3, one launch (start us, length us, event | category | flops | bytes accessed | tf_op | source)
XLA Modules:
  0.0 36.1 jit_solution(13701406859588977165)
XLA Ops:
  0.0 2.5 %pick.1 = (f32[128,384]{1,0:T(8,128)S(1)}, f32[128,384]{1,0:T(8,128)S(1)}, f32[128,384]{1,0:T(8,128)S(1)}, f32[128,384]{1,0:T(8,128)S(1)}, f32[128,384]{1,0:T(8,128)S(1)}, /*index=5*/f32[64,768]{1,0:T(8,128)S(1)}) custom-call(s32[1]{0:T(128)} %bitcast.me_ref, s32[1,512]{1,0:T(1,128)} %bitcast.2, f32[768,384]{1,0:T(8,128)} %matrix_ref.3, f32[64,768]{1,0:T(8,128)} %panel_ref.1), custom_call_target="tpu_custom_call" | custom-call | tf_op jit(solution)/shard_map/pick/pallas_call | solution.py:317
  2.5 3.6 %collective-permute-start.1 = (f32[128,384]{1,0:T(8,128)S(1)}, f32[128,384]{1,0:T(8,128)S(1)}, u32[]{:S(2)}, u32[]{:S(2)}) collective-permute-start(f32[128,384]{1,0:T(8,128)S(1)} %get-tuple-element.21.refs_0_), channel_id=1, source_target_pairs={{0,16},{16,8},{8,0},{1,17},{17,9},{9,1},{2,18},{18,10},{10,2},{3,1... | collective-permute-start | bytes 589832 | tf_op jit(solution)/shard_map/ppermute | solution.py:349
  6.1 1.3 %collective-permute-start = (f32[64,768]{1,0:T(8,128)S(1)}, f32[64,768]{1,0:T(8,128)S(1)}, u32[]{:S(2)}, u32[]{:S(2)}) collective-permute-start(f32[64,768]{1,0:T(8,128)S(1)} %get-tuple-element.20.first), channel_id=1, source_target_pairs={{0,4},{1,5},{2,6},{3,7},{4,0},{5,1},{6,2},{7,3},{8,12},{9,13},{10,... | collective-permute-start | bytes 589832 | tf_op jit(solution)/shard_map/ppermute | solution.py:291
  7.4 2.1 %collective-permute-start.4 = (f32[128,384]{1,0:T(8,128)S(1)}, f32[128,384]{1,0:T(8,128)S(1)}, u32[]{:S(2)}, u32[]{:S(2)}) collective-permute-start(f32[128,384]{1,0:T(8,128)S(1)} %get-tuple-element.29.refs_1_), channel_id=1, source_target_pairs={{0,16},{24,8},{16,24},{1,17},{25,9},{17,25},{2,18},{26,10},{18,26}... | collective-permute-start | bytes 589832 | tf_op jit(solution)/shard_map/ppermute | solution.py:349
  9.5 0.1 collective-permute-start.5
  9.6 2.9 %prepare.1 = (bf16[512,640]{1,0:T(8,128)(2,1)S(1)}, bf16[512,640]{1,0:T(8,128)(2,1)S(1)}, bf16[768,128]{1,0:T(8,128)(2,1)S(1)}, f32[768,384]{1,0:T(8,128)S(1)}) custom-call(s32[1]{0:T(128)} %bitcast.me_ref, s32[1,512]{1,0:T(1,128)} %bitcast.3, f32[512,512]{1,0:T(8,128)} %inverse_ref.1, f32[768,384]{1,0:T(8,128)} %matrix_ref.3), custom_call_target="tpu_custom_call" | custom-call | flops 1000000 | bytes 100000 | tf_op jit(solution)/shard_map/prepare/pallas_call | solution.py:358
  12.5 0.0 collective-permute-done.1.refs_1_.refs_2_
  12.5 0.0 copy-start
  12.6 0.5 %join.2.first = f32[128,768]{1,0:T(8,128)S(1)} custom-call(f32[64,768]{1,0:T(8,128)S(1)} %get-tuple-element.20.first, f32[64,768]{1,0:T(8,128)S(1)} %collective-permute-done.second, f32[128,384]{1,0:T(8,128)S(1)} %get-tuple-element.34.refs_0_, f32[128,384]{1,0:T(8,128)S(1)} %get-tuple-element.33.refs_1_, bf16[768,128]{1,0:T(8,128)(2,1)S(1)} %get-tuple-element.24.refs_2_.land_ref), custom_call_target="tpu_custom_call" | custom-call | tf_op jit(solution)/shard_map/join/pallas_call | solution.py:274
  13.2 0.3 collective-permute-start.2
  13.5 4.2 %collective-permute-start.6 = (f32[128,384]{1,0:T(8,128)S(1)}, f32[128,384]{1,0:T(8,128)S(1)}, u32[]{:S(2)}, u32[]{:S(2)}) collective-permute-start(f32[128,384]{1,0:T(8,128)S(1)} %get-tuple-element.34.refs_0_), channel_id=1, source_target_pairs={{16,24},{0,16},{24,0},{17,25},{1,17},{25,1},{18,26},{2,18},{26,2},... | collective-permute-start | bytes 589832 | tf_op jit(solution)/shard_map/ppermute | solution.py:349
  17.7 2.8 %collective-permute-start.7 = (f32[128,384]{1,0:T(8,128)S(1)}, f32[128,384]{1,0:T(8,128)S(1)}, u32[]{:S(2)}, u32[]{:S(2)}) collective-permute-start(f32[128,384]{1,0:T(8,128)S(1)} %get-tuple-element.33.refs_1_), channel_id=1, source_target_pairs={{16,8},{0,24},{8,16},{17,9},{1,25},{9,17},{18,10},{2,26},{10,18},{... | collective-permute-start | bytes 589832 | tf_op jit(solution)/shard_map/ppermute | solution.py:349
  20.6 0.8 %collective-permute-done.5.refs_3_.refs_4_ = f32[128,384]{1,0:T(8,128)S(1)} collective-permute-done((f32[128,384]{1,0:T(8,128)S(1)}, f32[128,384]{1,0:T(8,128)S(1)}, u32[]{:S(2)}, u32[]{:S(2)}) %collective-permute-start.5) | collective-permute-done | bytes 196640 | tf_op jit(solution)/shard_map/ppermute | solution.py:349
  21.4 0.7 %collective-permute-start.8 = (f32[128,384]{1,0:T(8,128)S(1)}, f32[128,384]{1,0:T(8,128)S(1)}, u32[]{:S(2)}, u32[]{:S(2)}) collective-permute-start(f32[128,384]{1,0:T(8,128)S(1)} %broadcast_select_fusion), channel_id=1, source_target_pairs={{16,24},{17,25},{18,26},{19,27},{20,28},{21,29},{22,30},{23,31}} | collective-permute-start | bytes 589832 | tf_op jit(solution)/shard_map/ppermute | solution.py:349
  22.1 0.7 %collective-permute-start.9 = (f32[128,384]{1,0:T(8,128)S(1)}, f32[128,384]{1,0:T(8,128)S(1)}, u32[]{:S(2)}, u32[]{:S(2)}) collective-permute-start(f32[128,384]{1,0:T(8,128)S(1)} %broadcast_select_fusion), channel_id=1, source_target_pairs={{16,8},{17,9},{18,10},{19,11},{20,12},{21,13},{22,14},{23,15}} | collective-permute-start | bytes 589832 | tf_op jit(solution)/shard_map/ppermute | solution.py:349
  22.8 0.4 %join.3.near_ref = f32[256,768]{1,0:T(8,128)S(1)} custom-call(f32[128,768]{1,0:T(8,128)S(1)} %join.2.first, f32[128,768]{1,0:T(8,128)S(1)} %collective-permute-done.2.second), custom_call_target="tpu_custom_call" | custom-call | tf_op jit(solution)/shard_map/join/pallas_call | solution.py:274
  23.2 4.3 %collective-permute-start.3 = (f32[256,768]{1,0:T(8,128)S(1)}, f32[256,768]{1,0:T(8,128)S(1)}, u32[]{:S(2)}, u32[]{:S(2)}) collective-permute-start(f32[256,768]{1,0:T(8,128)S(1)} %join.3.near_ref), channel_id=1, source_target_pairs={{0,1},{1,0},{2,3},{3,2},{4,5},{5,4},{6,7},{7,6},{8,9},{9,8},{10,11... | collective-permute-start | bytes 2359304 | tf_op jit(solution)/shard_map/ppermute | solution.py:291
  27.5 0.0 collective-permute-done.6.refs_4_.refs_5_
  27.5 0.6 %upper.1.upper_ref = f32[512,384]{1,0:T(8,128)S(1)} custom-call(s32[1]{0:T(128)} %bitcast.me_ref, bf16[512,640]{1,0:T(8,128)(2,1)S(1)} %get-tuple-element.25.inv_high.high_ref, bf16[512,640]{1,0:T(8,128)(2,1)S(1)} %get-tuple-element.26.inv_low.low_ref, f32[128,384]{1,0:T(8,128)S(1)} %get-tuple-element.21.refs_0_, ...), custom_call_target="tpu_custom_call" | custom-call | flops 40000000000 | bytes 100000000 | tf_op jit(solution)/shard_map/upper/pallas_call | solution.py:387
  28.1 1.3 %collective-permute-done.3.far_ref = f32[256,768]{1,0:T(8,128)S(1)} collective-permute-done((f32[256,768]{1,0:T(8,128)S(1)}, f32[256,768]{1,0:T(8,128)S(1)}, u32[]{:S(2)}, u32[]{:S(2)}) %collective-permute-start.3) | collective-permute-done | bytes 786464 | tf_op jit(solution)/shard_map/ppermute | solution.py:291
  29.4 2.0 %turn.1 = (bf16[768,512]{1,0:T(8,128)(2,1)S(1)}, bf16[768,512]{1,0:T(8,128)(2,1)S(1)}, bf16[768,512]{1,0:T(8,128)(2,1)S(1)}, bf16[768,512]{1,0:T(8,128)(2,1)S(1)}) custom-call(s32[1]{0:T(128)} %bitcast.me_ref, s32[8]{0:T(128)S(1)} %broadcast_xor_fusion.ids_ref, f32[256,768]{1,0:T(8,128)S(1)} %join.3.near_ref, f32[256,768]{1,0:T(8,128)S(1)} %collective-permute-done.3.far_ref, ...), custom_call_target="tpu_custom_call" | custom-call | tf_op jit(solution)/shard_map/turn/pallas_call | solution.py:398
  31.4 2.1 %update.1.part_ref = f32[768,384]{1,0:T(8,128)S(1)} custom-call(s32[1]{0:T(128)} %bitcast.me_ref, s32[8]{0:T(128)S(1)} %broadcast_xor_fusion.ids_ref, f32[768,384]{1,0:T(8,128)S(1)} %get-tuple-element.19.rows_ref, bf16[768,512]{1,0:T(8,128)(2,1)S(1)} %get-tuple-element.27.high_ref, bf16[768,512]{1,0:T(8,128)(2,1)S(1)} %get-tuple-element.28.low_ref, ...), custom_call_target="tpu_custom_call" | custom-call | tf_op jit(solution)/shard_map/update/pallas_call | solution.py:409
  33.5 0.0 collective-permute-done.8.refs_7_
  33.5 2.5 %finish.1 = f32[768,384]{1,0:T(8,128)} custom-call(s32[1]{0:T(128)} %bitcast.me_ref, f32[768,384]{1,0:T(8,128)S(1)} %update.1.part_ref, bf16[768,512]{1,0:T(8,128)(2,1)S(1)} %get-tuple-element.31.high_ref, bf16[768,512]{1,0:T(8,128)(2,1)S(1)} %get-tuple-element.32.low_ref, f32[128,384]{1,0:T(8,128)S(1)} %get-tuple-element.21.refs_0_, ...), custom_call_target="tpu_custom_call" | custom-call | tf_op jit(solution)/shard_map/finish/pallas_call | solution.py:420
  (9 shorter events, 0.1 us)
Async XLA Ops:
  2.5 10.0 %collective-permute-start.1 = (f32[128,384]{1,0:T(8,128)S(1)}, f32[128,384]{1,0:T(8,128)S(1)}, u32[]{:S(2)}, u32[]{:S(2)}) collective-permute-start(f32[128,384]{1,0:T(8,128)S(1)} %get-tuple-element.21.refs_0_), channel_id=1, source_target_pairs={{0,16},{16,8},{8,0},{1,17},{17,9},{9,1},{2,18},{18,10},{10,2},{3,1... | collective-permute-start | bytes 589832 | tf_op jit(solution)/shard_map/ppermute | solution.py:349
  6.1 6.5 %collective-permute-start = (f32[64,768]{1,0:T(8,128)S(1)}, f32[64,768]{1,0:T(8,128)S(1)}, u32[]{:S(2)}, u32[]{:S(2)}) collective-permute-start(f32[64,768]{1,0:T(8,128)S(1)} %get-tuple-element.20.first), channel_id=1, source_target_pairs={{0,4},{1,5},{2,6},{3,7},{4,0},{5,1},{6,2},{7,3},{8,12},{9,13},{10,... | collective-permute-start | bytes 589832 | tf_op jit(solution)/shard_map/ppermute | solution.py:291
  7.4 13.1 %collective-permute-start.4 = (f32[128,384]{1,0:T(8,128)S(1)}, f32[128,384]{1,0:T(8,128)S(1)}, u32[]{:S(2)}, u32[]{:S(2)}) collective-permute-start(f32[128,384]{1,0:T(8,128)S(1)} %get-tuple-element.29.refs_1_), channel_id=1, source_target_pairs={{0,16},{24,8},{16,24},{1,17},{25,9},{17,25},{2,18},{26,10},{18,26}... | collective-permute-start | bytes 589832 | tf_op jit(solution)/shard_map/ppermute | solution.py:349
  9.5 11.9 %collective-permute-start.5 = (f32[128,384]{1,0:T(8,128)S(1)}, f32[128,384]{1,0:T(8,128)S(1)}, u32[]{:S(2)}, u32[]{:S(2)}) collective-permute-start(f32[128,384]{1,0:T(8,128)S(1)} %get-tuple-element.30), channel_id=1, source_target_pairs={{24,16},{0,8},{8,24},{16,0},{25,17},{1,9},{9,25},{17,1},{26,18},{2... | collective-permute-start | bytes 589832 | tf_op jit(solution)/shard_map/ppermute | solution.py:349
  12.5 0.9 %copy-start = (s32[8]{0:T(128)S(1)}, s32[8]{0:T(128)}, u32[]{:S(2)}) copy-start(s32[8]{0:T(128)} %constant.12.clone) | copy-start | bytes 100
  13.2 9.7 %collective-permute-start.2 = (f32[128,768]{1,0:T(8,128)S(1)}, f32[128,768]{1,0:T(8,128)S(1)}, u32[]{:S(2)}, u32[]{:S(2)}) collective-permute-start(f32[128,768]{1,0:T(8,128)S(1)} %join.2.first), channel_id=1, source_target_pairs={{0,2},{1,3},{2,0},{3,1},{4,6},{5,7},{6,4},{7,5},{8,10},{9,11},{10,... | collective-permute-start | bytes 1179656 | tf_op jit(solution)/shard_map/ppermute | solution.py:291
  13.5 14.0 %collective-permute-start.6 = (f32[128,384]{1,0:T(8,128)S(1)}, f32[128,384]{1,0:T(8,128)S(1)}, u32[]{:S(2)}, u32[]{:S(2)}) collective-permute-start(f32[128,384]{1,0:T(8,128)S(1)} %get-tuple-element.34.refs_0_), channel_id=1, source_target_pairs={{16,24},{0,16},{24,0},{17,25},{1,17},{25,1},{18,26},{2,18},{26,2},... | collective-permute-start | bytes 589832 | tf_op jit(solution)/shard_map/ppermute | solution.py:349
  17.7 15.8 %collective-permute-start.7 = (f32[128,384]{1,0:T(8,128)S(1)}, f32[128,384]{1,0:T(8,128)S(1)}, u32[]{:S(2)}, u32[]{:S(2)}) collective-permute-start(f32[128,384]{1,0:T(8,128)S(1)} %get-tuple-element.33.refs_1_), channel_id=1, source_target_pairs={{16,8},{0,24},{8,16},{17,9},{1,25},{9,17},{18,10},{2,26},{10,18},{... | collective-permute-start | bytes 589832 | tf_op jit(solution)/shard_map/ppermute | solution.py:349
  21.4 12.1 %collective-permute-start.8 = (f32[128,384]{1,0:T(8,128)S(1)}, f32[128,384]{1,0:T(8,128)S(1)}, u32[]{:S(2)}, u32[]{:S(2)}) collective-permute-start(f32[128,384]{1,0:T(8,128)S(1)} %broadcast_select_fusion), channel_id=1, source_target_pairs={{16,24},{17,25},{18,26},{19,27},{20,28},{21,29},{22,30},{23,31}} | collective-permute-start | bytes 589832 | tf_op jit(solution)/shard_map/ppermute | solution.py:349
  22.1 11.4 %collective-permute-start.9 = (f32[128,384]{1,0:T(8,128)S(1)}, f32[128,384]{1,0:T(8,128)S(1)}, u32[]{:S(2)}, u32[]{:S(2)}) collective-permute-start(f32[128,384]{1,0:T(8,128)S(1)} %broadcast_select_fusion), channel_id=1, source_target_pairs={{16,8},{17,9},{18,10},{19,11},{20,12},{21,13},{22,14},{23,15}} | collective-permute-start | bytes 589832 | tf_op jit(solution)/shard_map/ppermute | solution.py:349
  23.2 6.2 %collective-permute-start.3 = (f32[256,768]{1,0:T(8,128)S(1)}, f32[256,768]{1,0:T(8,128)S(1)}, u32[]{:S(2)}, u32[]{:S(2)}) collective-permute-start(f32[256,768]{1,0:T(8,128)S(1)} %join.3.near_ref), channel_id=1, source_target_pairs={{0,1},{1,0},{2,3},{3,2},{4,5},{5,4},{6,7},{7,6},{8,9},{9,8},{10,11... | collective-permute-start | bytes 2359304 | tf_op jit(solution)/shard_map/ppermute | solution.py:291

commit v6 on v5

--- a/solution.py
+++ b/solution.py
@@ -184,12 +184,8 @@
 
 def turn_kernel(me_ref, ids_ref, near_ref, far_ref, inv_high, inv_low, land_ref, *refs):
     high_ref, low_ref, end_high, end_low, order_high, order_low = refs
-    half = near_ref.shape[0]
+    half, rows = near_ref.shape
     width, picked_rows = order_high.shape
-    for k, part in enumerate((near_ref, far_ref)):
-        high, low = halves(-part[...])
-        high_ref[:, k * half : (k + 1) * half] = high.T
-        low_ref[:, k * half : (k + 1) * half] = low.T
     first = inv_high.shape[1] - picked_rows
     depth = width // ids_ref.shape[0]
     for k in range(ids_ref.shape[0]):
@@ -197,16 +193,27 @@
         part = pl.ds(k * depth, depth)
         order_high[part, :] = inv_high[source, first:].astype(F32)
         order_low[part, :] = inv_low[source, first:].astype(F32)
-    pan_high, last_high = high_ref[...], order_high[...].astype(BF16)
-    value = mm(low_ref[...], last_high) + mm(pan_high, order_low[...].astype(BF16)) + mm(pan_high, last_high)
-    end_high[:, :picked_rows], end_low[:, :picked_rows] = halves(value)
     end_high[:, picked_rows:] = land_ref[...]
     end_low[:, picked_rows:] = jnp.zeros(land_ref.shape, BF16)
 
+    def work(start):
+        for k, part in enumerate((near_ref, far_ref)):
+            high, low = halves(-part[:, start:])
+            high_ref[start:, k * half : (k + 1) * half] = high.T
+            low_ref[start:, k * half : (k + 1) * half] = low.T
+        pan_high, last_high = high_ref[start:, :], order_high[...].astype(BF16)
+        value = mm(low_ref[start:, :], last_high) + mm(pan_high, order_low[...].astype(BF16)) + mm(pan_high, last_high)
+        end_high[start:, :picked_rows], end_low[start:, :picked_rows] = halves(value)
+
     @pl.when(me_ref[0] == 0)
     def _():
+        work(width)
         end_high[:width, :picked_rows] = inv_high[:, first:]
         end_low[:width, :picked_rows] = inv_low[:, first:]
+
+    @pl.when(me_ref[0] != 0)
+    def _():
+        work(0)
 
 
 def collect(places, me, arrays, row_high, row_low):
@@ -239,21 +246,37 @@
         source = pl.multiple_of(ids_ref[k] * depth, depth)
         part = pl.ds(k * depth, depth)
         up_high[part, :], up_low[part, :] = halves(upper_ref[pl.ds(source, depth), :])
-    high = high_ref[...]
-    part = mm(low_ref[...], up_high[...]) + mm(high, up_low[...]) + mm(high, up_high[...])
-    out_ref[...] = rows_ref[...] + part
+
+    def work(start):
+        high = high_ref[start:, :]
+        part = mm(low_ref[start:, :], up_high[...]) + mm(high, up_low[...]) + mm(high, up_high[...])
+        out_ref[start:, :] = rows_ref[start:, :] + part
 
     @pl.when(me_ref[0] == 0)
     def _():
+        work(width)
         out_ref[:width, :] = upper_ref[...]
 
+    @pl.when(me_ref[0] != 0)
+    def _():
+        work(0)
+
 
 def finish_kernel(places, me_ref, part_ref, high_ref, low_ref, *refs):
-    arrays, (out_ref, row_high, row_low) = refs[:-3], refs[-3:]
+    arrays, (out_ref, row_high, row_low, total, sem) = refs[:-5], refs[-5:]
     collect(places, me_ref[0], arrays, row_high, row_low)
-    high = high_ref[...]
-    value = mm(low_ref[...], row_high[...]) + mm(high, row_low[...]) + mm(high, row_high[...])
-    out_ref[...] = part_ref[...] + value
+    rows = part_ref.shape[0]
+    step = rows // sem.shape[0]
+    copies = []
+    for k in range(sem.shape[0]):
+        part = pl.ds(k * step, step)
+        high = high_ref[part, :]
+        value = mm(low_ref[part, :], row_high[...]) + mm(high, row_low[...]) + mm(high, row_high[...])
+        total[part, :] = part_ref[part, :] + value
+        copies.append(pltpu.make_async_copy(total.at[part], out_ref.at[part], sem.at[k]))
+        copies[-1].start()
+    for copy in copies:
+        copy.wait()
 
 
 def join_kernel(first, second, *refs):
@@ -417,12 +440,14 @@
     )(here, ids, base, pan_high, pan_low, upper)
 
     late_arrays, (late,) = used(late)
+    steps = next(k for k in (3, 2, 1) if rows % (k * 16) == 0)
     return pl.pallas_call(
         functools.partial(finish_kernel, late),
         out_shape=jax.ShapeDtypeStruct((rows, cols), F32),
         in_specs=[SMEM] + [VMEM] * (3 + len(late_arrays)),
-        out_specs=VMEM,
-        scratch_shapes=[pltpu.VMEM((late_rows + slot, cols), BF16)] * 2,
+        out_specs=HBM,
+        scratch_shapes=[pltpu.VMEM((late_rows + slot, cols), BF16)] * 2
+        + [pltpu.VMEM((rows, cols), F32), pltpu.SemaphoreType.DMA((steps,))],
         compiler_params=PARAMS,
         name="finish",
     )(here, part, end_high, end_low, *late_arrays)

time: 36.3 us -> 35.7 us (0.983)
  the two profiles are of different devices: /device:TPU:3 before, /device:TPU:23 now
where the time goes in v6:
time: 35.7 us; the launch traced here: 35.4 us
  starting transfers between devices  19.8 us (55%)
  Pallas kernels  12.9 us (36%)
  waiting for transfers between devices  2.44 us (7%)
    ppermute x7, starting transfers between devices, local(): lax.ppermute(operand, 'row', [(s, t) for s, t, item in moves])  18.2 us
    pallas_call x1, Pallas kernels, local(): pl.pallas_call(functools.partial(prepare_kernel, row_count), out_shape=(j...  2.92 us
    pallas_call x1, Pallas kernels, local(): pl.pallas_call(functools.partial(finish_kernel, late), out_shape=jax.Shap...  2.33 us
    pallas_call x1, Pallas kernels, local(): pl.pallas_call(turn_kernel, out_shape=(jax.ShapeDtypeStruct((rows, width)...  2.13 us
    pallas_call x1, Pallas kernels, local(): pl.pallas_call(update_kernel, out_shape=jax.ShapeDtypeStruct((rows, cols)...  2.06 us
    pallas_call x1, Pallas kernels, local(): pl.pallas_call(functools.partial(pick_kernel, row_count, order), out_shap...  1.91 us
    ppermute x3, starting transfers between devices, gather_shards(): other = lax.ppermute(held, 'col', [(i, i ^ bit) for i in range(count)])  1.65 us
    ppermute x3, waiting for transfers between devices, gather_shards(): other = lax.ppermute(held, 'col', [(i, i ^ bit) for i in range(count)])  1.28 us
  transfers between devices with their start and end apart: 10, of which 2 were waited for; matrix products, arithmetic and copies ran while one was open for 0% of the time, Pallas kernels for 24%

profile of v6, /device:TPU:23, one launch (start us, length us, event | category | flops | bytes accessed | tf_op | source)
XLA Modules:
  0.0 35.4 jit_solution(8025816828958878286)
XLA Ops:
  0.0 1.9 %pick.1 = (f32[128,384]{1,0:T(8,128)S(1)}, f32[128,384]{1,0:T(8,128)S(1)}, f32[128,384]{1,0:T(8,128)S(1)}, f32[128,384]{1,0:T(8,128)S(1)}, f32[128,384]{1,0:T(8,128)S(1)}, /*index=5*/f32[64,768]{1,0:T(8,128)S(1)}) custom-call(s32[1]{0:T(128)} %bitcast.me_ref, s32[1,512]{1,0:T(1,128)} %bitcast.2, f32[768,384]{1,0:T(8,128)} %matrix_ref.3, f32[64,768]{1,0:T(8,128)} %panel_ref.1), custom_call_target="tpu_custom_call" | custom-call | tf_op jit(solution)/shard_map/pick/pallas_call | solution.py:340
  1.9 2.1 %collective-permute-start.1 = (f32[128,384]{1,0:T(8,128)S(1)}, f32[128,384]{1,0:T(8,128)S(1)}, u32[]{:S(2)}, u32[]{:S(2)}) collective-permute-start(f32[128,384]{1,0:T(8,128)S(1)} %get-tuple-element.21.refs_0_), channel_id=1, source_target_pairs={{0,16},{16,8},{8,0},{1,17},{17,9},{9,1},{2,18},{18,10},{10,2},{3,1... | collective-permute-start | bytes 589832 | tf_op jit(solution)/shard_map/ppermute | solution.py:372
  4.0 0.3 collective-permute-start
  4.3 1.9 %collective-permute-start.4 = (f32[128,384]{1,0:T(8,128)S(1)}, f32[128,384]{1,0:T(8,128)S(1)}, u32[]{:S(2)}, u32[]{:S(2)}) collective-permute-start(f32[128,384]{1,0:T(8,128)S(1)} %get-tuple-element.29.refs_1_), channel_id=1, source_target_pairs={{0,16},{24,8},{16,24},{1,17},{25,9},{17,25},{2,18},{26,10},{18,26}... | collective-permute-start | bytes 589832 | tf_op jit(solution)/shard_map/ppermute | solution.py:372
  6.2 2.4 %collective-permute-start.5 = (f32[128,384]{1,0:T(8,128)S(1)}, f32[128,384]{1,0:T(8,128)S(1)}, u32[]{:S(2)}, u32[]{:S(2)}) collective-permute-start(f32[128,384]{1,0:T(8,128)S(1)} %get-tuple-element.30), channel_id=1, source_target_pairs={{24,16},{0,8},{8,24},{16,0},{25,17},{1,9},{9,25},{17,1},{26,18},{2... | collective-permute-start | bytes 589832 | tf_op jit(solution)/shard_map/ppermute | solution.py:372
  8.6 2.9 %prepare.1 = (bf16[512,640]{1,0:T(8,128)(2,1)S(1)}, bf16[512,640]{1,0:T(8,128)(2,1)S(1)}, bf16[768,128]{1,0:T(8,128)(2,1)S(1)}, f32[768,384]{1,0:T(8,128)S(1)}) custom-call(s32[1]{0:T(128)} %bitcast.me_ref, s32[1,512]{1,0:T(1,128)} %bitcast.3, f32[512,512]{1,0:T(8,128)} %inverse_ref.1, f32[768,384]{1,0:T(8,128)} %matrix_ref.3), custom_call_target="tpu_custom_call" | custom-call | flops 1000000 | bytes 100000 | tf_op jit(solution)/shard_map/prepare/pallas_call | solution.py:381
  11.6 0.0 copy-start
  11.6 0.5 %join.2.first = f32[128,768]{1,0:T(8,128)S(1)} custom-call(f32[64,768]{1,0:T(8,128)S(1)} %get-tuple-element.20.first, f32[64,768]{1,0:T(8,128)S(1)} %collective-permute-done.second, f32[128,384]{1,0:T(8,128)S(1)} %get-tuple-element.34.refs_0_, f32[128,384]{1,0:T(8,128)S(1)} %get-tuple-element.33.refs_1_, bf16[768,128]{1,0:T(8,128)(2,1)S(1)} %get-tuple-element.24.refs_2_.land_ref), custom_call_target="tpu_custom_call" | custom-call | tf_op jit(solution)/shard_map/join/pallas_call | solution.py:297
  12.2 0.3 collective-permute-start.2
  12.5 1.9 %collective-permute-start.6 = (f32[128,384]{1,0:T(8,128)S(1)}, f32[128,384]{1,0:T(8,128)S(1)}, u32[]{:S(2)}, u32[]{:S(2)}) collective-permute-start(f32[128,384]{1,0:T(8,128)S(1)} %get-tuple-element.34.refs_0_), channel_id=1, source_target_pairs={{16,24},{0,16},{24,0},{17,25},{1,17},{25,1},{18,26},{2,18},{26,2},... | collective-permute-start | bytes 589832 | tf_op jit(solution)/shard_map/ppermute | solution.py:372
  14.4 1.9 %collective-permute-start.7 = (f32[128,384]{1,0:T(8,128)S(1)}, f32[128,384]{1,0:T(8,128)S(1)}, u32[]{:S(2)}, u32[]{:S(2)}) collective-permute-start(f32[128,384]{1,0:T(8,128)S(1)} %get-tuple-element.33.refs_1_), channel_id=1, source_target_pairs={{16,8},{0,24},{8,16},{17,9},{1,25},{9,17},{18,10},{2,26},{10,18},{... | collective-permute-start | bytes 589832 | tf_op jit(solution)/shard_map/ppermute | solution.py:372
  16.3 0.0 collective-permute-done.4.refs_2_.refs_3_
  16.4 1.1 %collective-permute-done.5.refs_3_.refs_4_ = f32[128,384]{1,0:T(8,128)S(1)} collective-permute-done((f32[128,384]{1,0:T(8,128)S(1)}, f32[128,384]{1,0:T(8,128)S(1)}, u32[]{:S(2)}, u32[]{:S(2)}) %collective-permute-start.5) | collective-permute-done | bytes 196640 | tf_op jit(solution)/shard_map/ppermute | solution.py:372
  17.5 6.7 %collective-permute-start.8 = (f32[128,384]{1,0:T(8,128)S(1)}, f32[128,384]{1,0:T(8,128)S(1)}, u32[]{:S(2)}, u32[]{:S(2)}) collective-permute-start(f32[128,384]{1,0:T(8,128)S(1)} %broadcast_select_fusion), channel_id=1, source_target_pairs={{16,24},{17,25},{18,26},{19,27},{20,28},{21,29},{22,30},{23,31}} | collective-permute-start | bytes 589832 | tf_op jit(solution)/shard_map/ppermute | solution.py:372
  24.2 1.3 %collective-permute-start.9 = (f32[128,384]{1,0:T(8,128)S(1)}, f32[128,384]{1,0:T(8,128)S(1)}, u32[]{:S(2)}, u32[]{:S(2)}) collective-permute-start(f32[128,384]{1,0:T(8,128)S(1)} %broadcast_select_fusion), channel_id=1, source_target_pairs={{16,8},{17,9},{18,10},{19,11},{20,12},{21,13},{22,14},{23,15}} | collective-permute-start | bytes 589832 | tf_op jit(solution)/shard_map/ppermute | solution.py:372
  25.5 0.0 collective-permute-done.2.second
  25.5 0.4 %join.3.near_ref = f32[256,768]{1,0:T(8,128)S(1)} custom-call(f32[128,768]{1,0:T(8,128)S(1)} %join.2.first, f32[128,768]{1,0:T(8,128)S(1)} %collective-permute-done.2.second), custom_call_target="tpu_custom_call" | custom-call | tf_op jit(solution)/shard_map/join/pallas_call | solution.py:297
  25.9 1.0 %collective-permute-start.3 = (f32[256,768]{1,0:T(8,128)S(1)}, f32[256,768]{1,0:T(8,128)S(1)}, u32[]{:S(2)}, u32[]{:S(2)}) collective-permute-start(f32[256,768]{1,0:T(8,128)S(1)} %join.3.near_ref), channel_id=1, source_target_pairs={{0,1},{1,0},{2,3},{3,2},{4,5},{5,4},{6,7},{7,6},{8,9},{9,8},{10,11... | collective-permute-start | bytes 2359304 | tf_op jit(solution)/shard_map/ppermute | solution.py:314
  26.9 0.0 collective-permute-done.6.refs_4_.refs_5_
  26.9 0.6 %upper.1.upper_ref = f32[512,384]{1,0:T(8,128)S(1)} custom-call(s32[1]{0:T(128)} %bitcast.me_ref, bf16[512,640]{1,0:T(8,128)(2,1)S(1)} %get-tuple-element.25.inv_high.high_ref, bf16[512,640]{1,0:T(8,128)(2,1)S(1)} %get-tuple-element.26.inv_low.low_ref, f32[128,384]{1,0:T(8,128)S(1)} %get-tuple-element.21.refs_0_, ...), custom_call_target="tpu_custom_call" | custom-call | flops 40000000000 | bytes 100000000 | tf_op jit(solution)/shard_map/upper/pallas_call | solution.py:410
  27.6 1.3 %collective-permute-done.3.far_ref = f32[256,768]{1,0:T(8,128)S(1)} collective-permute-done((f32[256,768]{1,0:T(8,128)S(1)}, f32[256,768]{1,0:T(8,128)S(1)}, u32[]{:S(2)}, u32[]{:S(2)}) %collective-permute-start.3) | collective-permute-done | bytes 786464 | tf_op jit(solution)/shard_map/ppermute | solution.py:314
  28.9 2.1 %turn.1 = (bf16[768,512]{1,0:T(8,128)(2,1)S(1)}, bf16[768,512]{1,0:T(8,128)(2,1)S(1)}, bf16[768,512]{1,0:T(8,128)(2,1)S(1)}, bf16[768,512]{1,0:T(8,128)(2,1)S(1)}) custom-call(s32[1]{0:T(128)} %bitcast.me_ref, s32[8]{0:T(128)S(1)} %broadcast_xor_fusion.ids_ref, f32[256,768]{1,0:T(8,128)S(1)} %join.3.near_ref, f32[256,768]{1,0:T(8,128)S(1)} %collective-permute-done.3.far_ref, ...), custom_call_target="tpu_custom_call" | custom-call | tf_op jit(solution)/shard_map/turn/pallas_call | solution.py:421
  31.0 2.1 %update.1.part_ref = f32[768,384]{1,0:T(8,128)S(1)} custom-call(s32[1]{0:T(128)} %bitcast.me_ref, s32[8]{0:T(128)S(1)} %broadcast_xor_fusion.ids_ref, f32[768,384]{1,0:T(8,128)S(1)} %get-tuple-element.19.rows_ref, bf16[768,512]{1,0:T(8,128)(2,1)S(1)} %get-tuple-element.27.high_ref, bf16[768,512]{1,0:T(8,128)(2,1)S(1)} %get-tuple-element.28.low_ref, ...), custom_call_target="tpu_custom_call" | custom-call | tf_op jit(solution)/shard_map/update/pallas_call | solution.py:432
  33.1 2.3 %finish.1 = f32[768,384]{1,0:T(8,128)} custom-call(s32[1]{0:T(128)} %bitcast.me_ref, f32[768,384]{1,0:T(8,128)S(1)} %update.1.part_ref, bf16[768,512]{1,0:T(8,128)(2,1)S(1)} %get-tuple-element.31.high_ref, bf16[768,512]{1,0:T(8,128)(2,1)S(1)} %get-tuple-element.32.low_ref, f32[128,384]{1,0:T(8,128)S(1)} %get-tuple-element.21.refs_0_, ...), custom_call_target="tpu_custom_call" | custom-call | tf_op jit(solution)/shard_map/finish/pallas_call | solution.py:444
  (9 shorter events, 0.1 us)
Async XLA Ops:
  1.9 9.6 %collective-permute-start.1 = (f32[128,384]{1,0:T(8,128)S(1)}, f32[128,384]{1,0:T(8,128)S(1)}, u32[]{:S(2)}, u32[]{:S(2)}) collective-permute-start(f32[128,384]{1,0:T(8,128)S(1)} %get-tuple-element.21.refs_0_), channel_id=1, source_target_pairs={{0,16},{16,8},{8,0},{1,17},{17,9},{9,1},{2,18},{18,10},{10,2},{3,1... | collective-permute-start | bytes 589832 | tf_op jit(solution)/shard_map/ppermute | solution.py:372
  4.0 7.6 %collective-permute-start = (f32[64,768]{1,0:T(8,128)S(1)}, f32[64,768]{1,0:T(8,128)S(1)}, u32[]{:S(2)}, u32[]{:S(2)}) collective-permute-start(f32[64,768]{1,0:T(8,128)S(1)} %get-tuple-element.20.first), channel_id=1, source_target_pairs={{0,4},{1,5},{2,6},{3,7},{4,0},{5,1},{6,2},{7,3},{8,12},{9,13},{10,... | collective-permute-start | bytes 589832 | tf_op jit(solution)/shard_map/ppermute | solution.py:314
  4.3 12.1 %collective-permute-start.4 = (f32[128,384]{1,0:T(8,128)S(1)}, f32[128,384]{1,0:T(8,128)S(1)}, u32[]{:S(2)}, u32[]{:S(2)}) collective-permute-start(f32[128,384]{1,0:T(8,128)S(1)} %get-tuple-element.29.refs_1_), channel_id=1, source_target_pairs={{0,16},{24,8},{16,24},{1,17},{25,9},{17,25},{2,18},{26,10},{18,26}... | collective-permute-start | bytes 589832 | tf_op jit(solution)/shard_map/ppermute | solution.py:372
  6.2 11.3 %collective-permute-start.5 = (f32[128,384]{1,0:T(8,128)S(1)}, f32[128,384]{1,0:T(8,128)S(1)}, u32[]{:S(2)}, u32[]{:S(2)}) collective-permute-start(f32[128,384]{1,0:T(8,128)S(1)} %get-tuple-element.30), channel_id=1, source_target_pairs={{24,16},{0,8},{8,24},{16,0},{25,17},{1,9},{9,25},{17,1},{26,18},{2... | collective-permute-start | bytes 589832 | tf_op jit(solution)/shard_map/ppermute | solution.py:372
  11.6 0.9 %copy-start = (s32[8]{0:T(128)S(1)}, s32[8]{0:T(128)}, u32[]{:S(2)}) copy-start(s32[8]{0:T(128)} %constant.12.clone) | copy-start | bytes 100
  12.2 13.3 %collective-permute-start.2 = (f32[128,768]{1,0:T(8,128)S(1)}, f32[128,768]{1,0:T(8,128)S(1)}, u32[]{:S(2)}, u32[]{:S(2)}) collective-permute-start(f32[128,768]{1,0:T(8,128)S(1)} %join.2.first), channel_id=1, source_target_pairs={{0,2},{1,3},{2,0},{3,1},{4,6},{5,7},{6,4},{7,5},{8,10},{9,11},{10,... | collective-permute-start | bytes 1179656 | tf_op jit(solution)/shard_map/ppermute | solution.py:314
  12.5 14.5 %collective-permute-start.6 = (f32[128,384]{1,0:T(8,128)S(1)}, f32[128,384]{1,0:T(8,128)S(1)}, u32[]{:S(2)}, u32[]{:S(2)}) collective-permute-start(f32[128,384]{1,0:T(8,128)S(1)} %get-tuple-element.34.refs_0_), channel_id=1, source_target_pairs={{16,24},{0,16},{24,0},{17,25},{1,17},{25,1},{18,26},{2,18},{26,2},... | collective-permute-start | bytes 589832 | tf_op jit(solution)/shard_map/ppermute | solution.py:372
  14.4 18.7 %collective-permute-start.7 = (f32[128,384]{1,0:T(8,128)S(1)}, f32[128,384]{1,0:T(8,128)S(1)}, u32[]{:S(2)}, u32[]{:S(2)}) collective-permute-start(f32[128,384]{1,0:T(8,128)S(1)} %get-tuple-element.33.refs_1_), channel_id=1, source_target_pairs={{16,8},{0,24},{8,16},{17,9},{1,25},{9,17},{18,10},{2,26},{10,18},{... | collective-permute-start | bytes 589832 | tf_op jit(solution)/shard_map/ppermute | solution.py:372
  17.5 15.6 %collective-permute-start.8 = (f32[128,384]{1,0:T(8,128)S(1)}, f32[128,384]{1,0:T(8,128)S(1)}, u32[]{:S(2)}, u32[]{:S(2)}) collective-permute-start(f32[128,384]{1,0:T(8,128)S(1)} %broadcast_select_fusion), channel_id=1, source_target_pairs={{16,24},{17,25},{18,26},{19,27},{20,28},{21,29},{22,30},{23,31}} | collective-permute-start | bytes 589832 | tf_op jit(solution)/shard_map/ppermute | solution.py:372
  24.2 8.9 %collective-permute-start.9 = (f32[128,384]{1,0:T(8,128)S(1)}, f32[128,384]{1,0:T(8,128)S(1)}, u32[]{:S(2)}, u32[]{:S(2)}) collective-permute-start(f32[128,384]{1,0:T(8,128)S(1)} %broadcast_select_fusion), channel_id=1, source_target_pairs={{16,8},{17,9},{18,10},{19,11},{20,12},{21,13},{22,14},{23,15}} | collective-permute-start | bytes 589832 | tf_op jit(solution)/shard_map/ppermute | solution.py:372
  25.9 3.0 %collective-permute-start.3 = (f32[256,768]{1,0:T(8,128)S(1)}, f32[256,768]{1,0:T(8,128)S(1)}, u32[]{:S(2)}, u32[]{:S(2)}) collective-permute-start(f32[256,768]{1,0:T(8,128)S(1)} %join.3.near_ref), channel_id=1, source_target_pairs={{0,1},{1,0},{2,3},{3,2},{4,5},{5,4},{6,7},{7,6},{8,9},{9,8},{10,11... | collective-permute-start | bytes 2359304 | tf_op jit(solution)/shard_map/ppermute | solution.py:314

commit v7 on v6

--- a/solution.py
+++ b/solution.py
@@ -22,14 +22,6 @@
     high = x.astype(BF16)
     low = (x - high.astype(F32)).astype(BF16)
     return high, low
-
-
-def thirds(x):
-    high = x.astype(BF16)
-    rest = x - high.astype(F32)
-    middle = rest.astype(BF16)
-    low = (rest - middle.astype(F32)).astype(BF16)
-    return high, middle, low
 
 
 def mm(a, b):
@@ -64,9 +56,16 @@
     return (slot == position).astype(BF16)
 
 
-def picked(pick, rows):
-    high, middle, low = thirds(rows)
-    return mm(pick, low) + mm(pick, middle) + mm(pick, high)
+def picked(pick, rows_ref, copies):
+    step = rows_ref.shape[0] // len(copies)
+    total = None
+    for k in range(pick.shape[1] // step):
+        copies[k].wait()
+        high, low = halves(rows_ref[k * step : (k + 1) * step, :])
+        part = pick[:, k * step : (k + 1) * step]
+        value = mm(part, low) + mm(part, high)
+        total = value if total is None else total + value
+    return total
 
 
 def plan(count):
@@ -110,18 +109,19 @@
     slot = width // count
     me = me_ref[0]
     point = pltpu.make_async_copy(pivot_ref, pivot_v, sem.at[0])
-    head = pltpu.make_async_copy(matrix_ref.at[:width], rows_ref.at[:width], sem.at[1])
-    tail = pltpu.make_async_copy(matrix_ref.at[width:], rows_ref.at[width:], sem.at[2])
-    panel = pltpu.make_async_copy(panel_ref, panel_out, sem.at[3])
+    panel = pltpu.make_async_copy(panel_ref, panel_out, sem.at[1])
+    step = rows // (sem.shape[0] - 2)
+    copies = [
+        pltpu.make_async_copy(matrix_ref.at[pl.ds(k * step, step)], rows_ref.at[pl.ds(k * step, step)], sem.at[2 + k])
+        for k in range(rows // step)
+    ]
     point.start()
-    head.start()
-    tail.start()
+    for copy in copies:
+        copy.start()
     panel.start()
     point.wait()
     pivot = pivot_v[...]
     kind, place = classify(pivot, count, rows)
-    head.wait()
-    tail.wait()
 
     @pl.when(me == 0)
     def _():
@@ -132,16 +132,18 @@
             else:
                 inside = (kind == 0) & (place >= which * slot) & (place < (which + 1) * slot)
                 start = jnp.where(inside, (k - which) * slot, start)
-        got = picked(one_hot(start + place, len(order) * slot), rows_ref[:width, :])
+        got = picked(one_hot(start + place, len(order) * slot), rows_ref, copies)
         for k, out in enumerate(outs):
             out[...] = got[k * slot : (k + 1) * slot, :]
+        for copy in copies[width // step :]:
+            copy.wait()
 
     @pl.when(me != 0)
     def _():
         mine = lax.broadcasted_iota(jnp.int32, (slot, width), 0) == jnp.where(kind == me, place, -1)
         source = jnp.sum(jnp.where(mine, pivot - me * rows, 0), axis=1, keepdims=True)
         pick = (lax.broadcasted_iota(jnp.int32, (slot, rows), 1) == source).astype(BF16)
-        got = picked(pick, rows_ref[...])
+        got = picked(pick, rows_ref, copies)
         for out in outs:
             out[...] = got
 
@@ -182,38 +184,53 @@
     base_ref[...] = jnp.where(taken > 0.5, 0.0, rows_ref[...])
 
 
-def turn_kernel(me_ref, ids_ref, near_ref, far_ref, inv_high, inv_low, land_ref, *refs):
-    high_ref, low_ref, end_high, end_low, order_high, order_low = refs
-    half, rows = near_ref.shape
-    width, picked_rows = order_high.shape
+def share_kernel(first_shard, last, me_ref, ids_ref, shards_ref, inv_high, inv_low, upper_ref, rows_ref, *refs):
+    if last:
+        ends_ref, land_ref = refs[:2]
+    out_ref, end_high, end_low = refs[2:5] if last else (*refs[:2], None)
+    high_ref, low_ref, side_high, side_low = refs[-4:]
+    half, rows = shards_ref.shape
+    width, cols = upper_ref.shape
+    depth = width // ids_ref.shape[0]
+    picked_rows = side_high.shape[1] - cols
     first = inv_high.shape[1] - picked_rows
-    depth = width // ids_ref.shape[0]
-    for k in range(ids_ref.shape[0]):
-        source = pl.ds(pl.multiple_of(ids_ref[k] * depth, depth), depth)
+    for k in range(half // depth):
+        source = pl.ds(pl.multiple_of(ids_ref[first_shard + k] * depth, depth), depth)
         part = pl.ds(k * depth, depth)
-        order_high[part, :] = inv_high[source, first:].astype(F32)
-        order_low[part, :] = inv_low[source, first:].astype(F32)
-    end_high[:, picked_rows:] = land_ref[...]
-    end_low[:, picked_rows:] = jnp.zeros(land_ref.shape, BF16)
+        high, low = halves(upper_ref[source, :])
+        side_high[part, :cols], side_low[part, :cols] = high.astype(F32), low.astype(F32)
+        side_high[part, cols:] = inv_high[source, first:].astype(F32)
+        side_low[part, cols:] = inv_low[source, first:].astype(F32)
 
     def work(start):
-        for k, part in enumerate((near_ref, far_ref)):
-            high, low = halves(-part[:, start:])
-            high_ref[start:, k * half : (k + 1) * half] = high.T
-            low_ref[start:, k * half : (k + 1) * half] = low.T
-        pan_high, last_high = high_ref[start:, :], order_high[...].astype(BF16)
-        value = mm(low_ref[start:, :], last_high) + mm(pan_high, order_low[...].astype(BF16)) + mm(pan_high, last_high)
-        end_high[start:, :picked_rows], end_low[start:, :picked_rows] = halves(value)
+        high, low = halves(-shards_ref[:, start:])
+        high_ref[start:, :] = high.T
+        low_ref[start:, :] = low.T
+        pan_high, right = high_ref[start:, :], side_high[...].astype(BF16)
+        value = mm(low_ref[start:, :], right) + mm(pan_high, side_low[...].astype(BF16)) + mm(pan_high, right)
+        out_ref[start:, :] = rows_ref[start:, :] + value[:, :cols]
+        if last:
+            end_high[start:, :picked_rows], end_low[start:, :picked_rows] = halves(
+                ends_ref[start:, :] + value[:, cols:]
+            )
+        else:
+            end_high[start:, :] = value[:, cols:]
 
     @pl.when(me_ref[0] == 0)
     def _():
         work(width)
-        end_high[:width, :picked_rows] = inv_high[:, first:]
-        end_low[:width, :picked_rows] = inv_low[:, first:]
+        if last:
+            out_ref[:width, :] = upper_ref[...]
+            end_high[:width, :picked_rows] = inv_high[:, first:]
+            end_low[:width, :picked_rows] = inv_low[:, first:]
 
     @pl.when(me_ref[0] != 0)
     def _():
         work(0)
+
+    if last:
+        end_high[:, picked_rows:] = land_ref[...]
+        end_low[:, picked_rows:] = jnp.zeros(land_ref.shape, BF16)
 
 
 def collect(places, me, arrays, row_high, row_low):
@@ -237,29 +254,6 @@
     depth = row_high.shape[0]
     high = high_ref[:, :depth]
     out_ref[...] = mm(low_ref[:, :depth], row_high[...]) + mm(high, row_low[...]) + mm(high, row_high[...])
-
-
-def update_kernel(me_ref, ids_ref, rows_ref, high_ref, low_ref, upper_ref, out_ref, up_high, up_low):
-    width = upper_ref.shape[0]
-    depth = width // ids_ref.shape[0]
-    for k in range(ids_ref.shape[0]):
-        source = pl.multiple_of(ids_ref[k] * depth, depth)
-        part = pl.ds(k * depth, depth)
-        up_high[part, :], up_low[part, :] = halves(upper_ref[pl.ds(source, depth), :])
-
-    def work(start):
-        high = high_ref[start:, :]
-        part = mm(low_ref[start:, :], up_high[...]) + mm(high, up_low[...]) + mm(high, up_high[...])
-        out_ref[start:, :] = rows_ref[start:, :] + part
-
-    @pl.when(me_ref[0] == 0)
-    def _():
-        work(width)
-        out_ref[:width, :] = upper_ref[...]
-
-    @pl.when(me_ref[0] != 0)
-    def _():
-        work(0)
 
 
 def finish_kernel(places, me_ref, part_ref, high_ref, low_ref, *refs):
@@ -337,6 +331,7 @@
     pivot = pltpu.with_memory_space_constraint(pivot, pltpu.HBM)
     panel_t = pltpu.with_memory_space_constraint(panel_t, pltpu.HBM)
     inverse_lower = pltpu.with_memory_space_constraint(inverse_lower, pltpu.HBM)
+    pieces = next(k for k in range(3, 0, -1) if rows % (16 * k) == 0 and width % (rows // k) == 0)
     *own, panel = pl.pallas_call(
         functools.partial(pick_kernel, row_count, order),
         out_shape=(item_shape,) * len(order) + (jax.ShapeDtypeStruct(panel_t.shape, F32),),
@@ -345,7 +340,7 @@
         scratch_shapes=[
             pltpu.VMEM((rows, cols), F32),
             pltpu.VMEM((1, width), jnp.int32),
-            pltpu.SemaphoreType.DMA((4,)),
+            pltpu.SemaphoreType.DMA((2 + pieces,)),
         ],
         compiler_params=PARAMS,
         name="pick",
@@ -418,26 +413,27 @@
         name="upper",
     )(here, inv_high, inv_low, *early_arrays)
 
-    pan_high, pan_low, end_high, end_low = pl.pallas_call(
-        turn_kernel,
-        out_shape=(jax.ShapeDtypeStruct((rows, width), BF16),) * 2
+    half = width // 2
+    share_scratch = [pltpu.VMEM((rows, half), BF16)] * 2 + [pltpu.VMEM((half, cols + late_rows), F32)] * 2
+    part, ends = pl.pallas_call(
+        functools.partial(share_kernel, 0, False),
+        out_shape=(jax.ShapeDtypeStruct((rows, cols), F32), jax.ShapeDtypeStruct((rows, late_rows), F32)),
+        in_specs=[SMEM, SMEM] + [VMEM] * 5,
+        out_specs=(VMEM, VMEM),
+        scratch_shapes=share_scratch,
+        compiler_params=PARAMS,
+        name="near",
+    )(here, ids, near, inv_high, inv_low, upper, base)
+    part, end_high, end_low = pl.pallas_call(
+        functools.partial(share_kernel, col_count // 2, True),
+        out_shape=(jax.ShapeDtypeStruct((rows, cols), F32),)
         + (jax.ShapeDtypeStruct((rows, late_rows + slot), BF16),) * 2,
-        in_specs=[SMEM, SMEM] + [VMEM] * 5,
-        out_specs=(VMEM,) * 4,
-        scratch_shapes=[pltpu.VMEM((width, late_rows), F32)] * 2,
-        compiler_params=PARAMS,
-        name="turn",
-    )(here, ids, near, far, inv_high, inv_low, land)
-
-    part = pl.pallas_call(
-        update_kernel,
-        out_shape=jax.ShapeDtypeStruct((rows, cols), F32),
-        in_specs=[SMEM, SMEM] + [VMEM] * 4,
-        out_specs=VMEM,
-        scratch_shapes=[pltpu.VMEM((width, cols), BF16)] * 2,
-        compiler_params=PARAMS,
-        name="update",
-    )(here, ids, base, pan_high, pan_low, upper)
+        in_specs=[SMEM, SMEM] + [VMEM] * 7,
+        out_specs=(VMEM,) * 3,
+        scratch_shapes=share_scratch,
+        compiler_params=PARAMS,
+        name="far",
+    )(here, ids, far, inv_high, inv_low, upper, part, ends, land)
 
     late_arrays, (late,) = used(late)
     steps = next(k for k in (3, 2, 1) if rows % (k * 16) == 0)

time: 35.7 us -> 35.5 us (level)
  the two profiles are of different devices: /device:TPU:23 before, /device:TPU:8 now
where the time goes in v7:
time: 35.5 us; the launch traced here: 35.2 us
  starting transfers between devices  17.1 us (48%)
  Pallas kernels  12.3 us (35%)
  waiting for transfers between devices  5.55 us (16%)
    ppermute x7, starting transfers between devices, local(): lax.ppermute(operand, 'row', [(s, t) for s, t, item in moves])  13.6 us
    ppermute x7, waiting for transfers between devices, local(): lax.ppermute(operand, 'row', [(s, t) for s, t, item in moves])  5.1 us
    ppermute x3, starting transfers between devices, gather_shards(): other = lax.ppermute(held, 'col', [(i, i ^ bit) for i in range(count)])  3.5 us
    pallas_call x1, Pallas kernels, local(): pl.pallas_call(functools.partial(prepare_kernel, row_count), out_shape=(j...  2.93 us
    pallas_call x1, Pallas kernels, local(): pl.pallas_call(functools.partial(finish_kernel, late), out_shape=jax.Shap...  2.3 us
    pallas_call x1, Pallas kernels, local(): pl.pallas_call(functools.partial(share_kernel, col_count // 2, True), out...  1.98 us
    pallas_call x1, Pallas kernels, local(): pl.pallas_call(functools.partial(share_kernel, 0, False), out_shape=(jax....  1.81 us
    pallas_call x1, Pallas kernels, local(): pl.pallas_call(functools.partial(pick_kernel, row_count, order), out_shap...  1.77 us
  transfers between devices with their start and end apart: 10, of which 4 were waited for; matrix products, arithmetic and copies ran while one was open for 0% of the time, Pallas kernels for 24%

profile of v7, /device:TPU:8, one launch (start us, length us, event | category | flops | bytes accessed | tf_op | source)
XLA Modules:
  0.0 35.2 jit_solution(6244065833307667168)
XLA Ops:
  0.0 1.8 %pick.1 = (f32[128,384]{1,0:T(8,128)S(1)}, f32[128,384]{1,0:T(8,128)S(1)}, f32[128,384]{1,0:T(8,128)S(1)}, f32[128,384]{1,0:T(8,128)S(1)}, f32[128,384]{1,0:T(8,128)S(1)}, /*index=5*/f32[64,768]{1,0:T(8,128)S(1)}) custom-call(s32[1]{0:T(128)} %bitcast.me_ref, s32[1,512]{1,0:T(1,128)} %bitcast.2, f32[768,384]{1,0:T(8,128)} %matrix_ref.3, f32[64,768]{1,0:T(8,128)} %panel_ref.1), custom_call_target="tpu_custom_call" | custom-call | tf_op jit(solution)/shard_map/pick/pallas_call | solution.py:335
  1.8 1.9 %collective-permute-start.1 = (f32[128,384]{1,0:T(8,128)S(1)}, f32[128,384]{1,0:T(8,128)S(1)}, u32[]{:S(2)}, u32[]{:S(2)}) collective-permute-start(f32[128,384]{1,0:T(8,128)S(1)} %get-tuple-element.21.refs_0_), channel_id=1, source_target_pairs={{0,16},{16,8},{8,0},{1,17},{17,9},{9,1},{2,18},{18,10},{10,2},{3,1... | collective-permute-start | bytes 589832 | tf_op jit(solution)/shard_map/ppermute | solution.py:367
  3.7 1.3 %collective-permute-start.4 = (f32[128,384]{1,0:T(8,128)S(1)}, f32[128,384]{1,0:T(8,128)S(1)}, u32[]{:S(2)}, u32[]{:S(2)}) collective-permute-start(f32[128,384]{1,0:T(8,128)S(1)} %get-tuple-element.27.refs_1_), channel_id=1, source_target_pairs={{0,16},{24,8},{16,24},{1,17},{25,9},{17,25},{2,18},{26,10},{18,26}... | collective-permute-start | bytes 589832 | tf_op jit(solution)/shard_map/ppermute | solution.py:367
  5.0 3.6 %collective-permute-start.5 = (f32[128,384]{1,0:T(8,128)S(1)}, f32[128,384]{1,0:T(8,128)S(1)}, u32[]{:S(2)}, u32[]{:S(2)}) collective-permute-start(f32[128,384]{1,0:T(8,128)S(1)} %get-tuple-element.28), channel_id=1, source_target_pairs={{24,16},{0,8},{8,24},{16,0},{25,17},{1,9},{9,25},{17,1},{26,18},{2... | collective-permute-start | bytes 589832 | tf_op jit(solution)/shard_map/ppermute | solution.py:367
  8.6 2.2 %collective-permute-start = (f32[64,768]{1,0:T(8,128)S(1)}, f32[64,768]{1,0:T(8,128)S(1)}, u32[]{:S(2)}, u32[]{:S(2)}) collective-permute-start(f32[64,768]{1,0:T(8,128)S(1)} %get-tuple-element.20.first), channel_id=1, source_target_pairs={{0,4},{1,5},{2,6},{3,7},{4,0},{5,1},{6,2},{7,3},{8,12},{9,13},{10,... | collective-permute-start | bytes 589832 | tf_op jit(solution)/shard_map/ppermute | solution.py:308
  10.8 2.9 %prepare.1 = (bf16[512,640]{1,0:T(8,128)(2,1)S(1)}, bf16[512,640]{1,0:T(8,128)(2,1)S(1)}, bf16[768,128]{1,0:T(8,128)(2,1)S(1)}, f32[768,384]{1,0:T(8,128)S(1)}) custom-call(s32[1]{0:T(128)} %bitcast.me_ref, s32[1,512]{1,0:T(1,128)} %bitcast.3, f32[512,512]{1,0:T(8,128)} %inverse_ref.1, f32[768,384]{1,0:T(8,128)} %matrix_ref.3), custom_call_target="tpu_custom_call" | custom-call | flops 1000000 | bytes 100000 | tf_op jit(solution)/shard_map/prepare/pallas_call | solution.py:376
  13.7 1.9 %collective-permute-done.1.refs_1_.refs_2_ = f32[128,384]{1,0:T(8,128)S(1)} collective-permute-done((f32[128,384]{1,0:T(8,128)S(1)}, f32[128,384]{1,0:T(8,128)S(1)}, u32[]{:S(2)}, u32[]{:S(2)}) %collective-permute-start.1) | collective-permute-done | bytes 196640 | tf_op jit(solution)/shard_map/ppermute | solution.py:367
  15.7 0.0 collective-permute-done.second
  15.7 0.5 %join.2.first = f32[128,768]{1,0:T(8,128)S(1)} custom-call(f32[64,768]{1,0:T(8,128)S(1)} %get-tuple-element.20.first, f32[64,768]{1,0:T(8,128)S(1)} %collective-permute-done.second, f32[128,384]{1,0:T(8,128)S(1)} %get-tuple-element.36.refs_0_, f32[128,384]{1,0:T(8,128)S(1)} %get-tuple-element.35.refs_1_, bf16[768,128]{1,0:T(8,128)(2,1)S(1)} %get-tuple-element.24.refs_2_.refs_1_), custom_call_target="tpu_custom_call" | custom-call | tf_op jit(solution)/shard_map/join/pallas_call | solution.py:291
  16.3 1.2 %collective-permute-start.2 = (f32[128,768]{1,0:T(8,128)S(1)}, f32[128,768]{1,0:T(8,128)S(1)}, u32[]{:S(2)}, u32[]{:S(2)}) collective-permute-start(f32[128,768]{1,0:T(8,128)S(1)} %join.2.first), channel_id=1, source_target_pairs={{0,2},{1,3},{2,0},{3,1},{4,6},{5,7},{6,4},{7,5},{8,10},{9,11},{10,... | collective-permute-start | bytes 1179656 | tf_op jit(solution)/shard_map/ppermute | solution.py:308
  17.5 0.7 %collective-permute-start.6 = (f32[128,384]{1,0:T(8,128)S(1)}, f32[128,384]{1,0:T(8,128)S(1)}, u32[]{:S(2)}, u32[]{:S(2)}) collective-permute-start(f32[128,384]{1,0:T(8,128)S(1)} %get-tuple-element.36.refs_0_), channel_id=1, source_target_pairs={{16,24},{0,16},{24,0},{17,25},{1,17},{25,1},{18,26},{2,18},{26,2},... | collective-permute-start | bytes 589832 | tf_op jit(solution)/shard_map/ppermute | solution.py:367
  18.2 4.1 %collective-permute-start.7 = (f32[128,384]{1,0:T(8,128)S(1)}, f32[128,384]{1,0:T(8,128)S(1)}, u32[]{:S(2)}, u32[]{:S(2)}) collective-permute-start(f32[128,384]{1,0:T(8,128)S(1)} %get-tuple-element.35.refs_1_), channel_id=1, source_target_pairs={{16,8},{0,24},{8,16},{17,9},{1,25},{9,17},{18,10},{2,26},{10,18},{... | collective-permute-start | bytes 589832 | tf_op jit(solution)/shard_map/ppermute | solution.py:367
  22.3 0.0 collective-permute-done.5.refs_3_.refs_4_
  22.4 0.7 %collective-permute-start.8 = (f32[128,384]{1,0:T(8,128)S(1)}, f32[128,384]{1,0:T(8,128)S(1)}, u32[]{:S(2)}, u32[]{:S(2)}) collective-permute-start(f32[128,384]{1,0:T(8,128)S(1)} %broadcast_select_fusion), channel_id=1, source_target_pairs={{16,24},{17,25},{18,26},{19,27},{20,28},{21,29},{22,30},{23,31}} | collective-permute-start | bytes 589832 | tf_op jit(solution)/shard_map/ppermute | solution.py:367
  23.1 1.3 %collective-permute-start.9 = (f32[128,384]{1,0:T(8,128)S(1)}, f32[128,384]{1,0:T(8,128)S(1)}, u32[]{:S(2)}, u32[]{:S(2)}) collective-permute-start(f32[128,384]{1,0:T(8,128)S(1)} %broadcast_select_fusion), channel_id=1, source_target_pairs={{16,8},{17,9},{18,10},{19,11},{20,12},{21,13},{22,14},{23,15}} | collective-permute-start | bytes 589832 | tf_op jit(solution)/shard_map/ppermute | solution.py:367
  24.4 0.4 %collective-permute-done.2.second = f32[128,768]{1,0:T(8,128)S(1)} collective-permute-done((f32[128,768]{1,0:T(8,128)S(1)}, f32[128,768]{1,0:T(8,128)S(1)}, u32[]{:S(2)}, u32[]{:S(2)}) %collective-permute-start.2) | collective-permute-done | bytes 393248 | tf_op jit(solution)/shard_map/ppermute | solution.py:308
  24.8 0.4 %join.3.shards_ref = f32[256,768]{1,0:T(8,128)S(1)} custom-call(f32[128,768]{1,0:T(8,128)S(1)} %join.2.first, f32[128,768]{1,0:T(8,128)S(1)} %collective-permute-done.2.second), custom_call_target="tpu_custom_call" | custom-call | tf_op jit(solution)/shard_map/join/pallas_call | solution.py:291
  25.2 0.1 collective-permute-start.3
  25.3 0.7 %upper.1.upper_ref = f32[512,384]{1,0:T(8,128)S(1)} custom-call(s32[1]{0:T(128)} %bitcast.me_ref, bf16[512,640]{1,0:T(8,128)(2,1)S(1)} %get-tuple-element.25.high_ref.inv_high, bf16[512,640]{1,0:T(8,128)(2,1)S(1)} %get-tuple-element.26.low_ref.inv_low, f32[128,384]{1,0:T(8,128)S(1)} %get-tuple-element.21.refs_0_, ...), custom_call_target="tpu_custom_call" | custom-call | flops 40000000000 | bytes 100000000 | tf_op jit(solution)/shard_map/upper/pallas_call | solution.py:405
  25.9 1.8 %near.1 = (f32[768,384]{1,0:T(8,128)S(1)}, f32[768,384]{1,0:T(8,128)S(1)}) custom-call(s32[1]{0:T(128)} %bitcast.me_ref, s32[8]{0:T(128)S(1)} %broadcast_xor_fusion.ids_ref, f32[256,768]{1,0:T(8,128)S(1)} %join.3.shards_ref, bf16[512,640]{1,0:T(8,128)(2,1)S(1)} %get-tuple-element.25.high_ref.inv_high, ...), custom_call_target="tpu_custom_call" | custom-call | tf_op jit(solution)/shard_map/near/pallas_call | solution.py:418
  27.8 2.0 %far.1 = (f32[768,384]{1,0:T(8,128)S(1)}, bf16[768,512]{1,0:T(8,128)(2,1)S(1)}, bf16[768,512]{1,0:T(8,128)(2,1)S(1)}) custom-call(s32[1]{0:T(128)} %bitcast.me_ref, s32[8]{0:T(128)S(1)} %broadcast_xor_fusion.ids_ref, f32[256,768]{1,0:T(8,128)S(1)} %collective-permute-done.3.shards_ref, bf16[512,640]{1,0:T(8,128)(2,1)S(1)} %get-tuple-element.25.high_ref.inv_high, ...), custom_call_target="tpu_custom_call" | custom-call | tf_op jit(solution)/shard_map/far/pallas_call | solution.py:427
  29.8 2.1 %collective-permute-done.7.refs_6_ = f32[128,384]{1,0:T(8,128)S(1)} collective-permute-done((f32[128,384]{1,0:T(8,128)S(1)}, f32[128,384]{1,0:T(8,128)S(1)}, u32[]{:S(2)}, u32[]{:S(2)}) %collective-permute-start.7) | collective-permute-done | bytes 196640 | tf_op jit(solution)/shard_map/ppermute | solution.py:367
  31.8 1.1 %collective-permute-done.9.refs_8_ = f32[128,384]{1,0:T(8,128)S(1)} collective-permute-done((f32[128,384]{1,0:T(8,128)S(1)}, f32[128,384]{1,0:T(8,128)S(1)}, u32[]{:S(2)}, u32[]{:S(2)}) %collective-permute-start.9) | collective-permute-done | bytes 196640 | tf_op jit(solution)/shard_map/ppermute | solution.py:367
  32.9 2.3 %finish.1 = f32[768,384]{1,0:T(8,128)} custom-call(s32[1]{0:T(128)} %bitcast.me_ref, f32[768,384]{1,0:T(8,128)S(1)} %get-tuple-element.32.part_ref, bf16[768,512]{1,0:T(8,128)(2,1)S(1)} %get-tuple-element.33.high_ref, bf16[768,512]{1,0:T(8,128)(2,1)S(1)} %get-tuple-element.34.low_ref, f32[128,384]{1,0:T(8,128)S(1)} %get-tuple-element.21.refs_0_, ...), custom_call_target="tpu_custom_call" | custom-call | tf_op jit(solution)/shard_map/finish/pallas_call | solution.py:440
  (9 shorter events, 0.1 us)
Async XLA Ops:
  1.8 13.9 %collective-permute-start.1 = (f32[128,384]{1,0:T(8,128)S(1)}, f32[128,384]{1,0:T(8,128)S(1)}, u32[]{:S(2)}, u32[]{:S(2)}) collective-permute-start(f32[128,384]{1,0:T(8,128)S(1)} %get-tuple-element.21.refs_0_), channel_id=1, source_target_pairs={{0,16},{16,8},{8,0},{1,17},{17,9},{9,1},{2,18},{18,10},{10,2},{3,1... | collective-permute-start | bytes 589832 | tf_op jit(solution)/shard_map/ppermute | solution.py:367
  3.7 18.6 %collective-permute-start.4 = (f32[128,384]{1,0:T(8,128)S(1)}, f32[128,384]{1,0:T(8,128)S(1)}, u32[]{:S(2)}, u32[]{:S(2)}) collective-permute-start(f32[128,384]{1,0:T(8,128)S(1)} %get-tuple-element.27.refs_1_), channel_id=1, source_target_pairs={{0,16},{24,8},{16,24},{1,17},{25,9},{17,25},{2,18},{26,10},{18,26}... | collective-permute-start | bytes 589832 | tf_op jit(solution)/shard_map/ppermute | solution.py:367
  5.0 17.3 %collective-permute-start.5 = (f32[128,384]{1,0:T(8,128)S(1)}, f32[128,384]{1,0:T(8,128)S(1)}, u32[]{:S(2)}, u32[]{:S(2)}) collective-permute-start(f32[128,384]{1,0:T(8,128)S(1)} %get-tuple-element.28), channel_id=1, source_target_pairs={{24,16},{0,8},{8,24},{16,0},{25,17},{1,9},{9,25},{17,1},{26,18},{2... | collective-permute-start | bytes 589832 | tf_op jit(solution)/shard_map/ppermute | solution.py:367
  8.6 7.1 %collective-permute-start = (f32[64,768]{1,0:T(8,128)S(1)}, f32[64,768]{1,0:T(8,128)S(1)}, u32[]{:S(2)}, u32[]{:S(2)}) collective-permute-start(f32[64,768]{1,0:T(8,128)S(1)} %get-tuple-element.20.first), channel_id=1, source_target_pairs={{0,4},{1,5},{2,6},{3,7},{4,0},{5,1},{6,2},{7,3},{8,12},{9,13},{10,... | collective-permute-start | bytes 589832 | tf_op jit(solution)/shard_map/ppermute | solution.py:308
  15.7 1.8 %copy-start = (s32[8]{0:T(128)S(1)}, s32[8]{0:T(128)}, u32[]{:S(2)}) copy-start(s32[8]{0:T(128)} %constant.12.clone) | copy-start | bytes 100
  16.3 8.5 %collective-permute-start.2 = (f32[128,768]{1,0:T(8,128)S(1)}, f32[128,768]{1,0:T(8,128)S(1)}, u32[]{:S(2)}, u32[]{:S(2)}) collective-permute-start(f32[128,768]{1,0:T(8,128)S(1)} %join.2.first), channel_id=1, source_target_pairs={{0,2},{1,3},{2,0},{3,1},{4,6},{5,7},{6,4},{7,5},{8,10},{9,11},{10,... | collective-permute-start | bytes 1179656 | tf_op jit(solution)/shard_map/ppermute | solution.py:308
  17.5 7.8 %collective-permute-start.6 = (f32[128,384]{1,0:T(8,128)S(1)}, f32[128,384]{1,0:T(8,128)S(1)}, u32[]{:S(2)}, u32[]{:S(2)}) collective-permute-start(f32[128,384]{1,0:T(8,128)S(1)} %get-tuple-element.36.refs_0_), channel_id=1, source_target_pairs={{16,24},{0,16},{24,0},{17,25},{1,17},{25,1},{18,26},{2,18},{26,2},... | collective-permute-start | bytes 589832 | tf_op jit(solution)/shard_map/ppermute | solution.py:367
  18.2 13.6 %collective-permute-start.7 = (f32[128,384]{1,0:T(8,128)S(1)}, f32[128,384]{1,0:T(8,128)S(1)}, u32[]{:S(2)}, u32[]{:S(2)}) collective-permute-start(f32[128,384]{1,0:T(8,128)S(1)} %get-tuple-element.35.refs_1_), channel_id=1, source_target_pairs={{16,8},{0,24},{8,16},{17,9},{1,25},{9,17},{18,10},{2,26},{10,18},{... | collective-permute-start | bytes 589832 | tf_op jit(solution)/shard_map/ppermute | solution.py:367
  22.4 9.4 %collective-permute-start.8 = (f32[128,384]{1,0:T(8,128)S(1)}, f32[128,384]{1,0:T(8,128)S(1)}, u32[]{:S(2)}, u32[]{:S(2)}) collective-permute-start(f32[128,384]{1,0:T(8,128)S(1)} %broadcast_select_fusion), channel_id=1, source_target_pairs={{16,24},{17,25},{18,26},{19,27},{20,28},{21,29},{22,30},{23,31}} | collective-permute-start | bytes 589832 | tf_op jit(solution)/shard_map/ppermute | solution.py:367
  23.1 9.8 %collective-permute-start.9 = (f32[128,384]{1,0:T(8,128)S(1)}, f32[128,384]{1,0:T(8,128)S(1)}, u32[]{:S(2)}, u32[]{:S(2)}) collective-permute-start(f32[128,384]{1,0:T(8,128)S(1)} %broadcast_select_fusion), channel_id=1, source_target_pairs={{16,8},{17,9},{18,10},{19,11},{20,12},{21,13},{22,14},{23,15}} | collective-permute-start | bytes 589832 | tf_op jit(solution)/shard_map/ppermute | solution.py:367
  25.2 2.6 %collective-permute-start.3 = (f32[256,768]{1,0:T(8,128)S(1)}, f32[256,768]{1,0:T(8,128)S(1)}, u32[]{:S(2)}, u32[]{:S(2)}) collective-permute-start(f32[256,768]{1,0:T(8,128)S(1)} %join.3.shards_ref), channel_id=1, source_target_pairs={{0,1},{1,0},{2,3},{3,2},{4,5},{5,4},{6,7},{7,6},{8,9},{9,8},{10,11... | collective-permute-start | bytes 2359304 | tf_op jit(solution)/shard_map/ppermute | solution.py:308

commit v8 on v7

--- a/solution.py
+++ b/solution.py
@@ -9,6 +9,7 @@
 
 F32 = jnp.float32
 BF16 = jnp.bfloat16
+STEPS = 3
 VMEM = pl.BlockSpec(memory_space=pltpu.VMEM)
 SMEM = pl.BlockSpec(memory_space=pltpu.SMEM)
 ANY = pl.BlockSpec(memory_space=pl.ANY)
@@ -184,53 +185,77 @@
     base_ref[...] = jnp.where(taken > 0.5, 0.0, rows_ref[...])
 
 
-def share_kernel(first_shard, last, me_ref, ids_ref, shards_ref, inv_high, inv_low, upper_ref, rows_ref, *refs):
-    if last:
-        ends_ref, land_ref = refs[:2]
-    out_ref, end_high, end_low = refs[2:5] if last else (*refs[:2], None)
-    high_ref, low_ref, side_high, side_low = refs[-4:]
+def turn(shards_ref, start, high_ref, low_ref):
+    high, low = halves(-shards_ref[:, start:])
+    high_ref[start:, :] = high.T
+    low_ref[start:, :] = low.T
+
+
+def near_kernel(me_ref, ids_ref, shards_ref, inv_high, inv_low, ends_ref, high_ref, low_ref, side_high, side_low):
+    half, rows = shards_ref.shape
+    width = inv_high.shape[0]
+    depth = width // ids_ref.shape[0]
+    first = inv_high.shape[1] - side_high.shape[1]
+    for k in range(half // depth):
+        source = pl.ds(pl.multiple_of(ids_ref[k] * depth, depth), depth)
+        part = pl.ds(k * depth, depth)
+        side_high[part, :] = inv_high[source, first:].astype(F32)
+        side_low[part, :] = inv_low[source, first:].astype(F32)
+
+    def work(start):
+        turn(shards_ref, start, high_ref, low_ref)
+        high, right = high_ref[start:, :], side_high[...].astype(BF16)
+        ends_ref[start:, :] = mm(low_ref[start:, :], right) + mm(high, side_low[...].astype(BF16)) + mm(high, right)
+
+    pl.when(me_ref[0] == 0)(lambda: work(width))
+    pl.when(me_ref[0] != 0)(lambda: work(0))
+
+
+def far_kernel(me_ref, ids_ref, shards_ref, inv_high, inv_low, upper_ref, rows_ref, ends_ref, land_ref, *refs):
+    near_high, near_low, out_ref, end_high, end_low, high_ref, low_ref = refs[:7]
+    side_high, side_low, up_high, up_low = refs[7:]
     half, rows = shards_ref.shape
     width, cols = upper_ref.shape
     depth = width // ids_ref.shape[0]
-    picked_rows = side_high.shape[1] - cols
-    first = inv_high.shape[1] - picked_rows
-    for k in range(half // depth):
-        source = pl.ds(pl.multiple_of(ids_ref[first_shard + k] * depth, depth), depth)
-        part = pl.ds(k * depth, depth)
+    first = inv_high.shape[1] - (side_high.shape[1] - cols)
+    stay, slot = width // 2, land_ref.shape[1]
+    for k in range(width // depth):
+        source = pl.ds(pl.multiple_of(ids_ref[k] * depth, depth), depth)
         high, low = halves(upper_ref[source, :])
-        side_high[part, :cols], side_low[part, :cols] = high.astype(F32), low.astype(F32)
-        side_high[part, cols:] = inv_high[source, first:].astype(F32)
-        side_low[part, cols:] = inv_low[source, first:].astype(F32)
+        part = pl.ds(k * depth % half, depth)
+        if k * depth < half:
+            up_high[part, :], up_low[part, :] = high.astype(F32), low.astype(F32)
+        else:
+            side_high[part, :cols], side_low[part, :cols] = high.astype(F32), low.astype(F32)
+            side_high[part, cols:] = inv_high[source, first:].astype(F32)
+            side_low[part, cols:] = inv_low[source, first:].astype(F32)
 
     def work(start):
-        high, low = halves(-shards_ref[:, start:])
-        high_ref[start:, :] = high.T
-        low_ref[start:, :] = low.T
-        pan_high, right = high_ref[start:, :], side_high[...].astype(BF16)
-        value = mm(low_ref[start:, :], right) + mm(pan_high, side_low[...].astype(BF16)) + mm(pan_high, right)
-        out_ref[start:, :] = rows_ref[start:, :] + value[:, :cols]
-        if last:
-            end_high[start:, :picked_rows], end_low[start:, :picked_rows] = halves(
-                ends_ref[start:, :] + value[:, cols:]
-            )
-        else:
-            end_high[start:, :] = value[:, cols:]
+        turn(shards_ref, start, high_ref, low_ref)
+        high, right = high_ref[start:, :], side_high[...].astype(BF16)
+        value = mm(low_ref[start:, :], right) + mm(high, side_low[...].astype(BF16)) + mm(high, right)
+        high, right = near_high[start:, :], up_high[...].astype(BF16)
+        near = mm(near_low[start:, :], right) + mm(high, up_low[...].astype(BF16)) + mm(high, right)
+        out_ref[start:, :] = rows_ref[start:, :] + (near + value[:, :cols])
+        high, low = halves(ends_ref[start:, :] + value[:, cols:])
+        put(end_high, start, high)
+        put(end_low, start, low)
+
+    def put(end, start, columns):
+        part = pl.ds(start, columns.shape[0])
+        end[part, :stay] = columns[:, :stay]
+        end[part, stay + slot :] = columns[:, stay:]
 
     @pl.when(me_ref[0] == 0)
     def _():
         work(width)
-        if last:
-            out_ref[:width, :] = upper_ref[...]
-            end_high[:width, :picked_rows] = inv_high[:, first:]
-            end_low[:width, :picked_rows] = inv_low[:, first:]
-
-    @pl.when(me_ref[0] != 0)
-    def _():
-        work(0)
-
-    if last:
-        end_high[:, picked_rows:] = land_ref[...]
-        end_low[:, picked_rows:] = jnp.zeros(land_ref.shape, BF16)
+        out_ref[:width, :] = upper_ref[...]
+        put(end_high, 0, inv_high[:, first:])
+        put(end_low, 0, inv_low[:, first:])
+
+    pl.when(me_ref[0] != 0)(lambda: work(0))
+    end_high[:, stay : stay + slot] = land_ref[...]
+    end_low[:, stay : stay + slot] = jnp.zeros(land_ref.shape, BF16)
 
 
 def collect(places, me, arrays, row_high, row_low):
@@ -256,21 +281,56 @@
     out_ref[...] = mm(low_ref[:, :depth], row_high[...]) + mm(high, row_low[...]) + mm(high, row_high[...])
 
 
+def share(places, me, part_ref, high_ref, low_ref, arrays, row_high, row_low, give):
+    slot, cols = arrays[0].shape
+    rows = part_ref.shape[0]
+    step = rows // STEPS if rows % (STEPS * 16) == 0 else rows
+    for r, table in enumerate(places):
+
+        @pl.when(me == r)
+        def _(table=table):
+            here = [block for block, k in enumerate(table) if k is not None]
+            span = pl.ds(here[0] * slot, (here[-1] + 1 - here[0]) * slot) if here else None
+            for block in range(here[0], here[-1] + 1) if here else ():
+                part = pl.ds(block * slot, slot)
+                if table[block] is None:
+                    row_high[part, :] = jnp.zeros((slot, cols), BF16)
+                    row_low[part, :] = jnp.zeros((slot, cols), BF16)
+                else:
+                    row_high[part, :], row_low[part, :] = halves(arrays[table[block]][...])
+            for k in range(rows // step):
+                part = pl.ds(k * step, step)
+                value = part_ref[part, :]
+                if here:
+                    high = high_ref[part, span]
+                    more = mm(low_ref[part, span], row_high[span, :]) + mm(high, row_low[span, :])
+                    value = value + (more + mm(high, row_high[span, :]))
+                give(k, part, value)
+
+
+def middle_kernel(places, me_ref, part_ref, high_ref, low_ref, *refs):
+    arrays, (out_ref, row_high, row_low) = refs[:-3], refs[-3:]
+
+    def give(k, part, value):
+        out_ref[part, :] = value
+
+    share(places, me_ref[0], part_ref, high_ref, low_ref, arrays, row_high, row_low, give)
+
+
 def finish_kernel(places, me_ref, part_ref, high_ref, low_ref, *refs):
     arrays, (out_ref, row_high, row_low, total, sem) = refs[:-5], refs[-5:]
-    collect(places, me_ref[0], arrays, row_high, row_low)
-    rows = part_ref.shape[0]
-    step = rows // sem.shape[0]
-    copies = []
+
+    def copy(k, part):
+        return pltpu.make_async_copy(total.at[part], out_ref.at[part], sem.at[k])
+
+    def give(k, part, value):
+        total[part, :] = value
+        copy(k, part).start()
+
+    share(places, me_ref[0], part_ref, high_ref, low_ref, arrays, row_high, row_low, give)
+    step = total.shape[0] // sem.shape[0]
     for k in range(sem.shape[0]):
-        part = pl.ds(k * step, step)
-        high = high_ref[part, :]
-        value = mm(low_ref[part, :], row_high[...]) + mm(high, row_low[...]) + mm(high, row_high[...])
-        total[part, :] = part_ref[part, :] + value
-        copies.append(pltpu.make_async_copy(total.at[part], out_ref.at[part], sem.at[k]))
-        copies[-1].start()
-    for copy in copies:
-        copy.wait()
+        copy(k, pl.ds(k * step, step)).wait()
 
 
 def join_kernel(first, second, *refs):
@@ -368,8 +428,14 @@
     received = arrays[len(own) :]
     blocks = [("pick", p) for p in range(chunks, row_count)]
     late_blocks = [("stay", c) for c in range(chunks)] + [("pick", p) for p in range(1, chunks)]
+    soon = len(own) + chunks + 2
     places = [[found[r][item] for item in blocks] for r in range(row_count)]
-    late = [[found[r].get(item) for item in late_blocks + [("moved", r)]] for r in range(row_count)]
+    late = [
+        [found[r].get(item) for item in late_blocks[:chunks] + [("moved", r)] + late_blocks[chunks:]]
+        for r in range(row_count)
+    ]
+    soon_late = [[k if k is not None and k < soon else None for k in table] for table in late]
+    late = [[k if k is not None and k >= soon else None for k in table] for table in late]
     late_rows = len(late_blocks) * slot
 
     picked_rows = len(blocks) * slot + late_rows
@@ -414,36 +480,48 @@
     )(here, inv_high, inv_low, *early_arrays)
 
     half = width // 2
-    share_scratch = [pltpu.VMEM((rows, half), BF16)] * 2 + [pltpu.VMEM((half, cols + late_rows), F32)] * 2
-    part, ends = pl.pallas_call(
-        functools.partial(share_kernel, 0, False),
-        out_shape=(jax.ShapeDtypeStruct((rows, cols), F32), jax.ShapeDtypeStruct((rows, late_rows), F32)),
-        in_specs=[SMEM, SMEM] + [VMEM] * 5,
-        out_specs=(VMEM, VMEM),
-        scratch_shapes=share_scratch,
+    ends, near_high, near_low = pl.pallas_call(
+        near_kernel,
+        out_shape=(jax.ShapeDtypeStruct((rows, late_rows), F32),) + (jax.ShapeDtypeStruct((rows, half), BF16),) * 2,
+        in_specs=[SMEM, SMEM] + [VMEM] * 3,
+        out_specs=(VMEM,) * 3,
+        scratch_shapes=[pltpu.VMEM((half, late_rows), F32)] * 2,
         compiler_params=PARAMS,
         name="near",
-    )(here, ids, near, inv_high, inv_low, upper, base)
+    )(here, ids, near, inv_high, inv_low)
     part, end_high, end_low = pl.pallas_call(
-        functools.partial(share_kernel, col_count // 2, True),
+        far_kernel,
         out_shape=(jax.ShapeDtypeStruct((rows, cols), F32),)
         + (jax.ShapeDtypeStruct((rows, late_rows + slot), BF16),) * 2,
-        in_specs=[SMEM, SMEM] + [VMEM] * 7,
+        in_specs=[SMEM, SMEM] + [VMEM] * 9,
         out_specs=(VMEM,) * 3,
-        scratch_shapes=share_scratch,
+        scratch_shapes=[pltpu.VMEM((rows, half), BF16)] * 2
+        + [pltpu.VMEM((half, cols + late_rows), F32)] * 2
+        + [pltpu.VMEM((half, cols), F32)] * 2,
         compiler_params=PARAMS,
         name="far",
-    )(here, ids, far, inv_high, inv_low, upper, part, ends, land)
+    )(here, ids, far, inv_high, inv_low, upper, base, ends, land, near_high, near_low)
+
+    row_scratch = [pltpu.VMEM((late_rows + slot, cols), BF16)] * 2
+    soon_arrays, (soon_late,) = used(soon_late)
+    part = pl.pallas_call(
+        functools.partial(middle_kernel, soon_late),
+        out_shape=jax.ShapeDtypeStruct((rows, cols), F32),
+        in_specs=[SMEM] + [VMEM] * (3 + len(soon_arrays)),
+        out_specs=VMEM,
+        scratch_shapes=row_scratch,
+        compiler_params=PARAMS,
+        name="middle",
+    )(here, part, end_high, end_low, *soon_arrays)
 
     late_arrays, (late,) = used(late)
-    steps = next(k for k in (3, 2, 1) if rows % (k * 16) == 0)
+    steps = STEPS if rows % (STEPS * 16) == 0 else 1
     return pl.pallas_call(
         functools.partial(finish_kernel, late),
         out_shape=jax.ShapeDtypeStruct((rows, cols), F32),
         in_specs=[SMEM] + [VMEM] * (3 + len(late_arrays)),
         out_specs=HBM,
-        scratch_shapes=[pltpu.VMEM((late_rows + slot, cols), BF16)] * 2
-        + [pltpu.VMEM((rows, cols), F32), pltpu.SemaphoreType.DMA((steps,))],
+        scratch_shapes=row_scratch + [pltpu.VMEM((rows, cols), F32), pltpu.SemaphoreType.DMA((steps,))],
         compiler_params=PARAMS,
         name="finish",
     )(here, part, end_high, end_low, *late_arrays)

time: 35.5 us -> 35 us (0.986)
  the two profiles are of different devices: /device:TPU:8 before, /device:TPU:23 now
where the time goes in v8:
time: 35 us; the launch traced here: 34.8 us
  starting transfers between devices  20.6 us (59%)
  Pallas kernels  13.4 us (38%)
  waiting for transfers between devices  0.44 us (1%)
    ppermute x7, starting transfers between devices, local(): lax.ppermute(operand, 'row', [(s, t) for s, t, item in moves])  18.9 us
    pallas_call x1, Pallas kernels, local(): pl.pallas_call(functools.partial(prepare_kernel, row_count), out_shape=(j...  2.92 us
    pallas_call x1, Pallas kernels, local(): pl.pallas_call(far_kernel, out_shape=(jax.ShapeDtypeStruct((rows, cols),...  2.63 us
    pallas_call x1, Pallas kernels, local(): pl.pallas_call(functools.partial(pick_kernel, row_count, order), out_shap...  1.77 us
    ppermute x3, starting transfers between devices, gather_shards(): other = lax.ppermute(held, 'col', [(i, i ^ bit) for i in range(count)])  1.65 us
    pallas_call x1, Pallas kernels, local(): pl.pallas_call(functools.partial(finish_kernel, late), out_shape=jax.Shap...  1.57 us
    pallas_call x1, Pallas kernels, local(): pl.pallas_call(functools.partial(middle_kernel, soon_late), out_shape=jax...  1.48 us
    pallas_call x1, Pallas kernels, local(): pl.pallas_call(near_kernel, out_shape=(jax.ShapeDtypeStruct((rows, late_r...  1.43 us
  transfers between devices with their start and end apart: 10, of which 1 were waited for; matrix products, arithmetic and copies ran while one was open for 0% of the time, Pallas kernels for 29%

profile of v8, /device:TPU:23, one launch (start us, length us, event | category | flops | bytes accessed | tf_op | source)
XLA Modules:
  0.0 34.8 jit_solution(13281607933074372807)
XLA Ops:
  0.0 1.8 %pick.1 = (f32[128,384]{1,0:T(8,128)S(1)}, f32[128,384]{1,0:T(8,128)S(1)}, f32[128,384]{1,0:T(8,128)S(1)}, f32[128,384]{1,0:T(8,128)S(1)}, f32[128,384]{1,0:T(8,128)S(1)}, /*index=5*/f32[64,768]{1,0:T(8,128)S(1)}) custom-call(s32[1]{0:T(128)} %bitcast.me_ref, s32[1,512]{1,0:T(1,128)} %bitcast.2, f32[768,384]{1,0:T(8,128)} %matrix_ref.3, f32[64,768]{1,0:T(8,128)} %panel_ref.1), custom_call_target="tpu_custom_call" | custom-call | tf_op jit(solution)/shard_map/pick/pallas_call | solution.py:395
  1.8 2.1 %collective-permute-start.1 = (f32[128,384]{1,0:T(8,128)S(1)}, f32[128,384]{1,0:T(8,128)S(1)}, u32[]{:S(2)}, u32[]{:S(2)}) collective-permute-start(f32[128,384]{1,0:T(8,128)S(1)} %get-tuple-element.22.refs_0_), channel_id=1, source_target_pairs={{0,16},{16,8},{8,0},{1,17},{17,9},{9,1},{2,18},{18,10},{10,2},{3,1... | collective-permute-start | bytes 589832 | tf_op jit(solution)/shard_map/ppermute | solution.py:427
  3.9 0.3 collective-permute-start
  4.2 1.9 %collective-permute-start.4 = (f32[128,384]{1,0:T(8,128)S(1)}, f32[128,384]{1,0:T(8,128)S(1)}, u32[]{:S(2)}, u32[]{:S(2)}) collective-permute-start(f32[128,384]{1,0:T(8,128)S(1)} %get-tuple-element.28.refs_1_), channel_id=1, source_target_pairs={{0,16},{24,8},{16,24},{1,17},{25,9},{17,25},{2,18},{26,10},{18,26}... | collective-permute-start | bytes 589832 | tf_op jit(solution)/shard_map/ppermute | solution.py:427
  6.1 2.4 %collective-permute-start.5 = (f32[128,384]{1,0:T(8,128)S(1)}, f32[128,384]{1,0:T(8,128)S(1)}, u32[]{:S(2)}, u32[]{:S(2)}) collective-permute-start(f32[128,384]{1,0:T(8,128)S(1)} %get-tuple-element.29), channel_id=1, source_target_pairs={{24,16},{0,8},{8,24},{16,0},{25,17},{1,9},{9,25},{17,1},{26,18},{2... | collective-permute-start | bytes 589832 | tf_op jit(solution)/shard_map/ppermute | solution.py:427
  8.5 2.9 %prepare.1 = (bf16[512,640]{1,0:T(8,128)(2,1)S(1)}, bf16[512,640]{1,0:T(8,128)(2,1)S(1)}, bf16[768,128]{1,0:T(8,128)(2,1)S(1)}, f32[768,384]{1,0:T(8,128)S(1)}) custom-call(s32[1]{0:T(128)} %bitcast.me_ref, s32[1,512]{1,0:T(1,128)} %bitcast.3, f32[512,512]{1,0:T(8,128)} %inverse_ref.1, f32[768,384]{1,0:T(8,128)} %matrix_ref.3), custom_call_target="tpu_custom_call" | custom-call | flops 1000000 | bytes 100000 | tf_op jit(solution)/shard_map/prepare/pallas_call | solution.py:442
  11.4 0.0 copy-start
  11.5 0.5 %join.2.first = f32[128,768]{1,0:T(8,128)S(1)} custom-call(f32[64,768]{1,0:T(8,128)S(1)} %get-tuple-element.21.first, f32[64,768]{1,0:T(8,128)S(1)} %collective-permute-done.second, f32[128,384]{1,0:T(8,128)S(1)} %get-tuple-element.38.refs_0_, f32[128,384]{1,0:T(8,128)S(1)} %get-tuple-element.37.refs_1_, bf16[768,128]{1,0:T(8,128)(2,1)S(1)} %get-tuple-element.25.refs_2_.land_ref), custom_call_target="tpu_custom_call" | custom-call | tf_op jit(solution)/shard_map/join/pallas_call | solution.py:351
  12.0 0.3 collective-permute-start.2
  12.4 1.9 %collective-permute-start.6 = (f32[128,384]{1,0:T(8,128)S(1)}, f32[128,384]{1,0:T(8,128)S(1)}, u32[]{:S(2)}, u32[]{:S(2)}) collective-permute-start(f32[128,384]{1,0:T(8,128)S(1)} %get-tuple-element.38.refs_0_), channel_id=1, source_target_pairs={{16,24},{0,16},{24,0},{17,25},{1,17},{25,1},{18,26},{2,18},{26,2},... | collective-permute-start | bytes 589832 | tf_op jit(solution)/shard_map/ppermute | solution.py:427
  14.3 1.9 %collective-permute-start.7 = (f32[128,384]{1,0:T(8,128)S(1)}, f32[128,384]{1,0:T(8,128)S(1)}, u32[]{:S(2)}, u32[]{:S(2)}) collective-permute-start(f32[128,384]{1,0:T(8,128)S(1)} %get-tuple-element.37.refs_1_), channel_id=1, source_target_pairs={{16,8},{0,24},{8,16},{17,9},{1,25},{9,17},{18,10},{2,26},{10,18},{... | collective-permute-start | bytes 589832 | tf_op jit(solution)/shard_map/ppermute | solution.py:427
  16.2 0.0 collective-permute-done.4.refs_2_.refs_3_
  16.2 0.4 %collective-permute-done.5.refs_3_.refs_4_ = f32[128,384]{1,0:T(8,128)S(1)} collective-permute-done((f32[128,384]{1,0:T(8,128)S(1)}, f32[128,384]{1,0:T(8,128)S(1)}, u32[]{:S(2)}, u32[]{:S(2)}) %collective-permute-start.5) | collective-permute-done | bytes 196640 | tf_op jit(solution)/shard_map/ppermute | solution.py:427
  16.7 7.4 %collective-permute-start.8 = (f32[128,384]{1,0:T(8,128)S(1)}, f32[128,384]{1,0:T(8,128)S(1)}, u32[]{:S(2)}, u32[]{:S(2)}) collective-permute-start(f32[128,384]{1,0:T(8,128)S(1)} %broadcast_select_fusion), channel_id=1, source_target_pairs={{16,24},{17,25},{18,26},{19,27},{20,28},{21,29},{22,30},{23,31}} | collective-permute-start | bytes 589832 | tf_op jit(solution)/shard_map/ppermute | solution.py:427
  24.1 1.3 %collective-permute-start.9 = (f32[128,384]{1,0:T(8,128)S(1)}, f32[128,384]{1,0:T(8,128)S(1)}, u32[]{:S(2)}, u32[]{:S(2)}) collective-permute-start(f32[128,384]{1,0:T(8,128)S(1)} %broadcast_select_fusion), channel_id=1, source_target_pairs={{16,8},{17,9},{18,10},{19,11},{20,12},{21,13},{22,14},{23,15}} | collective-permute-start | bytes 589832 | tf_op jit(solution)/shard_map/ppermute | solution.py:427
  25.4 0.0 collective-permute-done.2.second
  25.4 0.4 %join.3.shards_ref = f32[256,768]{1,0:T(8,128)S(1)} custom-call(f32[128,768]{1,0:T(8,128)S(1)} %join.2.first, f32[128,768]{1,0:T(8,128)S(1)} %collective-permute-done.2.second), custom_call_target="tpu_custom_call" | custom-call | tf_op jit(solution)/shard_map/join/pallas_call | solution.py:351
  25.8 1.0 %collective-permute-start.3 = (f32[256,768]{1,0:T(8,128)S(1)}, f32[256,768]{1,0:T(8,128)S(1)}, u32[]{:S(2)}, u32[]{:S(2)}) collective-permute-start(f32[256,768]{1,0:T(8,128)S(1)} %join.3.shards_ref), channel_id=1, source_target_pairs={{0,1},{1,0},{2,3},{3,2},{4,5},{5,4},{6,7},{7,6},{8,9},{9,8},{10,11... | collective-permute-start | bytes 2359304 | tf_op jit(solution)/shard_map/ppermute | solution.py:368
  26.8 0.6 %upper.1.upper_ref = f32[512,384]{1,0:T(8,128)S(1)} custom-call(s32[1]{0:T(128)} %bitcast.me_ref, bf16[512,640]{1,0:T(8,128)(2,1)S(1)} %get-tuple-element.26.high_ref.inv_high, bf16[512,640]{1,0:T(8,128)(2,1)S(1)} %get-tuple-element.27.low_ref.inv_low, f32[128,384]{1,0:T(8,128)S(1)} %get-tuple-element.22.refs_0_, ...), custom_call_target="tpu_custom_call" | custom-call | flops 40000000000 | bytes 100000000 | tf_op jit(solution)/shard_map/upper/pallas_call | solution.py:471
  27.5 1.4 %near.1 = (f32[768,384]{1,0:T(8,128)S(1)}, bf16[768,256]{1,0:T(8,128)(2,1)S(1)}, bf16[768,256]{1,0:T(8,128)(2,1)S(1)}) custom-call(s32[1]{0:T(128)} %bitcast.me_ref, s32[8]{0:T(128)S(1)} %broadcast_xor_fusion.ids_ref, f32[256,768]{1,0:T(8,128)S(1)} %join.3.shards_ref, bf16[512,640]{1,0:T(8,128)(2,1)S(1)} %get-tuple-element.26.high_ref.inv_high, ...), custom_call_target="tpu_custom_call" | custom-call | tf_op jit(solution)/shard_map/near/pallas_call | solution.py:483
  28.9 0.0 collective-permute-done.3.shards_ref
  28.9 2.6 %far.1 = (f32[768,384]{1,0:T(8,128)S(1)}, bf16[768,512]{1,0:T(8,128)(2,1)S(1)}, bf16[768,512]{1,0:T(8,128)(2,1)S(1)}) custom-call(s32[1]{0:T(128)} %bitcast.me_ref, s32[8]{0:T(128)S(1)} %broadcast_xor_fusion.ids_ref, f32[256,768]{1,0:T(8,128)S(1)} %collective-permute-done.3.shards_ref, bf16[512,640]{1,0:T(8,128)(2,1)S(1)} %get-tuple-element.26.high_ref.inv_high, ...), custom_call_target="tpu_custom_call" | custom-call | tf_op jit(solution)/shard_map/far/pallas_call | solution.py:492
  31.5 1.5 %middle.1.part_ref = f32[768,384]{1,0:T(8,128)S(1)} custom-call(s32[1]{0:T(128)} %bitcast.me_ref, f32[768,384]{1,0:T(8,128)S(1)} %get-tuple-element.34.part_ref, bf16[768,512]{1,0:T(8,128)(2,1)S(1)} %get-tuple-element.35.high_ref, bf16[768,512]{1,0:T(8,128)(2,1)S(1)} %get-tuple-element.36.low_ref, f32[128,384]{1,0:T(8,128)S(1)} %get-tuple-element.22.refs_0_, ...), custom_call_target="tpu_custom_call" | custom-call | tf_op jit(solution)/shard_map/middle/pallas_call | solution.py:507
  33.1 1.6 %finish.1 = f32[768,384]{1,0:T(8,128)} custom-call(s32[1]{0:T(128)} %bitcast.me_ref, f32[768,384]{1,0:T(8,128)S(1)} %middle.1.part_ref, bf16[768,512]{1,0:T(8,128)(2,1)S(1)} %get-tuple-element.35.high_ref, bf16[768,512]{1,0:T(8,128)(2,1)S(1)} %get-tuple-element.36.low_ref, f32[128,384]{1,0:T(8,128)S(1)} %collective-permute-done.7.refs_0_, ...), custom_call_target="tpu_custom_call" | custom-call | tf_op jit(solution)/shard_map/finish/pallas_call | solution.py:519
  (10 shorter events, 0.1 us)
Async XLA Ops:
  1.8 9.6 %collective-permute-start.1 = (f32[128,384]{1,0:T(8,128)S(1)}, f32[128,384]{1,0:T(8,128)S(1)}, u32[]{:S(2)}, u32[]{:S(2)}) collective-permute-start(f32[128,384]{1,0:T(8,128)S(1)} %get-tuple-element.22.refs_0_), channel_id=1, source_target_pairs={{0,16},{16,8},{8,0},{1,17},{17,9},{9,1},{2,18},{18,10},{10,2},{3,1... | collective-permute-start | bytes 589832 | tf_op jit(solution)/shard_map/ppermute | solution.py:427
  3.9 7.6 %collective-permute-start = (f32[64,768]{1,0:T(8,128)S(1)}, f32[64,768]{1,0:T(8,128)S(1)}, u32[]{:S(2)}, u32[]{:S(2)}) collective-permute-start(f32[64,768]{1,0:T(8,128)S(1)} %get-tuple-element.21.first), channel_id=1, source_target_pairs={{0,4},{1,5},{2,6},{3,7},{4,0},{5,1},{6,2},{7,3},{8,12},{9,13},{10,... | collective-permute-start | bytes 589832 | tf_op jit(solution)/shard_map/ppermute | solution.py:368
  4.2 12.0 %collective-permute-start.4 = (f32[128,384]{1,0:T(8,128)S(1)}, f32[128,384]{1,0:T(8,128)S(1)}, u32[]{:S(2)}, u32[]{:S(2)}) collective-permute-start(f32[128,384]{1,0:T(8,128)S(1)} %get-tuple-element.28.refs_1_), channel_id=1, source_target_pairs={{0,16},{24,8},{16,24},{1,17},{25,9},{17,25},{2,18},{26,10},{18,26}... | collective-permute-start | bytes 589832 | tf_op jit(solution)/shard_map/ppermute | solution.py:427
  6.1 10.6 %collective-permute-start.5 = (f32[128,384]{1,0:T(8,128)S(1)}, f32[128,384]{1,0:T(8,128)S(1)}, u32[]{:S(2)}, u32[]{:S(2)}) collective-permute-start(f32[128,384]{1,0:T(8,128)S(1)} %get-tuple-element.29), channel_id=1, source_target_pairs={{24,16},{0,8},{8,24},{16,0},{25,17},{1,9},{9,25},{17,1},{26,18},{2... | collective-permute-start | bytes 589832 | tf_op jit(solution)/shard_map/ppermute | solution.py:427
  11.4 0.9 %copy-start = (s32[8]{0:T(128)S(1)}, s32[8]{0:T(128)}, u32[]{:S(2)}) copy-start(s32[8]{0:T(128)} %constant.12.clone) | copy-start | bytes 100
  12.0 13.3 %collective-permute-start.2 = (f32[128,768]{1,0:T(8,128)S(1)}, f32[128,768]{1,0:T(8,128)S(1)}, u32[]{:S(2)}, u32[]{:S(2)}) collective-permute-start(f32[128,768]{1,0:T(8,128)S(1)} %join.2.first), channel_id=1, source_target_pairs={{0,2},{1,3},{2,0},{3,1},{4,6},{5,7},{6,4},{7,5},{8,10},{9,11},{10,... | collective-permute-start | bytes 1179656 | tf_op jit(solution)/shard_map/ppermute | solution.py:368
  12.4 14.5 %collective-permute-start.6 = (f32[128,384]{1,0:T(8,128)S(1)}, f32[128,384]{1,0:T(8,128)S(1)}, u32[]{:S(2)}, u32[]{:S(2)}) collective-permute-start(f32[128,384]{1,0:T(8,128)S(1)} %get-tuple-element.38.refs_0_), channel_id=1, source_target_pairs={{16,24},{0,16},{24,0},{17,25},{1,17},{25,1},{18,26},{2,18},{26,2},... | collective-permute-start | bytes 589832 | tf_op jit(solution)/shard_map/ppermute | solution.py:427
  14.3 18.8 %collective-permute-start.7 = (f32[128,384]{1,0:T(8,128)S(1)}, f32[128,384]{1,0:T(8,128)S(1)}, u32[]{:S(2)}, u32[]{:S(2)}) collective-permute-start(f32[128,384]{1,0:T(8,128)S(1)} %get-tuple-element.37.refs_1_), channel_id=1, source_target_pairs={{16,8},{0,24},{8,16},{17,9},{1,25},{9,17},{18,10},{2,26},{10,18},{... | collective-permute-start | bytes 589832 | tf_op jit(solution)/shard_map/ppermute | solution.py:427
  16.7 16.4 %collective-permute-start.8 = (f32[128,384]{1,0:T(8,128)S(1)}, f32[128,384]{1,0:T(8,128)S(1)}, u32[]{:S(2)}, u32[]{:S(2)}) collective-permute-start(f32[128,384]{1,0:T(8,128)S(1)} %broadcast_select_fusion), channel_id=1, source_target_pairs={{16,24},{17,25},{18,26},{19,27},{20,28},{21,29},{22,30},{23,31}} | collective-permute-start | bytes 589832 | tf_op jit(solution)/shard_map/ppermute | solution.py:427
  24.1 9.0 %collective-permute-start.9 = (f32[128,384]{1,0:T(8,128)S(1)}, f32[128,384]{1,0:T(8,128)S(1)}, u32[]{:S(2)}, u32[]{:S(2)}) collective-permute-start(f32[128,384]{1,0:T(8,128)S(1)} %broadcast_select_fusion), channel_id=1, source_target_pairs={{16,8},{17,9},{18,10},{19,11},{20,12},{21,13},{22,14},{23,15}} | collective-permute-start | bytes 589832 | tf_op jit(solution)/shard_map/ppermute | solution.py:427
  25.8 3.1 %collective-permute-start.3 = (f32[256,768]{1,0:T(8,128)S(1)}, f32[256,768]{1,0:T(8,128)S(1)}, u32[]{:S(2)}, u32[]{:S(2)}) collective-permute-start(f32[256,768]{1,0:T(8,128)S(1)} %join.3.shards_ref), channel_id=1, source_target_pairs={{0,1},{1,0},{2,3},{3,2},{4,5},{5,4},{6,7},{7,6},{8,9},{9,8},{10,11... | collective-permute-start | bytes 2359304 | tf_op jit(solution)/shard_map/ppermute | solution.py:368

commit v9 on v8

--- a/solution.py
+++ b/solution.py
@@ -274,7 +274,7 @@
 
 
 def upper_kernel(places, me_ref, high_ref, low_ref, *refs):
-    arrays, (out_ref, row_high, row_low) = refs[:-3], refs[-3:]
+    arrays, (out_ref, row_high, row_low) = refs[:-4], refs[-3:]
     collect(places, me_ref[0], arrays, row_high, row_low)
     depth = row_high.shape[0]
     high = high_ref[:, :depth]
@@ -416,7 +416,7 @@
     for moves in rounds:
         leaving = [item for s, t, item in moves if s == 0]
         operand = own[order.index(leaving[0])] if leaving else own[0]
-        if len(operands) > chunks + 1 and all(item[0] == "stay" for s, t, item in moves):
+        if len(operands) > chunks + 3 and all(item[0] == "stay" for s, t, item in moves):
             operand = arrays[len(own) + chunks]
         for s, t, item in moves:
             if s != 0 and item[0] == "stay":
@@ -467,18 +467,6 @@
         names = sorted({k for table in tables for k in jax.tree.leaves(table)})
         return [arrays[k] for k in names], [jax.tree.map(names.index, table) for table in tables]
 
-    early_arrays, (places,) = used(places)
-    upper = pl.pallas_call(
-        functools.partial(upper_kernel, places),
-        out_shape=jax.ShapeDtypeStruct((width, cols), F32),
-        in_specs=[SMEM] + [VMEM] * (2 + len(early_arrays)),
-        out_specs=VMEM,
-        scratch_shapes=[pltpu.VMEM((picked_rows - late_rows, cols), BF16)] * 2,
-        compiler_params=PARAMS,
-        cost_estimate=LONG,
-        name="upper",
-    )(here, inv_high, inv_low, *early_arrays)
-
     half = width // 2
     ends, near_high, near_low = pl.pallas_call(
         near_kernel,
@@ -489,6 +477,18 @@
         compiler_params=PARAMS,
         name="near",
     )(here, ids, near, inv_high, inv_low)
+    early_arrays, (places,) = used(places)
+    upper = pl.pallas_call(
+        functools.partial(upper_kernel, places),
+        out_shape=jax.ShapeDtypeStruct((width, cols), F32),
+        in_specs=[SMEM] + [VMEM] * (2 + len(early_arrays)) + [ANY],
+        out_specs=VMEM,
+        scratch_shapes=[pltpu.VMEM((picked_rows - late_rows, cols), BF16)] * 2,
+        compiler_params=PARAMS,
+        cost_estimate=LONG,
+        name="upper",
+    )(here, inv_high, inv_low, *early_arrays, ends)
+
     part, end_high, end_low = pl.pallas_call(
         far_kernel,
         out_shape=(jax.ShapeDtypeStruct((rows, cols), F32),)

time: 35 us -> 35.1 us (level)
  no operation moved by 1% of the time
where the time goes in v9:
time: 35.1 us; the launch traced here: 34.8 us
  starting transfers between devices  20.6 us (59%)
  Pallas kernels  13.4 us (38%)
  waiting for transfers between devices  0.44 us (1%)
  between operations  0.36 us (1%)
    ppermute x7, starting transfers between devices, local(): lax.ppermute(operand, 'row', [(s, t) for s, t, item in moves])  18.9 us
    pallas_call x1, Pallas kernels, local(): pl.pallas_call(functools.partial(prepare_kernel, row_count), out_shape=(j...  2.92 us
    pallas_call x1, Pallas kernels, local(): pl.pallas_call(far_kernel, out_shape=(jax.ShapeDtypeStruct((rows, cols),...  2.62 us
    pallas_call x1, Pallas kernels, local(): pl.pallas_call(functools.partial(pick_kernel, row_count, order), out_shap...  1.77 us
    ppermute x3, starting transfers between devices, gather_shards(): other = lax.ppermute(held, 'col', [(i, i ^ bit) for i in range(count)])  1.65 us
    pallas_call x1, Pallas kernels, local(): pl.pallas_call(functools.partial(finish_kernel, late), out_shape=jax.Shap...  1.57 us
    pallas_call x1, Pallas kernels, local(): pl.pallas_call(functools.partial(middle_kernel, soon_late), out_shape=jax...  1.49 us
    pallas_call x1, Pallas kernels, local(): pl.pallas_call(near_kernel, out_shape=(jax.ShapeDtypeStruct((rows, late_r...  1.43 us
  transfers between devices with their start and end apart: 10, of which 1 were waited for; matrix products, arithmetic and copies ran while one was open for 0% of the time, Pallas kernels for 29%

profile of v9, /device:TPU:23, one launch (start us, length us, event | category | flops | bytes accessed | tf_op | source)
XLA Modules:
  0.0 34.8 jit_solution(7554968769315540195)
XLA Ops:
  0.0 1.8 %pick.1 = (f32[128,384]{1,0:T(8,128)S(1)}, f32[128,384]{1,0:T(8,128)S(1)}, f32[128,384]{1,0:T(8,128)S(1)}, f32[128,384]{1,0:T(8,128)S(1)}, f32[128,384]{1,0:T(8,128)S(1)}, /*index=5*/f32[64,768]{1,0:T(8,128)S(1)}) custom-call(s32[1]{0:T(128)} %bitcast.me_ref, s32[1,512]{1,0:T(1,128)} %bitcast.2, f32[768,384]{1,0:T(8,128)} %matrix_ref.3, f32[64,768]{1,0:T(8,128)} %panel_ref.1), custom_call_target="tpu_custom_call" | custom-call | tf_op jit(solution)/shard_map/pick/pallas_call | solution.py:395
  1.8 2.1 %collective-permute-start.1 = (f32[128,384]{1,0:T(8,128)S(1)}, f32[128,384]{1,0:T(8,128)S(1)}, u32[]{:S(2)}, u32[]{:S(2)}) collective-permute-start(f32[128,384]{1,0:T(8,128)S(1)} %get-tuple-element.22.refs_0_), channel_id=1, source_target_pairs={{0,16},{16,8},{8,0},{1,17},{17,9},{9,1},{2,18},{18,10},{10,2},{3,1... | collective-permute-start | bytes 589832 | tf_op jit(solution)/shard_map/ppermute | solution.py:427
  3.9 0.3 collective-permute-start
  4.2 1.9 %collective-permute-start.4 = (f32[128,384]{1,0:T(8,128)S(1)}, f32[128,384]{1,0:T(8,128)S(1)}, u32[]{:S(2)}, u32[]{:S(2)}) collective-permute-start(f32[128,384]{1,0:T(8,128)S(1)} %get-tuple-element.28.refs_1_), channel_id=1, source_target_pairs={{0,16},{24,8},{16,24},{1,17},{25,9},{17,25},{2,18},{26,10},{18,26}... | collective-permute-start | bytes 589832 | tf_op jit(solution)/shard_map/ppermute | solution.py:427
  6.1 2.4 %collective-permute-start.5 = (f32[128,384]{1,0:T(8,128)S(1)}, f32[128,384]{1,0:T(8,128)S(1)}, u32[]{:S(2)}, u32[]{:S(2)}) collective-permute-start(f32[128,384]{1,0:T(8,128)S(1)} %get-tuple-element.29), channel_id=1, source_target_pairs={{24,16},{0,8},{8,24},{16,0},{25,17},{1,9},{9,25},{17,1},{26,18},{2... | collective-permute-start | bytes 589832 | tf_op jit(solution)/shard_map/ppermute | solution.py:427
  8.5 2.9 %prepare.1 = (bf16[512,640]{1,0:T(8,128)(2,1)S(1)}, bf16[512,640]{1,0:T(8,128)(2,1)S(1)}, bf16[768,128]{1,0:T(8,128)(2,1)S(1)}, f32[768,384]{1,0:T(8,128)S(1)}) custom-call(s32[1]{0:T(128)} %bitcast.me_ref, s32[1,512]{1,0:T(1,128)} %bitcast.3, f32[512,512]{1,0:T(8,128)} %inverse_ref.1, f32[768,384]{1,0:T(8,128)} %matrix_ref.3), custom_call_target="tpu_custom_call" | custom-call | flops 1000000 | bytes 100000 | tf_op jit(solution)/shard_map/prepare/pallas_call | solution.py:442
  11.4 0.0 collective-permute-done.1.refs_1_.refs_2_
  11.4 0.0 copy-start
  11.5 0.0 collective-permute-done.second
  11.5 0.5 %join.2.first = f32[128,768]{1,0:T(8,128)S(1)} custom-call(f32[64,768]{1,0:T(8,128)S(1)} %get-tuple-element.21.first, f32[64,768]{1,0:T(8,128)S(1)} %collective-permute-done.second, f32[128,384]{1,0:T(8,128)S(1)} %get-tuple-element.40.refs_0_, f32[128,384]{1,0:T(8,128)S(1)} %get-tuple-element.39.refs_1_, bf16[768,128]{1,0:T(8,128)(2,1)S(1)} %get-tuple-element.25.refs_2_.land_ref), custom_call_target="tpu_custom_call" | custom-call | tf_op jit(solution)/shard_map/join/pallas_call | solution.py:351
  12.0 0.3 collective-permute-start.2
  12.4 1.9 %collective-permute-start.6 = (f32[128,384]{1,0:T(8,128)S(1)}, f32[128,384]{1,0:T(8,128)S(1)}, u32[]{:S(2)}, u32[]{:S(2)}) collective-permute-start(f32[128,384]{1,0:T(8,128)S(1)} %get-tuple-element.40.refs_0_), channel_id=1, source_target_pairs={{16,24},{0,16},{24,0},{17,25},{1,17},{25,1},{18,26},{2,18},{26,2},... | collective-permute-start | bytes 589832 | tf_op jit(solution)/shard_map/ppermute | solution.py:427
  14.3 1.9 %collective-permute-start.7 = (f32[128,384]{1,0:T(8,128)S(1)}, f32[128,384]{1,0:T(8,128)S(1)}, u32[]{:S(2)}, u32[]{:S(2)}) collective-permute-start(f32[128,384]{1,0:T(8,128)S(1)} %get-tuple-element.39.refs_1_), channel_id=1, source_target_pairs={{16,8},{0,24},{8,16},{17,9},{1,25},{9,17},{18,10},{2,26},{10,18},{... | collective-permute-start | bytes 589832 | tf_op jit(solution)/shard_map/ppermute | solution.py:427
  16.2 0.4 %collective-permute-done.5.refs_3_.refs_4_ = f32[128,384]{1,0:T(8,128)S(1)} collective-permute-done((f32[128,384]{1,0:T(8,128)S(1)}, f32[128,384]{1,0:T(8,128)S(1)}, u32[]{:S(2)}, u32[]{:S(2)}) %collective-permute-start.5) | collective-permute-done | bytes 196640 | tf_op jit(solution)/shard_map/ppermute | solution.py:427
  16.7 7.4 %collective-permute-start.8 = (f32[128,384]{1,0:T(8,128)S(1)}, f32[128,384]{1,0:T(8,128)S(1)}, u32[]{:S(2)}, u32[]{:S(2)}) collective-permute-start(f32[128,384]{1,0:T(8,128)S(1)} %get-tuple-element.38), channel_id=1, source_target_pairs={{16,24},{17,25},{18,26},{19,27},{20,28},{21,29},{22,30},{23,31}} | collective-permute-start | bytes 589832 | tf_op jit(solution)/shard_map/ppermute | solution.py:427
  24.1 1.3 %collective-permute-start.9 = (f32[128,384]{1,0:T(8,128)S(1)}, f32[128,384]{1,0:T(8,128)S(1)}, u32[]{:S(2)}, u32[]{:S(2)}) collective-permute-start(f32[128,384]{1,0:T(8,128)S(1)} %get-tuple-element.37), channel_id=1, source_target_pairs={{16,8},{17,9},{18,10},{19,11},{20,12},{21,13},{22,14},{23,15}} | collective-permute-start | bytes 589832 | tf_op jit(solution)/shard_map/ppermute | solution.py:427
  25.4 0.4 %join.3.shards_ref = f32[256,768]{1,0:T(8,128)S(1)} custom-call(f32[128,768]{1,0:T(8,128)S(1)} %join.2.first, f32[128,768]{1,0:T(8,128)S(1)} %collective-permute-done.2.second), custom_call_target="tpu_custom_call" | custom-call | tf_op jit(solution)/shard_map/join/pallas_call | solution.py:351
  25.8 1.0 %collective-permute-start.3 = (f32[256,768]{1,0:T(8,128)S(1)}, f32[256,768]{1,0:T(8,128)S(1)}, u32[]{:S(2)}, u32[]{:S(2)}) collective-permute-start(f32[256,768]{1,0:T(8,128)S(1)} %join.3.shards_ref), channel_id=1, source_target_pairs={{0,1},{1,0},{2,3},{3,2},{4,5},{5,4},{6,7},{7,6},{8,9},{9,8},{10,11... | collective-permute-start | bytes 2359304 | tf_op jit(solution)/shard_map/ppermute | solution.py:368
  26.8 1.4 %near.1 = (f32[768,384]{1,0:T(8,128)S(1)}, bf16[768,256]{1,0:T(8,128)(2,1)S(1)}, bf16[768,256]{1,0:T(8,128)(2,1)S(1)}) custom-call(s32[1]{0:T(128)} %bitcast.me_ref, s32[8]{0:T(128)S(1)} %broadcast_xor_fusion.ids_ref, f32[256,768]{1,0:T(8,128)S(1)} %join.3.shards_ref, bf16[512,640]{1,0:T(8,128)(2,1)S(1)} %get-tuple-element.26.inv_high.high_ref, ...), custom_call_target="tpu_custom_call" | custom-call | tf_op jit(solution)/shard_map/near/pallas_call | solution.py:471
  28.3 0.0 collective-permute-done.6.refs_4_.refs_5_
  28.3 0.7 %upper.1.upper_ref = f32[512,384]{1,0:T(8,128)S(1)} custom-call(s32[1]{0:T(128)} %bitcast.me_ref, bf16[512,640]{1,0:T(8,128)(2,1)S(1)} %get-tuple-element.26.inv_high.high_ref, bf16[512,640]{1,0:T(8,128)(2,1)S(1)} %get-tuple-element.27.inv_low.low_ref, f32[128,384]{1,0:T(8,128)S(1)} %get-tuple-element.22.refs_0_, ...), custom_call_target="tpu_custom_call" | custom-call | flops 40000000000 | bytes 100000000 | tf_op jit(solution)/shard_map/upper/pallas_call | solution.py:481
  28.9 2.6 %far.1 = (f32[768,384]{1,0:T(8,128)S(1)}, bf16[768,512]{1,0:T(8,128)(2,1)S(1)}, bf16[768,512]{1,0:T(8,128)(2,1)S(1)}) custom-call(s32[1]{0:T(128)} %bitcast.me_ref, s32[8]{0:T(128)S(1)} %broadcast_xor_fusion.ids_ref, f32[256,768]{1,0:T(8,128)S(1)} %collective-permute-done.3.shards_ref, bf16[512,640]{1,0:T(8,128)(2,1)S(1)} %get-tuple-element.26.inv_high.high_ref, ...), custom_call_target="tpu_custom_call" | custom-call | tf_op jit(solution)/shard_map/far/pallas_call | solution.py:492
  31.6 1.5 %middle.1.part_ref = f32[768,384]{1,0:T(8,128)S(1)} custom-call(s32[1]{0:T(128)} %bitcast.me_ref, f32[768,384]{1,0:T(8,128)S(1)} %get-tuple-element.34.part_ref, bf16[768,512]{1,0:T(8,128)(2,1)S(1)} %get-tuple-element.35.high_ref, bf16[768,512]{1,0:T(8,128)(2,1)S(1)} %get-tuple-element.36.low_ref, f32[128,384]{1,0:T(8,128)S(1)} %get-tuple-element.22.refs_0_, ...), custom_call_target="tpu_custom_call" | custom-call | tf_op jit(solution)/shard_map/middle/pallas_call | solution.py:507
  33.1 1.6 %finish.1 = f32[768,384]{1,0:T(8,128)} custom-call(s32[1]{0:T(128)} %bitcast.me_ref, f32[768,384]{1,0:T(8,128)S(1)} %middle.1.part_ref, bf16[768,512]{1,0:T(8,128)(2,1)S(1)} %get-tuple-element.35.high_ref, bf16[768,512]{1,0:T(8,128)(2,1)S(1)} %get-tuple-element.36.low_ref, f32[128,384]{1,0:T(8,128)S(1)} %collective-permute-done.7.refs_0_, ...), custom_call_target="tpu_custom_call" | custom-call | tf_op jit(solution)/shard_map/finish/pallas_call | solution.py:519
  (10 shorter events, 0.1 us)
Async XLA Ops:
  1.8 9.6 %collective-permute-start.1 = (f32[128,384]{1,0:T(8,128)S(1)}, f32[128,384]{1,0:T(8,128)S(1)}, u32[]{:S(2)}, u32[]{:S(2)}) collective-permute-start(f32[128,384]{1,0:T(8,128)S(1)} %get-tuple-element.22.refs_0_), channel_id=1, source_target_pairs={{0,16},{16,8},{8,0},{1,17},{17,9},{9,1},{2,18},{18,10},{10,2},{3,1... | collective-permute-start | bytes 589832 | tf_op jit(solution)/shard_map/ppermute | solution.py:427
  3.9 7.6 %collective-permute-start = (f32[64,768]{1,0:T(8,128)S(1)}, f32[64,768]{1,0:T(8,128)S(1)}, u32[]{:S(2)}, u32[]{:S(2)}) collective-permute-start(f32[64,768]{1,0:T(8,128)S(1)} %get-tuple-element.21.first), channel_id=1, source_target_pairs={{0,4},{1,5},{2,6},{3,7},{4,0},{5,1},{6,2},{7,3},{8,12},{9,13},{10,... | collective-permute-start | bytes 589832 | tf_op jit(solution)/shard_map/ppermute | solution.py:368
  4.2 12.0 %collective-permute-start.4 = (f32[128,384]{1,0:T(8,128)S(1)}, f32[128,384]{1,0:T(8,128)S(1)}, u32[]{:S(2)}, u32[]{:S(2)}) collective-permute-start(f32[128,384]{1,0:T(8,128)S(1)} %get-tuple-element.28.refs_1_), channel_id=1, source_target_pairs={{0,16},{24,8},{16,24},{1,17},{25,9},{17,25},{2,18},{26,10},{18,26}... | collective-permute-start | bytes 589832 | tf_op jit(solution)/shard_map/ppermute | solution.py:427
  6.1 10.6 %collective-permute-start.5 = (f32[128,384]{1,0:T(8,128)S(1)}, f32[128,384]{1,0:T(8,128)S(1)}, u32[]{:S(2)}, u32[]{:S(2)}) collective-permute-start(f32[128,384]{1,0:T(8,128)S(1)} %get-tuple-element.29), channel_id=1, source_target_pairs={{24,16},{0,8},{8,24},{16,0},{25,17},{1,9},{9,25},{17,1},{26,18},{2... | collective-permute-start | bytes 589832 | tf_op jit(solution)/shard_map/ppermute | solution.py:427
  11.4 0.9 %copy-start = (s32[8]{0:T(128)S(1)}, s32[8]{0:T(128)}, u32[]{:S(2)}) copy-start(s32[8]{0:T(128)} %constant.12.clone) | copy-start | bytes 100
  12.0 13.3 %collective-permute-start.2 = (f32[128,768]{1,0:T(8,128)S(1)}, f32[128,768]{1,0:T(8,128)S(1)}, u32[]{:S(2)}, u32[]{:S(2)}) collective-permute-start(f32[128,768]{1,0:T(8,128)S(1)} %join.2.first), channel_id=1, source_target_pairs={{0,2},{1,3},{2,0},{3,1},{4,6},{5,7},{6,4},{7,5},{8,10},{9,11},{10,... | collective-permute-start | bytes 1179656 | tf_op jit(solution)/shard_map/ppermute | solution.py:368
  12.4 15.9 %collective-permute-start.6 = (f32[128,384]{1,0:T(8,128)S(1)}, f32[128,384]{1,0:T(8,128)S(1)}, u32[]{:S(2)}, u32[]{:S(2)}) collective-permute-start(f32[128,384]{1,0:T(8,128)S(1)} %get-tuple-element.40.refs_0_), channel_id=1, source_target_pairs={{16,24},{0,16},{24,0},{17,25},{1,17},{25,1},{18,26},{2,18},{26,2},... | collective-permute-start | bytes 589832 | tf_op jit(solution)/shard_map/ppermute | solution.py:427
  14.3 18.8 %collective-permute-start.7 = (f32[128,384]{1,0:T(8,128)S(1)}, f32[128,384]{1,0:T(8,128)S(1)}, u32[]{:S(2)}, u32[]{:S(2)}) collective-permute-start(f32[128,384]{1,0:T(8,128)S(1)} %get-tuple-element.39.refs_1_), channel_id=1, source_target_pairs={{16,8},{0,24},{8,16},{17,9},{1,25},{9,17},{18,10},{2,26},{10,18},{... | collective-permute-start | bytes 589832 | tf_op jit(solution)/shard_map/ppermute | solution.py:427
  16.7 16.4 %collective-permute-start.8 = (f32[128,384]{1,0:T(8,128)S(1)}, f32[128,384]{1,0:T(8,128)S(1)}, u32[]{:S(2)}, u32[]{:S(2)}) collective-permute-start(f32[128,384]{1,0:T(8,128)S(1)} %get-tuple-element.38), channel_id=1, source_target_pairs={{16,24},{17,25},{18,26},{19,27},{20,28},{21,29},{22,30},{23,31}} | collective-permute-start | bytes 589832 | tf_op jit(solution)/shard_map/ppermute | solution.py:427
  24.1 9.0 %collective-permute-start.9 = (f32[128,384]{1,0:T(8,128)S(1)}, f32[128,384]{1,0:T(8,128)S(1)}, u32[]{:S(2)}, u32[]{:S(2)}) collective-permute-start(f32[128,384]{1,0:T(8,128)S(1)} %get-tuple-element.37), channel_id=1, source_target_pairs={{16,8},{17,9},{18,10},{19,11},{20,12},{21,13},{22,14},{23,15}} | collective-permute-start | bytes 589832 | tf_op jit(solution)/shard_map/ppermute | solution.py:427
  25.8 3.1 %collective-permute-start.3 = (f32[256,768]{1,0:T(8,128)S(1)}, f32[256,768]{1,0:T(8,128)S(1)}, u32[]{:S(2)}, u32[]{:S(2)}) collective-permute-start(f32[256,768]{1,0:T(8,128)S(1)} %join.3.shards_ref), channel_id=1, source_target_pairs={{0,1},{1,0},{2,3},{3,2},{4,5},{5,4},{6,7},{7,6},{8,9},{9,8},{10,11... | collective-permute-start | bytes 2359304 | tf_op jit(solution)/shard_map/ppermute | solution.py:368

commit v10 on v9

--- a/solution.py
+++ b/solution.py
@@ -75,20 +75,21 @@
     relays = []
     for c in range(chunks):
         for k in range(1, count):
-            if middle + k < count:
-                relays.append((middle + k - 1, middle + k, ("stay", c)))
-            if middle - k > 0:
-                relays.append((middle - k + 1, middle - k, ("stay", c)))
-    early = [(s, t, ("pick", s)) for t in range(1, count) for s in range(middle, count) if s != t]
-    late = [(0, t, ("moved", t)) for t in range(1, count)]
-    late += [(s, t, ("pick", s)) for t in range(count - 1, 0, -1) for s in range(1, middle) if s != t]
+            step = [(middle + k - 1, middle + k, ("stay", c)), (middle - k + 1, middle - k, ("stay", c))]
+            relays += [move for move in (step if c + 1 < chunks else step[::-1]) if 0 < move[1] < count]
+    early = [(s, t, ("pick", s)) for t in range(1, count) for s in range(middle, count) if t not in (s, middle)]
+    early += [(s, 0, ("pick", s)) for s in range(1, middle)]
+    late = [(s, t, ("pick", s)) for s in range(1, middle) for t in range(middle + 1, count)]
+    late += [(0, t, ("moved", t)) for t in range(1, count)]
+    late += [(s, middle, ("pick", s)) for s in range(middle + 1, count)]
     late += [(s, 0, ("pick", s)) for s in range(middle, count)]
-    early += [(s, 0, ("pick", s)) for s in range(1, middle)]
+    last = [(s, t, ("pick", s)) for s in range(1, middle) for t in range(1, middle + 1) if s != t]
     ready = {(0, ("stay", c)): 0 for c in range(chunks)}
     rounds = []
-    while first or relays or early or late:
+    while first or relays or early or late or last:
         now, senders, targets = [], set(), set()
-        for queue in (first, relays, early, [] if len(rounds) < chunks else late):
+        queues = [first, relays, early] + [late] * (len(rounds) >= chunks) + [last] * (len(rounds) > chunks + 2)
+        for queue in queues:
             for move in list(queue):
                 s, t, item = move
                 known = item[0] != "stay" or ready.get((s, item), len(rounds) + 1) <= len(rounds)

time: 35.1 us -> 34.8 us (level)
  starting transfers between devices: 20.6 us -> 19.2 us
  waiting for transfers between devices: 0.44 us -> 1.24 us
    ppermute x7, starting transfers between devices: 18.9 us -> 17.7 us  [local(): lax.ppermute(operand, 'row', [(s, t) for s, t, item in moves])]
    ppermute x7, waiting for transfers between devices: 0.43 us -> 1.23 us  [local(): lax.ppermute(operand, 'row', [(s, t) for s, t, item in moves])]
  transfers between devices with their start and end apart: 10 -> 10, of which waited for: 1 -> 2; matrix products, arithmetic and copies ran while one was open for 0% -> 0% of each run, Pallas kernels for 29% -> 29%
where the time goes in v10:
time: 34.8 us; the launch traced here: 34.2 us
  starting transfers between devices  19.2 us (55%)
  Pallas kernels  13.4 us (39%)
  waiting for transfers between devices  1.24 us (4%)
    ppermute x7, starting transfers between devices, local(): lax.ppermute(operand, 'row', [(s, t) for s, t, item in moves])  17.7 us
    pallas_call x1, Pallas kernels, local(): pl.pallas_call(functools.partial(prepare_kernel, row_count), out_shape=(j...  2.92 us
    pallas_call x1, Pallas kernels, local(): pl.pallas_call(far_kernel, out_shape=(jax.ShapeDtypeStruct((rows, cols),...  2.62 us
    pallas_call x1, Pallas kernels, local(): pl.pallas_call(functools.partial(pick_kernel, row_count, order), out_shap...  1.77 us
    pallas_call x1, Pallas kernels, local(): pl.pallas_call(functools.partial(finish_kernel, late), out_shape=jax.Shap...  1.56 us
    ppermute x3, starting transfers between devices, gather_shards(): other = lax.ppermute(held, 'col', [(i, i ^ bit) for i in range(count)])  1.55 us
    pallas_call x1, Pallas kernels, local(): pl.pallas_call(functools.partial(middle_kernel, soon_late), out_shape=jax...  1.49 us
    pallas_call x1, Pallas kernels, local(): pl.pallas_call(near_kernel, out_shape=(jax.ShapeDtypeStruct((rows, late_r...  1.43 us
  transfers between devices with their start and end apart: 10, of which 2 were waited for; matrix products, arithmetic and copies ran while one was open for 0% of the time, Pallas kernels for 29%

profile of v10, /device:TPU:23, one launch (start us, length us, event | category | flops | bytes accessed | tf_op | source)
XLA Modules:
  0.0 34.2 jit_solution(207686557948689970)
XLA Ops:
  0.0 1.8 %pick.1 = (f32[128,384]{1,0:T(8,128)S(1)}, f32[128,384]{1,0:T(8,128)S(1)}, f32[128,384]{1,0:T(8,128)S(1)}, f32[128,384]{1,0:T(8,128)S(1)}, f32[128,384]{1,0:T(8,128)S(1)}, /*index=5*/f32[64,768]{1,0:T(8,128)S(1)}) custom-call(s32[1]{0:T(128)} %bitcast.me_ref, s32[1,512]{1,0:T(1,128)} %bitcast.2, f32[768,384]{1,0:T(8,128)} %matrix_ref.3, f32[64,768]{1,0:T(8,128)} %panel_ref.1), custom_call_target="tpu_custom_call" | custom-call | tf_op jit(solution)/shard_map/pick/pallas_call | solution.py:396
  1.8 2.1 %collective-permute-start.1 = (f32[128,384]{1,0:T(8,128)S(1)}, f32[128,384]{1,0:T(8,128)S(1)}, u32[]{:S(2)}, u32[]{:S(2)}) collective-permute-start(f32[128,384]{1,0:T(8,128)S(1)} %get-tuple-element.22.refs_0_), channel_id=1, source_target_pairs={{0,16},{16,8},{8,0},{1,17},{17,9},{9,1},{2,18},{18,10},{10,2},{3,1... | collective-permute-start | bytes 589832 | tf_op jit(solution)/shard_map/ppermute | solution.py:428
  3.9 0.3 collective-permute-start
  4.2 1.9 %collective-permute-start.4 = (f32[128,384]{1,0:T(8,128)S(1)}, f32[128,384]{1,0:T(8,128)S(1)}, u32[]{:S(2)}, u32[]{:S(2)}) collective-permute-start(f32[128,384]{1,0:T(8,128)S(1)} %get-tuple-element.28.refs_1_), channel_id=1, source_target_pairs={{0,16},{24,8},{16,24},{1,17},{25,9},{17,25},{2,18},{26,10},{18,26}... | collective-permute-start | bytes 589832 | tf_op jit(solution)/shard_map/ppermute | solution.py:428
  6.1 2.4 %collective-permute-start.5 = (f32[128,384]{1,0:T(8,128)S(1)}, f32[128,384]{1,0:T(8,128)S(1)}, u32[]{:S(2)}, u32[]{:S(2)}) collective-permute-start(f32[128,384]{1,0:T(8,128)S(1)} %get-tuple-element.29), channel_id=1, source_target_pairs={{8,24},{0,8},{24,16},{16,0},{9,25},{1,9},{25,17},{17,1},{10,26},{2... | collective-permute-start | bytes 589832 | tf_op jit(solution)/shard_map/ppermute | solution.py:428
  8.5 2.9 %prepare.1 = (bf16[512,640]{1,0:T(8,128)(2,1)S(1)}, bf16[512,640]{1,0:T(8,128)(2,1)S(1)}, bf16[768,128]{1,0:T(8,128)(2,1)S(1)}, f32[768,384]{1,0:T(8,128)S(1)}) custom-call(s32[1]{0:T(128)} %bitcast.me_ref, s32[1,512]{1,0:T(1,128)} %bitcast.3, f32[512,512]{1,0:T(8,128)} %inverse_ref.1, f32[768,384]{1,0:T(8,128)} %matrix_ref.3), custom_call_target="tpu_custom_call" | custom-call | flops 1000000 | bytes 100000 | tf_op jit(solution)/shard_map/prepare/pallas_call | solution.py:443
  11.4 0.0 collective-permute-done.1.refs_1_.refs_2_
  11.4 0.0 copy-start
  11.5 0.0 collective-permute-done.second
  11.5 0.5 %join.2.first = f32[128,768]{1,0:T(8,128)S(1)} custom-call(f32[64,768]{1,0:T(8,128)S(1)} %get-tuple-element.21.first, f32[64,768]{1,0:T(8,128)S(1)} %collective-permute-done.second, f32[128,384]{1,0:T(8,128)S(1)} %get-tuple-element.40.refs_0_, f32[128,384]{1,0:T(8,128)S(1)} %get-tuple-element.39.refs_1_, bf16[768,128]{1,0:T(8,128)(2,1)S(1)} %get-tuple-element.25.refs_2_.land_ref), custom_call_target="tpu_custom_call" | custom-call | tf_op jit(solution)/shard_map/join/pallas_call | solution.py:352
  12.0 0.3 collective-permute-start.2
  12.4 1.9 %collective-permute-start.6 = (f32[128,384]{1,0:T(8,128)S(1)}, f32[128,384]{1,0:T(8,128)S(1)}, u32[]{:S(2)}, u32[]{:S(2)}) collective-permute-start(f32[128,384]{1,0:T(8,128)S(1)} %get-tuple-element.40.refs_0_), channel_id=1, source_target_pairs={{16,24},{0,16},{24,0},{17,25},{1,17},{25,1},{18,26},{2,18},{26,2},... | collective-permute-start | bytes 589832 | tf_op jit(solution)/shard_map/ppermute | solution.py:428
  14.3 1.3 %collective-permute-start.7 = (f32[128,384]{1,0:T(8,128)S(1)}, f32[128,384]{1,0:T(8,128)S(1)}, u32[]{:S(2)}, u32[]{:S(2)}) collective-permute-start(f32[128,384]{1,0:T(8,128)S(1)} %get-tuple-element.39.refs_1_), channel_id=1, source_target_pairs={{16,8},{0,24},{17,9},{1,25},{18,10},{2,26},{19,11},{3,27},{20,12},... | collective-permute-start | bytes 589832 | tf_op jit(solution)/shard_map/ppermute | solution.py:428
  15.6 1.0 %collective-permute-done.5.refs_3_.refs_4_ = f32[128,384]{1,0:T(8,128)S(1)} collective-permute-done((f32[128,384]{1,0:T(8,128)S(1)}, f32[128,384]{1,0:T(8,128)S(1)}, u32[]{:S(2)}, u32[]{:S(2)}) %collective-permute-start.5) | collective-permute-done | bytes 196640 | tf_op jit(solution)/shard_map/ppermute | solution.py:428
  16.7 5.0 %collective-permute-start.8 = (f32[128,384]{1,0:T(8,128)S(1)}, f32[128,384]{1,0:T(8,128)S(1)}, u32[]{:S(2)}, u32[]{:S(2)}) collective-permute-start(f32[128,384]{1,0:T(8,128)S(1)} %get-tuple-element.38), channel_id=1, source_target_pairs={{16,8},{8,16},{17,9},{9,17},{18,10},{10,18},{19,11},{11,19},{20,12... | collective-permute-start | bytes 589832 | tf_op jit(solution)/shard_map/ppermute | solution.py:428
  21.6 3.1 %collective-permute-start.9 = (f32[128,384]{1,0:T(8,128)S(1)}, f32[128,384]{1,0:T(8,128)S(1)}, u32[]{:S(2)}, u32[]{:S(2)}) collective-permute-start(f32[128,384]{1,0:T(8,128)S(1)} %get-tuple-element.37), channel_id=1, source_target_pairs={{16,24},{17,25},{18,26},{19,27},{20,28},{21,29},{22,30},{23,31}} | collective-permute-start | bytes 589832 | tf_op jit(solution)/shard_map/ppermute | solution.py:428
  24.8 0.4 %join.3.shards_ref = f32[256,768]{1,0:T(8,128)S(1)} custom-call(f32[128,768]{1,0:T(8,128)S(1)} %join.2.first, f32[128,768]{1,0:T(8,128)S(1)} %collective-permute-done.2.second), custom_call_target="tpu_custom_call" | custom-call | tf_op jit(solution)/shard_map/join/pallas_call | solution.py:352
  25.2 0.9 %collective-permute-start.3 = (f32[256,768]{1,0:T(8,128)S(1)}, f32[256,768]{1,0:T(8,128)S(1)}, u32[]{:S(2)}, u32[]{:S(2)}) collective-permute-start(f32[256,768]{1,0:T(8,128)S(1)} %join.3.shards_ref), channel_id=1, source_target_pairs={{0,1},{1,0},{2,3},{3,2},{4,5},{5,4},{6,7},{7,6},{8,9},{9,8},{10,11... | collective-permute-start | bytes 2359304 | tf_op jit(solution)/shard_map/ppermute | solution.py:369
  26.1 1.4 %near.1 = (f32[768,384]{1,0:T(8,128)S(1)}, bf16[768,256]{1,0:T(8,128)(2,1)S(1)}, bf16[768,256]{1,0:T(8,128)(2,1)S(1)}) custom-call(s32[1]{0:T(128)} %bitcast.me_ref, s32[8]{0:T(128)S(1)} %broadcast_xor_fusion.ids_ref, f32[256,768]{1,0:T(8,128)S(1)} %join.3.shards_ref, bf16[512,640]{1,0:T(8,128)(2,1)S(1)} %get-tuple-element.26.inv_high.high_ref, ...), custom_call_target="tpu_custom_call" | custom-call | tf_op jit(solution)/shard_map/near/pallas_call | solution.py:472
  27.5 0.7 %upper.1.upper_ref = f32[512,384]{1,0:T(8,128)S(1)} custom-call(s32[1]{0:T(128)} %bitcast.me_ref, bf16[512,640]{1,0:T(8,128)(2,1)S(1)} %get-tuple-element.26.inv_high.high_ref, bf16[512,640]{1,0:T(8,128)(2,1)S(1)} %get-tuple-element.27.inv_low.low_ref, f32[128,384]{1,0:T(8,128)S(1)} %get-tuple-element.22.refs_0_, ...), custom_call_target="tpu_custom_call" | custom-call | flops 40000000000 | bytes 100000000 | tf_op jit(solution)/shard_map/upper/pallas_call | solution.py:482
  28.2 2.6 %far.1 = (f32[768,384]{1,0:T(8,128)S(1)}, bf16[768,512]{1,0:T(8,128)(2,1)S(1)}, bf16[768,512]{1,0:T(8,128)(2,1)S(1)}) custom-call(s32[1]{0:T(128)} %bitcast.me_ref, s32[8]{0:T(128)S(1)} %broadcast_xor_fusion.ids_ref, f32[256,768]{1,0:T(8,128)S(1)} %collective-permute-done.3.shards_ref, bf16[512,640]{1,0:T(8,128)(2,1)S(1)} %get-tuple-element.26.inv_high.high_ref, ...), custom_call_target="tpu_custom_call" | custom-call | tf_op jit(solution)/shard_map/far/pallas_call | solution.py:493
  30.8 1.5 %middle.1.part_ref = f32[768,384]{1,0:T(8,128)S(1)} custom-call(s32[1]{0:T(128)} %bitcast.me_ref, f32[768,384]{1,0:T(8,128)S(1)} %get-tuple-element.34.part_ref, bf16[768,512]{1,0:T(8,128)(2,1)S(1)} %get-tuple-element.35.high_ref, bf16[768,512]{1,0:T(8,128)(2,1)S(1)} %get-tuple-element.36.low_ref, f32[128,384]{1,0:T(8,128)S(1)} %get-tuple-element.22.refs_0_, ...), custom_call_target="tpu_custom_call" | custom-call | tf_op jit(solution)/shard_map/middle/pallas_call | solution.py:508
  32.3 0.2 collective-permute-done.8.refs_1_
  32.5 1.6 %finish.1 = f32[768,384]{1,0:T(8,128)} custom-call(s32[1]{0:T(128)} %bitcast.me_ref, f32[768,384]{1,0:T(8,128)S(1)} %middle.1.part_ref, bf16[768,512]{1,0:T(8,128)(2,1)S(1)} %get-tuple-element.35.high_ref, bf16[768,512]{1,0:T(8,128)(2,1)S(1)} %get-tuple-element.36.low_ref, f32[128,384]{1,0:T(8,128)S(1)} %collective-permute-done.7.refs_0_, ...), custom_call_target="tpu_custom_call" | custom-call | tf_op jit(solution)/shard_map/finish/pallas_call | solution.py:520
  (10 shorter events, 0.1 us)
Async XLA Ops:
  1.8 9.6 %collective-permute-start.1 = (f32[128,384]{1,0:T(8,128)S(1)}, f32[128,384]{1,0:T(8,128)S(1)}, u32[]{:S(2)}, u32[]{:S(2)}) collective-permute-start(f32[128,384]{1,0:T(8,128)S(1)} %get-tuple-element.22.refs_0_), channel_id=1, source_target_pairs={{0,16},{16,8},{8,0},{1,17},{17,9},{9,1},{2,18},{18,10},{10,2},{3,1... | collective-permute-start | bytes 589832 | tf_op jit(solution)/shard_map/ppermute | solution.py:428
  3.9 7.6 %collective-permute-start = (f32[64,768]{1,0:T(8,128)S(1)}, f32[64,768]{1,0:T(8,128)S(1)}, u32[]{:S(2)}, u32[]{:S(2)}) collective-permute-start(f32[64,768]{1,0:T(8,128)S(1)} %get-tuple-element.21.first), channel_id=1, source_target_pairs={{0,4},{1,5},{2,6},{3,7},{4,0},{5,1},{6,2},{7,3},{8,12},{9,13},{10,... | collective-permute-start | bytes 589832 | tf_op jit(solution)/shard_map/ppermute | solution.py:369
  4.2 11.4 %collective-permute-start.4 = (f32[128,384]{1,0:T(8,128)S(1)}, f32[128,384]{1,0:T(8,128)S(1)}, u32[]{:S(2)}, u32[]{:S(2)}) collective-permute-start(f32[128,384]{1,0:T(8,128)S(1)} %get-tuple-element.28.refs_1_), channel_id=1, source_target_pairs={{0,16},{24,8},{16,24},{1,17},{25,9},{17,25},{2,18},{26,10},{18,26}... | collective-permute-start | bytes 589832 | tf_op jit(solution)/shard_map/ppermute | solution.py:428
  6.1 10.6 %collective-permute-start.5 = (f32[128,384]{1,0:T(8,128)S(1)}, f32[128,384]{1,0:T(8,128)S(1)}, u32[]{:S(2)}, u32[]{:S(2)}) collective-permute-start(f32[128,384]{1,0:T(8,128)S(1)} %get-tuple-element.29), channel_id=1, source_target_pairs={{8,24},{0,8},{24,16},{16,0},{9,25},{1,9},{25,17},{17,1},{10,26},{2... | collective-permute-start | bytes 589832 | tf_op jit(solution)/shard_map/ppermute | solution.py:428
  11.4 0.9 %copy-start = (s32[8]{0:T(128)S(1)}, s32[8]{0:T(128)}, u32[]{:S(2)}) copy-start(s32[8]{0:T(128)} %constant.12.clone) | copy-start | bytes 100
  12.0 12.7 %collective-permute-start.2 = (f32[128,768]{1,0:T(8,128)S(1)}, f32[128,768]{1,0:T(8,128)S(1)}, u32[]{:S(2)}, u32[]{:S(2)}) collective-permute-start(f32[128,768]{1,0:T(8,128)S(1)} %join.2.first), channel_id=1, source_target_pairs={{0,2},{1,3},{2,0},{3,1},{4,6},{5,7},{6,4},{7,5},{8,10},{9,11},{10,... | collective-permute-start | bytes 1179656 | tf_op jit(solution)/shard_map/ppermute | solution.py:369
  12.4 15.2 %collective-permute-start.6 = (f32[128,384]{1,0:T(8,128)S(1)}, f32[128,384]{1,0:T(8,128)S(1)}, u32[]{:S(2)}, u32[]{:S(2)}) collective-permute-start(f32[128,384]{1,0:T(8,128)S(1)} %get-tuple-element.40.refs_0_), channel_id=1, source_target_pairs={{16,24},{0,16},{24,0},{17,25},{1,17},{25,1},{18,26},{2,18},{26,2},... | collective-permute-start | bytes 589832 | tf_op jit(solution)/shard_map/ppermute | solution.py:428
  14.3 18.2 %collective-permute-start.7 = (f32[128,384]{1,0:T(8,128)S(1)}, f32[128,384]{1,0:T(8,128)S(1)}, u32[]{:S(2)}, u32[]{:S(2)}) collective-permute-start(f32[128,384]{1,0:T(8,128)S(1)} %get-tuple-element.39.refs_1_), channel_id=1, source_target_pairs={{16,8},{0,24},{17,9},{1,25},{18,10},{2,26},{19,11},{3,27},{20,12},... | collective-permute-start | bytes 589832 | tf_op jit(solution)/shard_map/ppermute | solution.py:428
  16.7 15.8 %collective-permute-start.8 = (f32[128,384]{1,0:T(8,128)S(1)}, f32[128,384]{1,0:T(8,128)S(1)}, u32[]{:S(2)}, u32[]{:S(2)}) collective-permute-start(f32[128,384]{1,0:T(8,128)S(1)} %get-tuple-element.38), channel_id=1, source_target_pairs={{16,8},{8,16},{17,9},{9,17},{18,10},{10,18},{19,11},{11,19},{20,12... | collective-permute-start | bytes 589832 | tf_op jit(solution)/shard_map/ppermute | solution.py:428
  21.6 10.9 %collective-permute-start.9 = (f32[128,384]{1,0:T(8,128)S(1)}, f32[128,384]{1,0:T(8,128)S(1)}, u32[]{:S(2)}, u32[]{:S(2)}) collective-permute-start(f32[128,384]{1,0:T(8,128)S(1)} %get-tuple-element.37), channel_id=1, source_target_pairs={{16,24},{17,25},{18,26},{19,27},{20,28},{21,29},{22,30},{23,31}} | collective-permute-start | bytes 589832 | tf_op jit(solution)/shard_map/ppermute | solution.py:428
  25.2 3.0 %collective-permute-start.3 = (f32[256,768]{1,0:T(8,128)S(1)}, f32[256,768]{1,0:T(8,128)S(1)}, u32[]{:S(2)}, u32[]{:S(2)}) collective-permute-start(f32[256,768]{1,0:T(8,128)S(1)} %join.3.shards_ref), channel_id=1, source_target_pairs={{0,1},{1,0},{2,3},{3,2},{4,5},{5,4},{6,7},{7,6},{8,9},{9,8},{10,11... | collective-permute-start | bytes 2359304 | tf_op jit(solution)/shard_map/ppermute | solution.py:369

commit v11 on v10

--- a/solution.py
+++ b/solution.py
@@ -153,7 +153,7 @@
 
 
 def prepare_kernel(count, me_ref, pivot_ref, inverse_ref, matrix_ref, *refs):
-    high_ref, low_ref, land_ref, base_ref, pivot_v, inv_ref, rows_ref, sem = refs[-8:]
+    high_ref, low_ref, land_ref, pivot_v, inv_ref, sem = refs[-6:]
     rows, cols = matrix_ref.shape
     width = pivot_ref.shape[1]
     slot = width // count
@@ -162,7 +162,6 @@
     copies = [
         pltpu.make_async_copy(pivot_ref, pivot_v, sem.at[0]),
         pltpu.make_async_copy(inverse_ref, inv_ref, sem.at[1]),
-        pltpu.make_async_copy(matrix_ref, rows_ref, sem.at[2]),
     ]
     for copy in copies:
         copy.start()
@@ -177,13 +176,10 @@
     landing = lax.broadcasted_iota(jnp.int32, (rows, width), 0) == jnp.where(mine, pivot - me * rows, -1)
     land = mm_nt(landing.astype(BF16), one_hot(jnp.where(mine, place, -1), slot))
     land_ref[...] = land.astype(BF16)
-    taken = jnp.sum(land, axis=1, keepdims=True)
     copies[1].wait()
     inv_high, inv_low = halves(inv_ref[...])
     high_ref[...] = mm_nt(inv_high, spread).astype(BF16)
     low_ref[...] = mm_nt(inv_low, spread).astype(BF16)
-    copies[2].wait()
-    base_ref[...] = jnp.where(taken > 0.5, 0.0, rows_ref[...])
 
 
 def turn(shards_ref, start, high_ref, low_ref):
@@ -212,9 +208,12 @@
     pl.when(me_ref[0] != 0)(lambda: work(0))
 
 
-def far_kernel(me_ref, ids_ref, shards_ref, inv_high, inv_low, upper_ref, rows_ref, ends_ref, land_ref, *refs):
+def far_kernel(me_ref, ids_ref, shards_ref, inv_high, inv_low, upper_ref, matrix_ref, ends_ref, land_ref, *refs):
     near_high, near_low, out_ref, end_high, end_low, high_ref, low_ref = refs[:7]
-    side_high, side_low, up_high, up_low = refs[7:]
+    side_high, side_low, up_high, up_low = refs[7:-2]
+    rows_ref, sem = refs[-2:]
+    fetch = pltpu.make_async_copy(matrix_ref, rows_ref, sem)
+    fetch.start()
     half, rows = shards_ref.shape
     width, cols = upper_ref.shape
     depth = width // ids_ref.shape[0]
@@ -231,13 +230,17 @@
             side_high[part, cols:] = inv_high[source, first:].astype(F32)
             side_low[part, cols:] = inv_low[source, first:].astype(F32)
 
+    fetch.wait()
+
     def work(start):
         turn(shards_ref, start, high_ref, low_ref)
         high, right = high_ref[start:, :], side_high[...].astype(BF16)
         value = mm(low_ref[start:, :], right) + mm(high, side_low[...].astype(BF16)) + mm(high, right)
         high, right = near_high[start:, :], up_high[...].astype(BF16)
         near = mm(near_low[start:, :], right) + mm(high, up_low[...].astype(BF16)) + mm(high, right)
-        out_ref[start:, :] = rows_ref[start:, :] + (near + value[:, :cols])
+        taken = jnp.sum(land_ref[start:, :].astype(F32), axis=1, keepdims=True)
+        kept = jnp.where(taken > 0.5, 0.0, rows_ref[start:, :])
+        out_ref[start:, :] = kept + (near + value[:, :cols])
         high, low = halves(ends_ref[start:, :] + value[:, cols:])
         put(end_high, start, high)
         put(end_low, start, low)
@@ -440,21 +443,19 @@
     late_rows = len(late_blocks) * slot
 
     picked_rows = len(blocks) * slot + late_rows
-    inv_high, inv_low, land, base = pl.pallas_call(
+    inv_high, inv_low, land = pl.pallas_call(
         functools.partial(prepare_kernel, row_count),
         out_shape=(
             jax.ShapeDtypeStruct((width, picked_rows), BF16),
             jax.ShapeDtypeStruct((width, picked_rows), BF16),
             jax.ShapeDtypeStruct((rows, slot), BF16),
-            jax.ShapeDtypeStruct((rows, cols), F32),
         ),
         in_specs=[SMEM, HBM, HBM, HBM],
-        out_specs=(VMEM,) * 4,
+        out_specs=(VMEM,) * 3,
         scratch_shapes=[
             pltpu.VMEM((1, width), jnp.int32),
             pltpu.VMEM((width, width), F32),
-            pltpu.VMEM((rows, cols), F32),
-            pltpu.SemaphoreType.DMA((3,)),
+            pltpu.SemaphoreType.DMA((2,)),
         ],
         compiler_params=PARAMS,
         cost_estimate=SHORT,
@@ -494,14 +495,15 @@
         far_kernel,
         out_shape=(jax.ShapeDtypeStruct((rows, cols), F32),)
         + (jax.ShapeDtypeStruct((rows, late_rows + slot), BF16),) * 2,
-        in_specs=[SMEM, SMEM] + [VMEM] * 9,
+        in_specs=[SMEM, SMEM] + [VMEM] * 4 + [HBM] + [VMEM] * 4,
         out_specs=(VMEM,) * 3,
         scratch_shapes=[pltpu.VMEM((rows, half), BF16)] * 2
         + [pltpu.VMEM((half, cols + late_rows), F32)] * 2
-        + [pltpu.VMEM((half, cols), F32)] * 2,
+        + [pltpu.VMEM((half, cols), F32)] * 2
+        + [pltpu.VMEM((rows, cols), F32), pltpu.SemaphoreType.DMA(())],
         compiler_params=PARAMS,
         name="far",
-    )(here, ids, far, inv_high, inv_low, upper, base, ends, land, near_high, near_low)
+    )(here, ids, far, inv_high, inv_low, upper, matrix, ends, land, near_high, near_low)
 
     row_scratch = [pltpu.VMEM((late_rows + slot, cols), BF16)] * 2
     soon_arrays, (soon_late,) = used(soon_late)

time: 34.8 us -> 35.8 us (1.029)
  Pallas kernels: 13.4 us -> 14.3 us
    pallas_call x1, Pallas kernels: 2.62 us -> 3.72 us  [local(): pl.pallas_call(far_kernel, out_shape=(jax.ShapeDtypeStruct((rows, cols),...]
  transfers between devices with their start and end apart: 10 -> 10, of which waited for: 2 -> 1; matrix products, arithmetic and copies ran while one was open for 0% -> 0% of each run, Pallas kernels for 29% -> 31%
where the time goes in v11:
time: 35.8 us; the launch traced here: 35.2 us
  starting transfers between devices  19.2 us (54%)
  Pallas kernels  14.3 us (40%)
  waiting for transfers between devices  1.24 us (3%)
  between operations  0.36 us (1%)
    ppermute x7, starting transfers between devices, local(): lax.ppermute(operand, 'row', [(s, t) for s, t, item in moves])  17.7 us
    pallas_call x1, Pallas kernels, local(): pl.pallas_call(far_kernel, out_shape=(jax.ShapeDtypeStruct((rows, cols),...  3.72 us
    pallas_call x1, Pallas kernels, local(): pl.pallas_call(functools.partial(prepare_kernel, row_count), out_shape=(j...  2.74 us
    pallas_call x1, Pallas kernels, local(): pl.pallas_call(functools.partial(pick_kernel, row_count, order), out_shap...  1.77 us
    pallas_call x1, Pallas kernels, local(): pl.pallas_call(functools.partial(finish_kernel, late), out_shape=jax.Shap...  1.57 us
    ppermute x3, starting transfers between devices, gather_shards(): other = lax.ppermute(held, 'col', [(i, i ^ bit) for i in range(count)])  1.55 us
    pallas_call x1, Pallas kernels, local(): pl.pallas_call(functools.partial(middle_kernel, soon_late), out_shape=jax...  1.47 us
    pallas_call x1, Pallas kernels, local(): pl.pallas_call(near_kernel, out_shape=(jax.ShapeDtypeStruct((rows, late_r...  1.42 us
  transfers between devices with their start and end apart: 10, of which 1 were waited for; matrix products, arithmetic and copies ran while one was open for 0% of the time, Pallas kernels for 31%

profile of v11, /device:TPU:23, one launch (start us, length us, event | category | flops | bytes accessed | tf_op | source)
XLA Modules:
  0.0 35.2 jit_solution(9032412019196335518)
XLA Ops:
  0.0 1.8 %pick.1 = (f32[128,384]{1,0:T(8,128)S(1)}, f32[128,384]{1,0:T(8,128)S(1)}, f32[128,384]{1,0:T(8,128)S(1)}, f32[128,384]{1,0:T(8,128)S(1)}, f32[128,384]{1,0:T(8,128)S(1)}, /*index=5*/f32[64,768]{1,0:T(8,128)S(1)}) custom-call(s32[1]{0:T(128)} %bitcast.me_ref, s32[1,512]{1,0:T(1,128)} %bitcast.2, f32[768,384]{1,0:T(8,128)} %matrix_ref.5, f32[64,768]{1,0:T(8,128)} %panel_ref.1), custom_call_target="tpu_custom_call" | custom-call | tf_op jit(solution)/shard_map/pick/pallas_call | solution.py:399
  1.8 2.1 %collective-permute-start.1 = (f32[128,384]{1,0:T(8,128)S(1)}, f32[128,384]{1,0:T(8,128)S(1)}, u32[]{:S(2)}, u32[]{:S(2)}) collective-permute-start(f32[128,384]{1,0:T(8,128)S(1)} %get-tuple-element.21.refs_0_), channel_id=1, source_target_pairs={{0,16},{16,8},{8,0},{1,17},{17,9},{9,1},{2,18},{18,10},{10,2},{3,1... | collective-permute-start | bytes 589832 | tf_op jit(solution)/shard_map/ppermute | solution.py:431
  3.9 0.3 collective-permute-start
  4.2 1.9 %collective-permute-start.4 = (f32[128,384]{1,0:T(8,128)S(1)}, f32[128,384]{1,0:T(8,128)S(1)}, u32[]{:S(2)}, u32[]{:S(2)}) collective-permute-start(f32[128,384]{1,0:T(8,128)S(1)} %get-tuple-element.27.refs_1_), channel_id=1, source_target_pairs={{0,16},{24,8},{16,24},{1,17},{25,9},{17,25},{2,18},{26,10},{18,26}... | collective-permute-start | bytes 589832 | tf_op jit(solution)/shard_map/ppermute | solution.py:431
  6.1 2.4 %collective-permute-start.5 = (f32[128,384]{1,0:T(8,128)S(1)}, f32[128,384]{1,0:T(8,128)S(1)}, u32[]{:S(2)}, u32[]{:S(2)}) collective-permute-start(f32[128,384]{1,0:T(8,128)S(1)} %get-tuple-element.28), channel_id=1, source_target_pairs={{8,24},{0,8},{24,16},{16,0},{9,25},{1,9},{25,17},{17,1},{10,26},{2... | collective-permute-start | bytes 589832 | tf_op jit(solution)/shard_map/ppermute | solution.py:431
  8.5 2.7 %prepare.1 = (bf16[512,640]{1,0:T(8,128)(2,1)S(1)}, bf16[512,640]{1,0:T(8,128)(2,1)S(1)}, bf16[768,128]{1,0:T(8,128)(2,1)S(1)}) custom-call(s32[1]{0:T(128)} %bitcast.me_ref, s32[1,512]{1,0:T(1,128)} %bitcast.3, f32[512,512]{1,0:T(8,128)} %inverse_ref.1, f32[768,384]{1,0:T(8,128)} %matrix_ref.5), custom_call_target="tpu_custom_call" | custom-call | flops 1000000 | bytes 100000 | tf_op jit(solution)/shard_map/prepare/pallas_call | solution.py:446
  11.2 0.0 copy-start
  11.3 0.5 %join.2.first = f32[128,768]{1,0:T(8,128)S(1)} custom-call(f32[64,768]{1,0:T(8,128)S(1)} %get-tuple-element.20.first, f32[64,768]{1,0:T(8,128)S(1)} %collective-permute-done.second, f32[128,384]{1,0:T(8,128)S(1)} %get-tuple-element.38.refs_0_, f32[128,384]{1,0:T(8,128)S(1)} %get-tuple-element.37.refs_1_, bf16[768,128]{1,0:T(8,128)(2,1)S(1)} %get-tuple-element.24.refs_2_.land_ref), custom_call_target="tpu_custom_call" | custom-call | tf_op jit(solution)/shard_map/join/pallas_call | solution.py:355
  11.8 0.3 collective-permute-start.2
  12.2 1.9 %collective-permute-start.6 = (f32[128,384]{1,0:T(8,128)S(1)}, f32[128,384]{1,0:T(8,128)S(1)}, u32[]{:S(2)}, u32[]{:S(2)}) collective-permute-start(f32[128,384]{1,0:T(8,128)S(1)} %get-tuple-element.38.refs_0_), channel_id=1, source_target_pairs={{16,24},{0,16},{24,0},{17,25},{1,17},{25,1},{18,26},{2,18},{26,2},... | collective-permute-start | bytes 589832 | tf_op jit(solution)/shard_map/ppermute | solution.py:431
  14.1 1.3 %collective-permute-start.7 = (f32[128,384]{1,0:T(8,128)S(1)}, f32[128,384]{1,0:T(8,128)S(1)}, u32[]{:S(2)}, u32[]{:S(2)}) collective-permute-start(f32[128,384]{1,0:T(8,128)S(1)} %get-tuple-element.37.refs_1_), channel_id=1, source_target_pairs={{16,8},{0,24},{17,9},{1,25},{18,10},{2,26},{19,11},{3,27},{20,12},... | collective-permute-start | bytes 589832 | tf_op jit(solution)/shard_map/ppermute | solution.py:431
  15.4 0.0 collective-permute-done.4.refs_2_.refs_3_
  15.4 1.2 %collective-permute-done.5.refs_3_.refs_4_ = f32[128,384]{1,0:T(8,128)S(1)} collective-permute-done((f32[128,384]{1,0:T(8,128)S(1)}, f32[128,384]{1,0:T(8,128)S(1)}, u32[]{:S(2)}, u32[]{:S(2)}) %collective-permute-start.5) | collective-permute-done | bytes 196640 | tf_op jit(solution)/shard_map/ppermute | solution.py:431
  16.7 5.0 %collective-permute-start.8 = (f32[128,384]{1,0:T(8,128)S(1)}, f32[128,384]{1,0:T(8,128)S(1)}, u32[]{:S(2)}, u32[]{:S(2)}) collective-permute-start(f32[128,384]{1,0:T(8,128)S(1)} %get-tuple-element.36), channel_id=1, source_target_pairs={{16,8},{8,16},{17,9},{9,17},{18,10},{10,18},{19,11},{11,19},{20,12... | collective-permute-start | bytes 589832 | tf_op jit(solution)/shard_map/ppermute | solution.py:431
  21.6 3.1 %collective-permute-start.9 = (f32[128,384]{1,0:T(8,128)S(1)}, f32[128,384]{1,0:T(8,128)S(1)}, u32[]{:S(2)}, u32[]{:S(2)}) collective-permute-start(f32[128,384]{1,0:T(8,128)S(1)} %get-tuple-element.35), channel_id=1, source_target_pairs={{16,24},{17,25},{18,26},{19,27},{20,28},{21,29},{22,30},{23,31}} | collective-permute-start | bytes 589832 | tf_op jit(solution)/shard_map/ppermute | solution.py:431
  24.7 0.0 collective-permute-done.2.second
  24.8 0.4 %join.3.shards_ref = f32[256,768]{1,0:T(8,128)S(1)} custom-call(f32[128,768]{1,0:T(8,128)S(1)} %join.2.first, f32[128,768]{1,0:T(8,128)S(1)} %collective-permute-done.2.second), custom_call_target="tpu_custom_call" | custom-call | tf_op jit(solution)/shard_map/join/pallas_call | solution.py:355
  25.2 0.9 %collective-permute-start.3 = (f32[256,768]{1,0:T(8,128)S(1)}, f32[256,768]{1,0:T(8,128)S(1)}, u32[]{:S(2)}, u32[]{:S(2)}) collective-permute-start(f32[256,768]{1,0:T(8,128)S(1)} %join.3.shards_ref), channel_id=1, source_target_pairs={{0,1},{1,0},{2,3},{3,2},{4,5},{5,4},{6,7},{7,6},{8,9},{9,8},{10,11... | collective-permute-start | bytes 2359304 | tf_op jit(solution)/shard_map/ppermute | solution.py:372
  26.1 1.4 %near.1 = (f32[768,384]{1,0:T(8,128)S(1)}, bf16[768,256]{1,0:T(8,128)(2,1)S(1)}, bf16[768,256]{1,0:T(8,128)(2,1)S(1)}) custom-call(s32[1]{0:T(128)} %bitcast.me_ref, s32[8]{0:T(128)S(1)} %broadcast_xor_fusion.ids_ref, f32[256,768]{1,0:T(8,128)S(1)} %join.3.shards_ref, bf16[512,640]{1,0:T(8,128)(2,1)S(1)} %get-tuple-element.25.inv_high.high_ref, ...), custom_call_target="tpu_custom_call" | custom-call | tf_op jit(solution)/shard_map/near/pallas_call | solution.py:473
  27.5 0.0 collective-permute-done.6.refs_4_.refs_5_
  27.5 0.7 %upper.1.upper_ref = f32[512,384]{1,0:T(8,128)S(1)} custom-call(s32[1]{0:T(128)} %bitcast.me_ref, bf16[512,640]{1,0:T(8,128)(2,1)S(1)} %get-tuple-element.25.inv_high.high_ref, bf16[512,640]{1,0:T(8,128)(2,1)S(1)} %get-tuple-element.26.inv_low.low_ref, f32[128,384]{1,0:T(8,128)S(1)} %get-tuple-element.21.refs_0_, ...), custom_call_target="tpu_custom_call" | custom-call | flops 40000000000 | bytes 100000000 | tf_op jit(solution)/shard_map/upper/pallas_call | solution.py:483
  28.2 3.7 %far.1 = (f32[768,384]{1,0:T(8,128)S(1)}, bf16[768,512]{1,0:T(8,128)(2,1)S(1)}, bf16[768,512]{1,0:T(8,128)(2,1)S(1)}) custom-call(s32[1]{0:T(128)} %bitcast.me_ref, s32[8]{0:T(128)S(1)} %broadcast_xor_fusion.ids_ref, f32[256,768]{1,0:T(8,128)S(1)} %collective-permute-done.3.shards_ref, bf16[512,640]{1,0:T(8,128)(2,1)S(1)} %get-tuple-element.25.inv_high.high_ref, ...), custom_call_target="tpu_custom_call" | custom-call | tf_op jit(solution)/shard_map/far/pallas_call | solution.py:494
  31.9 1.5 %middle.1.part_ref = f32[768,384]{1,0:T(8,128)S(1)} custom-call(s32[1]{0:T(128)} %bitcast.me_ref, f32[768,384]{1,0:T(8,128)S(1)} %get-tuple-element.32.part_ref, bf16[768,512]{1,0:T(8,128)(2,1)S(1)} %get-tuple-element.33.high_ref, bf16[768,512]{1,0:T(8,128)(2,1)S(1)} %get-tuple-element.34.low_ref, f32[128,384]{1,0:T(8,128)S(1)} %get-tuple-element.21.refs_0_, ...), custom_call_target="tpu_custom_call" | custom-call | tf_op jit(solution)/shard_map/middle/pallas_call | solution.py:510
  33.4 1.6 %finish.1 = f32[768,384]{1,0:T(8,128)} custom-call(s32[1]{0:T(128)} %bitcast.me_ref, f32[768,384]{1,0:T(8,128)S(1)} %middle.1.part_ref, bf16[768,512]{1,0:T(8,128)(2,1)S(1)} %get-tuple-element.33.high_ref, bf16[768,512]{1,0:T(8,128)(2,1)S(1)} %get-tuple-element.34.low_ref, f32[128,384]{1,0:T(8,128)S(1)} %collective-permute-done.7.refs_0_, ...), custom_call_target="tpu_custom_call" | custom-call | tf_op jit(solution)/shard_map/finish/pallas_call | solution.py:522
  (10 shorter events, 0.1 us)
Async XLA Ops:
  1.8 9.5 %collective-permute-start.1 = (f32[128,384]{1,0:T(8,128)S(1)}, f32[128,384]{1,0:T(8,128)S(1)}, u32[]{:S(2)}, u32[]{:S(2)}) collective-permute-start(f32[128,384]{1,0:T(8,128)S(1)} %get-tuple-element.21.refs_0_), channel_id=1, source_target_pairs={{0,16},{16,8},{8,0},{1,17},{17,9},{9,1},{2,18},{18,10},{10,2},{3,1... | collective-permute-start | bytes 589832 | tf_op jit(solution)/shard_map/ppermute | solution.py:431
  3.9 7.4 %collective-permute-start = (f32[64,768]{1,0:T(8,128)S(1)}, f32[64,768]{1,0:T(8,128)S(1)}, u32[]{:S(2)}, u32[]{:S(2)}) collective-permute-start(f32[64,768]{1,0:T(8,128)S(1)} %get-tuple-element.20.first), channel_id=1, source_target_pairs={{0,4},{1,5},{2,6},{3,7},{4,0},{5,1},{6,2},{7,3},{8,12},{9,13},{10,... | collective-permute-start | bytes 589832 | tf_op jit(solution)/shard_map/ppermute | solution.py:372
  4.2 11.2 %collective-permute-start.4 = (f32[128,384]{1,0:T(8,128)S(1)}, f32[128,384]{1,0:T(8,128)S(1)}, u32[]{:S(2)}, u32[]{:S(2)}) collective-permute-start(f32[128,384]{1,0:T(8,128)S(1)} %get-tuple-element.27.refs_1_), channel_id=1, source_target_pairs={{0,16},{24,8},{16,24},{1,17},{25,9},{17,25},{2,18},{26,10},{18,26}... | collective-permute-start | bytes 589832 | tf_op jit(solution)/shard_map/ppermute | solution.py:431
  6.1 10.6 %collective-permute-start.5 = (f32[128,384]{1,0:T(8,128)S(1)}, f32[128,384]{1,0:T(8,128)S(1)}, u32[]{:S(2)}, u32[]{:S(2)}) collective-permute-start(f32[128,384]{1,0:T(8,128)S(1)} %get-tuple-element.28), channel_id=1, source_target_pairs={{8,24},{0,8},{24,16},{16,0},{9,25},{1,9},{25,17},{17,1},{10,26},{2... | collective-permute-start | bytes 589832 | tf_op jit(solution)/shard_map/ppermute | solution.py:431
  11.2 0.9 %copy-start = (s32[8]{0:T(128)S(1)}, s32[8]{0:T(128)}, u32[]{:S(2)}) copy-start(s32[8]{0:T(128)} %constant.12.clone) | copy-start | bytes 100
  11.8 12.9 %collective-permute-start.2 = (f32[128,768]{1,0:T(8,128)S(1)}, f32[128,768]{1,0:T(8,128)S(1)}, u32[]{:S(2)}, u32[]{:S(2)}) collective-permute-start(f32[128,768]{1,0:T(8,128)S(1)} %join.2.first), channel_id=1, source_target_pairs={{0,2},{1,3},{2,0},{3,1},{4,6},{5,7},{6,4},{7,5},{8,10},{9,11},{10,... | collective-permute-start | bytes 1179656 | tf_op jit(solution)/shard_map/ppermute | solution.py:372
  12.2 15.4 %collective-permute-start.6 = (f32[128,384]{1,0:T(8,128)S(1)}, f32[128,384]{1,0:T(8,128)S(1)}, u32[]{:S(2)}, u32[]{:S(2)}) collective-permute-start(f32[128,384]{1,0:T(8,128)S(1)} %get-tuple-element.38.refs_0_), channel_id=1, source_target_pairs={{16,24},{0,16},{24,0},{17,25},{1,17},{25,1},{18,26},{2,18},{26,2},... | collective-permute-start | bytes 589832 | tf_op jit(solution)/shard_map/ppermute | solution.py:431
  14.1 19.3 %collective-permute-start.7 = (f32[128,384]{1,0:T(8,128)S(1)}, f32[128,384]{1,0:T(8,128)S(1)}, u32[]{:S(2)}, u32[]{:S(2)}) collective-permute-start(f32[128,384]{1,0:T(8,128)S(1)} %get-tuple-element.37.refs_1_), channel_id=1, source_target_pairs={{16,8},{0,24},{17,9},{1,25},{18,10},{2,26},{19,11},{3,27},{20,12},... | collective-permute-start | bytes 589832 | tf_op jit(solution)/shard_map/ppermute | solution.py:431
  16.7 16.8 %collective-permute-start.8 = (f32[128,384]{1,0:T(8,128)S(1)}, f32[128,384]{1,0:T(8,128)S(1)}, u32[]{:S(2)}, u32[]{:S(2)}) collective-permute-start(f32[128,384]{1,0:T(8,128)S(1)} %get-tuple-element.36), channel_id=1, source_target_pairs={{16,8},{8,16},{17,9},{9,17},{18,10},{10,18},{19,11},{11,19},{20,12... | collective-permute-start | bytes 589832 | tf_op jit(solution)/shard_map/ppermute | solution.py:431
  21.6 11.8 %collective-permute-start.9 = (f32[128,384]{1,0:T(8,128)S(1)}, f32[128,384]{1,0:T(8,128)S(1)}, u32[]{:S(2)}, u32[]{:S(2)}) collective-permute-start(f32[128,384]{1,0:T(8,128)S(1)} %get-tuple-element.35), channel_id=1, source_target_pairs={{16,24},{17,25},{18,26},{19,27},{20,28},{21,29},{22,30},{23,31}} | collective-permute-start | bytes 589832 | tf_op jit(solution)/shard_map/ppermute | solution.py:431
  25.2 3.0 %collective-permute-start.3 = (f32[256,768]{1,0:T(8,128)S(1)}, f32[256,768]{1,0:T(8,128)S(1)}, u32[]{:S(2)}, u32[]{:S(2)}) collective-permute-start(f32[256,768]{1,0:T(8,128)S(1)} %join.3.shards_ref), channel_id=1, source_target_pairs={{0,1},{1,0},{2,3},{3,2},{4,5},{5,4},{6,7},{7,6},{8,9},{9,8},{10,11... | collective-permute-start | bytes 2359304 | tf_op jit(solution)/shard_map/ppermute | solution.py:372

commit v12 on v10

--- a/solution.py
+++ b/solution.py
@@ -9,7 +9,7 @@
 
 F32 = jnp.float32
 BF16 = jnp.bfloat16
-STEPS = 3
+STEPS = 6
 VMEM = pl.BlockSpec(memory_space=pltpu.VMEM)
 SMEM = pl.BlockSpec(memory_space=pltpu.SMEM)
 ANY = pl.BlockSpec(memory_space=pl.ANY)

time: 34.8 us -> 34.7 us (level)
  transfers between devices with their start and end apart: 10 -> 10, of which waited for: 2 -> 2; matrix products, arithmetic and copies ran while one was open for 0% -> 0% of each run, Pallas kernels for 29% -> 30%
where the time goes in v12:
time: 34.7 us; the launch traced here: 34.1 us
  starting transfers between devices  19.2 us (55%)
  Pallas kernels  13.4 us (39%)
  waiting for transfers between devices  1.12 us (3%)
    ppermute x7, starting transfers between devices, local(): lax.ppermute(operand, 'row', [(s, t) for s, t, item in moves])  17.7 us
    pallas_call x1, Pallas kernels, local(): pl.pallas_call(functools.partial(prepare_kernel, row_count), out_shape=(j...  2.92 us
    pallas_call x1, Pallas kernels, local(): pl.pallas_call(far_kernel, out_shape=(jax.ShapeDtypeStruct((rows, cols),...  2.62 us
    pallas_call x1, Pallas kernels, local(): pl.pallas_call(functools.partial(pick_kernel, row_count, order), out_shap...  1.77 us
    pallas_call x1, Pallas kernels, local(): pl.pallas_call(functools.partial(middle_kernel, soon_late), out_shape=jax...  1.61 us
    ppermute x3, starting transfers between devices, gather_shards(): other = lax.ppermute(held, 'col', [(i, i ^ bit) for i in range(count)])  1.55 us
    pallas_call x1, Pallas kernels, local(): pl.pallas_call(functools.partial(finish_kernel, late), out_shape=jax.Shap...  1.44 us
    pallas_call x1, Pallas kernels, local(): pl.pallas_call(near_kernel, out_shape=(jax.ShapeDtypeStruct((rows, late_r...  1.43 us
  transfers between devices with their start and end apart: 10, of which 2 were waited for; matrix products, arithmetic and copies ran while one was open for 0% of the time, Pallas kernels for 30%

profile of v12, /device:TPU:23, one launch (start us, length us, event | category | flops | bytes accessed | tf_op | source)
XLA Modules:
  0.0 34.1 jit_solution(12202977655930537909)
XLA Ops:
  0.0 1.8 %pick.1 = (f32[128,384]{1,0:T(8,128)S(1)}, f32[128,384]{1,0:T(8,128)S(1)}, f32[128,384]{1,0:T(8,128)S(1)}, f32[128,384]{1,0:T(8,128)S(1)}, f32[128,384]{1,0:T(8,128)S(1)}, /*index=5*/f32[64,768]{1,0:T(8,128)S(1)}) custom-call(s32[1]{0:T(128)} %bitcast.me_ref, s32[1,512]{1,0:T(1,128)} %bitcast.2, f32[768,384]{1,0:T(8,128)} %matrix_ref.3, f32[64,768]{1,0:T(8,128)} %panel_ref.1), custom_call_target="tpu_custom_call" | custom-call | tf_op jit(solution)/shard_map/pick/pallas_call | solution.py:396
  1.8 2.1 %collective-permute-start.1 = (f32[128,384]{1,0:T(8,128)S(1)}, f32[128,384]{1,0:T(8,128)S(1)}, u32[]{:S(2)}, u32[]{:S(2)}) collective-permute-start(f32[128,384]{1,0:T(8,128)S(1)} %get-tuple-element.22.refs_0_), channel_id=1, source_target_pairs={{0,16},{16,8},{8,0},{1,17},{17,9},{9,1},{2,18},{18,10},{10,2},{3,1... | collective-permute-start | bytes 589832 | tf_op jit(solution)/shard_map/ppermute | solution.py:428
  3.9 0.3 collective-permute-start
  4.2 1.9 %collective-permute-start.4 = (f32[128,384]{1,0:T(8,128)S(1)}, f32[128,384]{1,0:T(8,128)S(1)}, u32[]{:S(2)}, u32[]{:S(2)}) collective-permute-start(f32[128,384]{1,0:T(8,128)S(1)} %get-tuple-element.28.refs_1_), channel_id=1, source_target_pairs={{0,16},{24,8},{16,24},{1,17},{25,9},{17,25},{2,18},{26,10},{18,26}... | collective-permute-start | bytes 589832 | tf_op jit(solution)/shard_map/ppermute | solution.py:428
  6.1 2.4 %collective-permute-start.5 = (f32[128,384]{1,0:T(8,128)S(1)}, f32[128,384]{1,0:T(8,128)S(1)}, u32[]{:S(2)}, u32[]{:S(2)}) collective-permute-start(f32[128,384]{1,0:T(8,128)S(1)} %get-tuple-element.29), channel_id=1, source_target_pairs={{8,24},{0,8},{24,16},{16,0},{9,25},{1,9},{25,17},{17,1},{10,26},{2... | collective-permute-start | bytes 589832 | tf_op jit(solution)/shard_map/ppermute | solution.py:428
  8.5 2.9 %prepare.1 = (bf16[512,640]{1,0:T(8,128)(2,1)S(1)}, bf16[512,640]{1,0:T(8,128)(2,1)S(1)}, bf16[768,128]{1,0:T(8,128)(2,1)S(1)}, f32[768,384]{1,0:T(8,128)S(1)}) custom-call(s32[1]{0:T(128)} %bitcast.me_ref, s32[1,512]{1,0:T(1,128)} %bitcast.3, f32[512,512]{1,0:T(8,128)} %inverse_ref.1, f32[768,384]{1,0:T(8,128)} %matrix_ref.3), custom_call_target="tpu_custom_call" | custom-call | flops 1000000 | bytes 100000 | tf_op jit(solution)/shard_map/prepare/pallas_call | solution.py:443
  11.4 0.0 collective-permute-done.1.refs_1_.refs_2_
  11.4 0.0 copy-start
  11.5 0.0 collective-permute-done.second
  11.5 0.5 %join.2.first = f32[128,768]{1,0:T(8,128)S(1)} custom-call(f32[64,768]{1,0:T(8,128)S(1)} %get-tuple-element.21.first, f32[64,768]{1,0:T(8,128)S(1)} %collective-permute-done.second, f32[128,384]{1,0:T(8,128)S(1)} %get-tuple-element.40.refs_0_, f32[128,384]{1,0:T(8,128)S(1)} %get-tuple-element.39.refs_1_, bf16[768,128]{1,0:T(8,128)(2,1)S(1)} %get-tuple-element.25.refs_2_.land_ref), custom_call_target="tpu_custom_call" | custom-call | tf_op jit(solution)/shard_map/join/pallas_call | solution.py:352
  12.0 0.3 collective-permute-start.2
  12.4 1.9 %collective-permute-start.6 = (f32[128,384]{1,0:T(8,128)S(1)}, f32[128,384]{1,0:T(8,128)S(1)}, u32[]{:S(2)}, u32[]{:S(2)}) collective-permute-start(f32[128,384]{1,0:T(8,128)S(1)} %get-tuple-element.40.refs_0_), channel_id=1, source_target_pairs={{16,24},{0,16},{24,0},{17,25},{1,17},{25,1},{18,26},{2,18},{26,2},... | collective-permute-start | bytes 589832 | tf_op jit(solution)/shard_map/ppermute | solution.py:428
  14.3 1.3 %collective-permute-start.7 = (f32[128,384]{1,0:T(8,128)S(1)}, f32[128,384]{1,0:T(8,128)S(1)}, u32[]{:S(2)}, u32[]{:S(2)}) collective-permute-start(f32[128,384]{1,0:T(8,128)S(1)} %get-tuple-element.39.refs_1_), channel_id=1, source_target_pairs={{16,8},{0,24},{17,9},{1,25},{18,10},{2,26},{19,11},{3,27},{20,12},... | collective-permute-start | bytes 589832 | tf_op jit(solution)/shard_map/ppermute | solution.py:428
  15.6 1.0 %collective-permute-done.5.refs_3_.refs_4_ = f32[128,384]{1,0:T(8,128)S(1)} collective-permute-done((f32[128,384]{1,0:T(8,128)S(1)}, f32[128,384]{1,0:T(8,128)S(1)}, u32[]{:S(2)}, u32[]{:S(2)}) %collective-permute-start.5) | collective-permute-done | bytes 196640 | tf_op jit(solution)/shard_map/ppermute | solution.py:428
  16.7 5.0 %collective-permute-start.8 = (f32[128,384]{1,0:T(8,128)S(1)}, f32[128,384]{1,0:T(8,128)S(1)}, u32[]{:S(2)}, u32[]{:S(2)}) collective-permute-start(f32[128,384]{1,0:T(8,128)S(1)} %get-tuple-element.38), channel_id=1, source_target_pairs={{16,8},{8,16},{17,9},{9,17},{18,10},{10,18},{19,11},{11,19},{20,12... | collective-permute-start | bytes 589832 | tf_op jit(solution)/shard_map/ppermute | solution.py:428
  21.6 3.1 %collective-permute-start.9 = (f32[128,384]{1,0:T(8,128)S(1)}, f32[128,384]{1,0:T(8,128)S(1)}, u32[]{:S(2)}, u32[]{:S(2)}) collective-permute-start(f32[128,384]{1,0:T(8,128)S(1)} %get-tuple-element.37), channel_id=1, source_target_pairs={{16,24},{17,25},{18,26},{19,27},{20,28},{21,29},{22,30},{23,31}} | collective-permute-start | bytes 589832 | tf_op jit(solution)/shard_map/ppermute | solution.py:428
  24.8 0.4 %join.3.shards_ref = f32[256,768]{1,0:T(8,128)S(1)} custom-call(f32[128,768]{1,0:T(8,128)S(1)} %join.2.first, f32[128,768]{1,0:T(8,128)S(1)} %collective-permute-done.2.second), custom_call_target="tpu_custom_call" | custom-call | tf_op jit(solution)/shard_map/join/pallas_call | solution.py:352
  25.2 0.9 %collective-permute-start.3 = (f32[256,768]{1,0:T(8,128)S(1)}, f32[256,768]{1,0:T(8,128)S(1)}, u32[]{:S(2)}, u32[]{:S(2)}) collective-permute-start(f32[256,768]{1,0:T(8,128)S(1)} %join.3.shards_ref), channel_id=1, source_target_pairs={{0,1},{1,0},{2,3},{3,2},{4,5},{5,4},{6,7},{7,6},{8,9},{9,8},{10,11... | collective-permute-start | bytes 2359304 | tf_op jit(solution)/shard_map/ppermute | solution.py:369
  26.1 1.4 %near.1 = (f32[768,384]{1,0:T(8,128)S(1)}, bf16[768,256]{1,0:T(8,128)(2,1)S(1)}, bf16[768,256]{1,0:T(8,128)(2,1)S(1)}) custom-call(s32[1]{0:T(128)} %bitcast.me_ref, s32[8]{0:T(128)S(1)} %broadcast_xor_fusion.ids_ref, f32[256,768]{1,0:T(8,128)S(1)} %join.3.shards_ref, bf16[512,640]{1,0:T(8,128)(2,1)S(1)} %get-tuple-element.26.inv_high.high_ref, ...), custom_call_target="tpu_custom_call" | custom-call | tf_op jit(solution)/shard_map/near/pallas_call | solution.py:472
  27.5 0.7 %upper.1.upper_ref = f32[512,384]{1,0:T(8,128)S(1)} custom-call(s32[1]{0:T(128)} %bitcast.me_ref, bf16[512,640]{1,0:T(8,128)(2,1)S(1)} %get-tuple-element.26.inv_high.high_ref, bf16[512,640]{1,0:T(8,128)(2,1)S(1)} %get-tuple-element.27.inv_low.low_ref, f32[128,384]{1,0:T(8,128)S(1)} %get-tuple-element.22.refs_0_, ...), custom_call_target="tpu_custom_call" | custom-call | flops 40000000000 | bytes 100000000 | tf_op jit(solution)/shard_map/upper/pallas_call | solution.py:482
  28.2 2.6 %far.1 = (f32[768,384]{1,0:T(8,128)S(1)}, bf16[768,512]{1,0:T(8,128)(2,1)S(1)}, bf16[768,512]{1,0:T(8,128)(2,1)S(1)}) custom-call(s32[1]{0:T(128)} %bitcast.me_ref, s32[8]{0:T(128)S(1)} %broadcast_xor_fusion.ids_ref, f32[256,768]{1,0:T(8,128)S(1)} %collective-permute-done.3.shards_ref, bf16[512,640]{1,0:T(8,128)(2,1)S(1)} %get-tuple-element.26.inv_high.high_ref, ...), custom_call_target="tpu_custom_call" | custom-call | tf_op jit(solution)/shard_map/far/pallas_call | solution.py:493
  30.8 1.6 %middle.1.part_ref = f32[768,384]{1,0:T(8,128)S(1)} custom-call(s32[1]{0:T(128)} %bitcast.me_ref, f32[768,384]{1,0:T(8,128)S(1)} %get-tuple-element.34.part_ref, bf16[768,512]{1,0:T(8,128)(2,1)S(1)} %get-tuple-element.35.high_ref, bf16[768,512]{1,0:T(8,128)(2,1)S(1)} %get-tuple-element.36.low_ref, f32[128,384]{1,0:T(8,128)S(1)} %get-tuple-element.22.refs_0_, ...), custom_call_target="tpu_custom_call" | custom-call | tf_op jit(solution)/shard_map/middle/pallas_call | solution.py:508
  32.4 0.1 collective-permute-done.8.refs_1_
  32.5 1.4 %finish.1 = f32[768,384]{1,0:T(8,128)} custom-call(s32[1]{0:T(128)} %bitcast.me_ref, f32[768,384]{1,0:T(8,128)S(1)} %middle.1.part_ref, bf16[768,512]{1,0:T(8,128)(2,1)S(1)} %get-tuple-element.35.high_ref, bf16[768,512]{1,0:T(8,128)(2,1)S(1)} %get-tuple-element.36.low_ref, f32[128,384]{1,0:T(8,128)S(1)} %collective-permute-done.7.refs_0_, ...), custom_call_target="tpu_custom_call" | custom-call | tf_op jit(solution)/shard_map/finish/pallas_call | solution.py:520
  (10 shorter events, 0.1 us)
Async XLA Ops:
  1.8 9.6 %collective-permute-start.1 = (f32[128,384]{1,0:T(8,128)S(1)}, f32[128,384]{1,0:T(8,128)S(1)}, u32[]{:S(2)}, u32[]{:S(2)}) collective-permute-start(f32[128,384]{1,0:T(8,128)S(1)} %get-tuple-element.22.refs_0_), channel_id=1, source_target_pairs={{0,16},{16,8},{8,0},{1,17},{17,9},{9,1},{2,18},{18,10},{10,2},{3,1... | collective-permute-start | bytes 589832 | tf_op jit(solution)/shard_map/ppermute | solution.py:428
  3.9 7.6 %collective-permute-start = (f32[64,768]{1,0:T(8,128)S(1)}, f32[64,768]{1,0:T(8,128)S(1)}, u32[]{:S(2)}, u32[]{:S(2)}) collective-permute-start(f32[64,768]{1,0:T(8,128)S(1)} %get-tuple-element.21.first), channel_id=1, source_target_pairs={{0,4},{1,5},{2,6},{3,7},{4,0},{5,1},{6,2},{7,3},{8,12},{9,13},{10,... | collective-permute-start | bytes 589832 | tf_op jit(solution)/shard_map/ppermute | solution.py:369
  4.2 11.4 %collective-permute-start.4 = (f32[128,384]{1,0:T(8,128)S(1)}, f32[128,384]{1,0:T(8,128)S(1)}, u32[]{:S(2)}, u32[]{:S(2)}) collective-permute-start(f32[128,384]{1,0:T(8,128)S(1)} %get-tuple-element.28.refs_1_), channel_id=1, source_target_pairs={{0,16},{24,8},{16,24},{1,17},{25,9},{17,25},{2,18},{26,10},{18,26}... | collective-permute-start | bytes 589832 | tf_op jit(solution)/shard_map/ppermute | solution.py:428
  6.1 10.6 %collective-permute-start.5 = (f32[128,384]{1,0:T(8,128)S(1)}, f32[128,384]{1,0:T(8,128)S(1)}, u32[]{:S(2)}, u32[]{:S(2)}) collective-permute-start(f32[128,384]{1,0:T(8,128)S(1)} %get-tuple-element.29), channel_id=1, source_target_pairs={{8,24},{0,8},{24,16},{16,0},{9,25},{1,9},{25,17},{17,1},{10,26},{2... | collective-permute-start | bytes 589832 | tf_op jit(solution)/shard_map/ppermute | solution.py:428
  11.4 0.9 %copy-start = (s32[8]{0:T(128)S(1)}, s32[8]{0:T(128)}, u32[]{:S(2)}) copy-start(s32[8]{0:T(128)} %constant.12.clone) | copy-start | bytes 100
  12.0 12.7 %collective-permute-start.2 = (f32[128,768]{1,0:T(8,128)S(1)}, f32[128,768]{1,0:T(8,128)S(1)}, u32[]{:S(2)}, u32[]{:S(2)}) collective-permute-start(f32[128,768]{1,0:T(8,128)S(1)} %join.2.first), channel_id=1, source_target_pairs={{0,2},{1,3},{2,0},{3,1},{4,6},{5,7},{6,4},{7,5},{8,10},{9,11},{10,... | collective-permute-start | bytes 1179656 | tf_op jit(solution)/shard_map/ppermute | solution.py:369
  12.4 15.2 %collective-permute-start.6 = (f32[128,384]{1,0:T(8,128)S(1)}, f32[128,384]{1,0:T(8,128)S(1)}, u32[]{:S(2)}, u32[]{:S(2)}) collective-permute-start(f32[128,384]{1,0:T(8,128)S(1)} %get-tuple-element.40.refs_0_), channel_id=1, source_target_pairs={{16,24},{0,16},{24,0},{17,25},{1,17},{25,1},{18,26},{2,18},{26,2},... | collective-permute-start | bytes 589832 | tf_op jit(solution)/shard_map/ppermute | solution.py:428
  14.3 18.2 %collective-permute-start.7 = (f32[128,384]{1,0:T(8,128)S(1)}, f32[128,384]{1,0:T(8,128)S(1)}, u32[]{:S(2)}, u32[]{:S(2)}) collective-permute-start(f32[128,384]{1,0:T(8,128)S(1)} %get-tuple-element.39.refs_1_), channel_id=1, source_target_pairs={{16,8},{0,24},{17,9},{1,25},{18,10},{2,26},{19,11},{3,27},{20,12},... | collective-permute-start | bytes 589832 | tf_op jit(solution)/shard_map/ppermute | solution.py:428
  16.7 15.8 %collective-permute-start.8 = (f32[128,384]{1,0:T(8,128)S(1)}, f32[128,384]{1,0:T(8,128)S(1)}, u32[]{:S(2)}, u32[]{:S(2)}) collective-permute-start(f32[128,384]{1,0:T(8,128)S(1)} %get-tuple-element.38), channel_id=1, source_target_pairs={{16,8},{8,16},{17,9},{9,17},{18,10},{10,18},{19,11},{11,19},{20,12... | collective-permute-start | bytes 589832 | tf_op jit(solution)/shard_map/ppermute | solution.py:428
  21.6 10.9 %collective-permute-start.9 = (f32[128,384]{1,0:T(8,128)S(1)}, f32[128,384]{1,0:T(8,128)S(1)}, u32[]{:S(2)}, u32[]{:S(2)}) collective-permute-start(f32[128,384]{1,0:T(8,128)S(1)} %get-tuple-element.37), channel_id=1, source_target_pairs={{16,24},{17,25},{18,26},{19,27},{20,28},{21,29},{22,30},{23,31}} | collective-permute-start | bytes 589832 | tf_op jit(solution)/shard_map/ppermute | solution.py:428
  25.2 3.0 %collective-permute-start.3 = (f32[256,768]{1,0:T(8,128)S(1)}, f32[256,768]{1,0:T(8,128)S(1)}, u32[]{:S(2)}, u32[]{:S(2)}) collective-permute-start(f32[256,768]{1,0:T(8,128)S(1)} %join.3.shards_ref), channel_id=1, source_target_pairs={{0,1},{1,0},{2,3},{3,2},{4,5},{5,4},{6,7},{7,6},{8,9},{9,8},{10,11... | collective-permute-start | bytes 2359304 | tf_op jit(solution)/shard_map/ppermute | solution.py:369

commit v13 on v12

--- a/solution.py
+++ b/solution.py
@@ -9,7 +9,7 @@
 
 F32 = jnp.float32
 BF16 = jnp.bfloat16
-STEPS = 6
+STEPS = 2
 VMEM = pl.BlockSpec(memory_space=pltpu.VMEM)
 SMEM = pl.BlockSpec(memory_space=pltpu.SMEM)
 ANY = pl.BlockSpec(memory_space=pl.ANY)

time: 34.7 us -> 34.8 us (level)
  transfers between devices with their start and end apart: 10 -> 10, of which waited for: 2 -> 2; matrix products, arithmetic and copies ran while one was open for 0% -> 0% of each run, Pallas kernels for 30% -> 29%
where the time goes in v13:
time: 34.8 us; the launch traced here: 34.2 us
  starting transfers between devices  19.2 us (55%)
  Pallas kernels  13.4 us (39%)
  waiting for transfers between devices  1.22 us (4%)
    ppermute x7, starting transfers between devices, local(): lax.ppermute(operand, 'row', [(s, t) for s, t, item in moves])  17.7 us
    pallas_call x1, Pallas kernels, local(): pl.pallas_call(functools.partial(prepare_kernel, row_count), out_shape=(j...  2.92 us
    pallas_call x1, Pallas kernels, local(): pl.pallas_call(far_kernel, out_shape=(jax.ShapeDtypeStruct((rows, cols),...  2.62 us
    pallas_call x1, Pallas kernels, local(): pl.pallas_call(functools.partial(pick_kernel, row_count, order), out_shap...  1.77 us
    pallas_call x1, Pallas kernels, local(): pl.pallas_call(functools.partial(finish_kernel, late), out_shape=jax.Shap...  1.55 us
    ppermute x3, starting transfers between devices, gather_shards(): other = lax.ppermute(held, 'col', [(i, i ^ bit) for i in range(count)])  1.55 us
    pallas_call x1, Pallas kernels, local(): pl.pallas_call(functools.partial(middle_kernel, soon_late), out_shape=jax...  1.51 us
    pallas_call x1, Pallas kernels, local(): pl.pallas_call(near_kernel, out_shape=(jax.ShapeDtypeStruct((rows, late_r...  1.43 us
  transfers between devices with their start and end apart: 10, of which 2 were waited for; matrix products, arithmetic and copies ran while one was open for 0% of the time, Pallas kernels for 29%

profile of v13, /device:TPU:23, one launch (start us, length us, event | category | flops | bytes accessed | tf_op | source)
XLA Modules:
  0.0 34.2 jit_solution(3779822969691511491)
XLA Ops:
  0.0 1.8 %pick.1 = (f32[128,384]{1,0:T(8,128)S(1)}, f32[128,384]{1,0:T(8,128)S(1)}, f32[128,384]{1,0:T(8,128)S(1)}, f32[128,384]{1,0:T(8,128)S(1)}, f32[128,384]{1,0:T(8,128)S(1)}, /*index=5*/f32[64,768]{1,0:T(8,128)S(1)}) custom-call(s32[1]{0:T(128)} %bitcast.me_ref, s32[1,512]{1,0:T(1,128)} %bitcast.2, f32[768,384]{1,0:T(8,128)} %matrix_ref.3, f32[64,768]{1,0:T(8,128)} %panel_ref.1), custom_call_target="tpu_custom_call" | custom-call | tf_op jit(solution)/shard_map/pick/pallas_call | solution.py:396
  1.8 2.1 %collective-permute-start.1 = (f32[128,384]{1,0:T(8,128)S(1)}, f32[128,384]{1,0:T(8,128)S(1)}, u32[]{:S(2)}, u32[]{:S(2)}) collective-permute-start(f32[128,384]{1,0:T(8,128)S(1)} %get-tuple-element.22.refs_0_), channel_id=1, source_target_pairs={{0,16},{16,8},{8,0},{1,17},{17,9},{9,1},{2,18},{18,10},{10,2},{3,1... | collective-permute-start | bytes 589832 | tf_op jit(solution)/shard_map/ppermute | solution.py:428
  3.9 0.3 collective-permute-start
  4.2 1.9 %collective-permute-start.4 = (f32[128,384]{1,0:T(8,128)S(1)}, f32[128,384]{1,0:T(8,128)S(1)}, u32[]{:S(2)}, u32[]{:S(2)}) collective-permute-start(f32[128,384]{1,0:T(8,128)S(1)} %get-tuple-element.28.refs_1_), channel_id=1, source_target_pairs={{0,16},{24,8},{16,24},{1,17},{25,9},{17,25},{2,18},{26,10},{18,26}... | collective-permute-start | bytes 589832 | tf_op jit(solution)/shard_map/ppermute | solution.py:428
  6.1 2.4 %collective-permute-start.5 = (f32[128,384]{1,0:T(8,128)S(1)}, f32[128,384]{1,0:T(8,128)S(1)}, u32[]{:S(2)}, u32[]{:S(2)}) collective-permute-start(f32[128,384]{1,0:T(8,128)S(1)} %get-tuple-element.29), channel_id=1, source_target_pairs={{8,24},{0,8},{24,16},{16,0},{9,25},{1,9},{25,17},{17,1},{10,26},{2... | collective-permute-start | bytes 589832 | tf_op jit(solution)/shard_map/ppermute | solution.py:428
  8.5 2.9 %prepare.1 = (bf16[512,640]{1,0:T(8,128)(2,1)S(1)}, bf16[512,640]{1,0:T(8,128)(2,1)S(1)}, bf16[768,128]{1,0:T(8,128)(2,1)S(1)}, f32[768,384]{1,0:T(8,128)S(1)}) custom-call(s32[1]{0:T(128)} %bitcast.me_ref, s32[1,512]{1,0:T(1,128)} %bitcast.3, f32[512,512]{1,0:T(8,128)} %inverse_ref.1, f32[768,384]{1,0:T(8,128)} %matrix_ref.3), custom_call_target="tpu_custom_call" | custom-call | flops 1000000 | bytes 100000 | tf_op jit(solution)/shard_map/prepare/pallas_call | solution.py:443
  11.4 0.0 copy-start
  11.5 0.5 %join.2.first = f32[128,768]{1,0:T(8,128)S(1)} custom-call(f32[64,768]{1,0:T(8,128)S(1)} %get-tuple-element.21.first, f32[64,768]{1,0:T(8,128)S(1)} %collective-permute-done.second, f32[128,384]{1,0:T(8,128)S(1)} %get-tuple-element.40.refs_0_, f32[128,384]{1,0:T(8,128)S(1)} %get-tuple-element.39.refs_1_, bf16[768,128]{1,0:T(8,128)(2,1)S(1)} %get-tuple-element.25.refs_2_.land_ref), custom_call_target="tpu_custom_call" | custom-call | tf_op jit(solution)/shard_map/join/pallas_call | solution.py:352
  12.0 0.3 collective-permute-start.2
  12.4 1.9 %collective-permute-start.6 = (f32[128,384]{1,0:T(8,128)S(1)}, f32[128,384]{1,0:T(8,128)S(1)}, u32[]{:S(2)}, u32[]{:S(2)}) collective-permute-start(f32[128,384]{1,0:T(8,128)S(1)} %get-tuple-element.40.refs_0_), channel_id=1, source_target_pairs={{16,24},{0,16},{24,0},{17,25},{1,17},{25,1},{18,26},{2,18},{26,2},... | collective-permute-start | bytes 589832 | tf_op jit(solution)/shard_map/ppermute | solution.py:428
  14.3 1.3 %collective-permute-start.7 = (f32[128,384]{1,0:T(8,128)S(1)}, f32[128,384]{1,0:T(8,128)S(1)}, u32[]{:S(2)}, u32[]{:S(2)}) collective-permute-start(f32[128,384]{1,0:T(8,128)S(1)} %get-tuple-element.39.refs_1_), channel_id=1, source_target_pairs={{16,8},{0,24},{17,9},{1,25},{18,10},{2,26},{19,11},{3,27},{20,12},... | collective-permute-start | bytes 589832 | tf_op jit(solution)/shard_map/ppermute | solution.py:428
  15.6 0.0 collective-permute-done.4.refs_2_.refs_3_
  15.6 1.0 %collective-permute-done.5.refs_3_.refs_4_ = f32[128,384]{1,0:T(8,128)S(1)} collective-permute-done((f32[128,384]{1,0:T(8,128)S(1)}, f32[128,384]{1,0:T(8,128)S(1)}, u32[]{:S(2)}, u32[]{:S(2)}) %collective-permute-start.5) | collective-permute-done | bytes 196640 | tf_op jit(solution)/shard_map/ppermute | solution.py:428
  16.7 5.0 %collective-permute-start.8 = (f32[128,384]{1,0:T(8,128)S(1)}, f32[128,384]{1,0:T(8,128)S(1)}, u32[]{:S(2)}, u32[]{:S(2)}) collective-permute-start(f32[128,384]{1,0:T(8,128)S(1)} %get-tuple-element.38), channel_id=1, source_target_pairs={{16,8},{8,16},{17,9},{9,17},{18,10},{10,18},{19,11},{11,19},{20,12... | collective-permute-start | bytes 589832 | tf_op jit(solution)/shard_map/ppermute | solution.py:428
  21.6 3.1 %collective-permute-start.9 = (f32[128,384]{1,0:T(8,128)S(1)}, f32[128,384]{1,0:T(8,128)S(1)}, u32[]{:S(2)}, u32[]{:S(2)}) collective-permute-start(f32[128,384]{1,0:T(8,128)S(1)} %get-tuple-element.37), channel_id=1, source_target_pairs={{16,24},{17,25},{18,26},{19,27},{20,28},{21,29},{22,30},{23,31}} | collective-permute-start | bytes 589832 | tf_op jit(solution)/shard_map/ppermute | solution.py:428
  24.7 0.0 collective-permute-done.2.second
  24.8 0.4 %join.3.shards_ref = f32[256,768]{1,0:T(8,128)S(1)} custom-call(f32[128,768]{1,0:T(8,128)S(1)} %join.2.first, f32[128,768]{1,0:T(8,128)S(1)} %collective-permute-done.2.second), custom_call_target="tpu_custom_call" | custom-call | tf_op jit(solution)/shard_map/join/pallas_call | solution.py:352
  25.2 0.9 %collective-permute-start.3 = (f32[256,768]{1,0:T(8,128)S(1)}, f32[256,768]{1,0:T(8,128)S(1)}, u32[]{:S(2)}, u32[]{:S(2)}) collective-permute-start(f32[256,768]{1,0:T(8,128)S(1)} %join.3.shards_ref), channel_id=1, source_target_pairs={{0,1},{1,0},{2,3},{3,2},{4,5},{5,4},{6,7},{7,6},{8,9},{9,8},{10,11... | collective-permute-start | bytes 2359304 | tf_op jit(solution)/shard_map/ppermute | solution.py:369
  26.1 1.4 %near.1 = (f32[768,384]{1,0:T(8,128)S(1)}, bf16[768,256]{1,0:T(8,128)(2,1)S(1)}, bf16[768,256]{1,0:T(8,128)(2,1)S(1)}) custom-call(s32[1]{0:T(128)} %bitcast.me_ref, s32[8]{0:T(128)S(1)} %broadcast_xor_fusion.ids_ref, f32[256,768]{1,0:T(8,128)S(1)} %join.3.shards_ref, bf16[512,640]{1,0:T(8,128)(2,1)S(1)} %get-tuple-element.26.inv_high.high_ref, ...), custom_call_target="tpu_custom_call" | custom-call | tf_op jit(solution)/shard_map/near/pallas_call | solution.py:472
  27.5 0.7 %upper.1.upper_ref = f32[512,384]{1,0:T(8,128)S(1)} custom-call(s32[1]{0:T(128)} %bitcast.me_ref, bf16[512,640]{1,0:T(8,128)(2,1)S(1)} %get-tuple-element.26.inv_high.high_ref, bf16[512,640]{1,0:T(8,128)(2,1)S(1)} %get-tuple-element.27.inv_low.low_ref, f32[128,384]{1,0:T(8,128)S(1)} %get-tuple-element.22.refs_0_, ...), custom_call_target="tpu_custom_call" | custom-call | flops 40000000000 | bytes 100000000 | tf_op jit(solution)/shard_map/upper/pallas_call | solution.py:482
  28.2 2.6 %far.1 = (f32[768,384]{1,0:T(8,128)S(1)}, bf16[768,512]{1,0:T(8,128)(2,1)S(1)}, bf16[768,512]{1,0:T(8,128)(2,1)S(1)}) custom-call(s32[1]{0:T(128)} %bitcast.me_ref, s32[8]{0:T(128)S(1)} %broadcast_xor_fusion.ids_ref, f32[256,768]{1,0:T(8,128)S(1)} %collective-permute-done.3.shards_ref, bf16[512,640]{1,0:T(8,128)(2,1)S(1)} %get-tuple-element.26.inv_high.high_ref, ...), custom_call_target="tpu_custom_call" | custom-call | tf_op jit(solution)/shard_map/far/pallas_call | solution.py:493
  30.8 1.5 %middle.1.part_ref = f32[768,384]{1,0:T(8,128)S(1)} custom-call(s32[1]{0:T(128)} %bitcast.me_ref, f32[768,384]{1,0:T(8,128)S(1)} %get-tuple-element.34.part_ref, bf16[768,512]{1,0:T(8,128)(2,1)S(1)} %get-tuple-element.35.high_ref, bf16[768,512]{1,0:T(8,128)(2,1)S(1)} %get-tuple-element.36.low_ref, f32[128,384]{1,0:T(8,128)S(1)} %get-tuple-element.22.refs_0_, ...), custom_call_target="tpu_custom_call" | custom-call | tf_op jit(solution)/shard_map/middle/pallas_call | solution.py:508
  32.3 0.2 collective-permute-done.8.refs_1_
  32.5 1.6 %finish.1 = f32[768,384]{1,0:T(8,128)} custom-call(s32[1]{0:T(128)} %bitcast.me_ref, f32[768,384]{1,0:T(8,128)S(1)} %middle.1.part_ref, bf16[768,512]{1,0:T(8,128)(2,1)S(1)} %get-tuple-element.35.high_ref, bf16[768,512]{1,0:T(8,128)(2,1)S(1)} %get-tuple-element.36.low_ref, f32[128,384]{1,0:T(8,128)S(1)} %collective-permute-done.7.refs_0_, ...), custom_call_target="tpu_custom_call" | custom-call | tf_op jit(solution)/shard_map/finish/pallas_call | solution.py:520
  (10 shorter events, 0.1 us)
Async XLA Ops:
  1.8 9.6 %collective-permute-start.1 = (f32[128,384]{1,0:T(8,128)S(1)}, f32[128,384]{1,0:T(8,128)S(1)}, u32[]{:S(2)}, u32[]{:S(2)}) collective-permute-start(f32[128,384]{1,0:T(8,128)S(1)} %get-tuple-element.22.refs_0_), channel_id=1, source_target_pairs={{0,16},{16,8},{8,0},{1,17},{17,9},{9,1},{2,18},{18,10},{10,2},{3,1... | collective-permute-start | bytes 589832 | tf_op jit(solution)/shard_map/ppermute | solution.py:428
  3.9 7.6 %collective-permute-start = (f32[64,768]{1,0:T(8,128)S(1)}, f32[64,768]{1,0:T(8,128)S(1)}, u32[]{:S(2)}, u32[]{:S(2)}) collective-permute-start(f32[64,768]{1,0:T(8,128)S(1)} %get-tuple-element.21.first), channel_id=1, source_target_pairs={{0,4},{1,5},{2,6},{3,7},{4,0},{5,1},{6,2},{7,3},{8,12},{9,13},{10,... | collective-permute-start | bytes 589832 | tf_op jit(solution)/shard_map/ppermute | solution.py:369
  4.2 11.4 %collective-permute-start.4 = (f32[128,384]{1,0:T(8,128)S(1)}, f32[128,384]{1,0:T(8,128)S(1)}, u32[]{:S(2)}, u32[]{:S(2)}) collective-permute-start(f32[128,384]{1,0:T(8,128)S(1)} %get-tuple-element.28.refs_1_), channel_id=1, source_target_pairs={{0,16},{24,8},{16,24},{1,17},{25,9},{17,25},{2,18},{26,10},{18,26}... | collective-permute-start | bytes 589832 | tf_op jit(solution)/shard_map/ppermute | solution.py:428
  6.1 10.6 %collective-permute-start.5 = (f32[128,384]{1,0:T(8,128)S(1)}, f32[128,384]{1,0:T(8,128)S(1)}, u32[]{:S(2)}, u32[]{:S(2)}) collective-permute-start(f32[128,384]{1,0:T(8,128)S(1)} %get-tuple-element.29), channel_id=1, source_target_pairs={{8,24},{0,8},{24,16},{16,0},{9,25},{1,9},{25,17},{17,1},{10,26},{2... | collective-permute-start | bytes 589832 | tf_op jit(solution)/shard_map/ppermute | solution.py:428
  11.4 0.9 %copy-start = (s32[8]{0:T(128)S(1)}, s32[8]{0:T(128)}, u32[]{:S(2)}) copy-start(s32[8]{0:T(128)} %constant.12.clone) | copy-start | bytes 100
  12.0 12.7 %collective-permute-start.2 = (f32[128,768]{1,0:T(8,128)S(1)}, f32[128,768]{1,0:T(8,128)S(1)}, u32[]{:S(2)}, u32[]{:S(2)}) collective-permute-start(f32[128,768]{1,0:T(8,128)S(1)} %join.2.first), channel_id=1, source_target_pairs={{0,2},{1,3},{2,0},{3,1},{4,6},{5,7},{6,4},{7,5},{8,10},{9,11},{10,... | collective-permute-start | bytes 1179656 | tf_op jit(solution)/shard_map/ppermute | solution.py:369
  12.4 15.2 %collective-permute-start.6 = (f32[128,384]{1,0:T(8,128)S(1)}, f32[128,384]{1,0:T(8,128)S(1)}, u32[]{:S(2)}, u32[]{:S(2)}) collective-permute-start(f32[128,384]{1,0:T(8,128)S(1)} %get-tuple-element.40.refs_0_), channel_id=1, source_target_pairs={{16,24},{0,16},{24,0},{17,25},{1,17},{25,1},{18,26},{2,18},{26,2},... | collective-permute-start | bytes 589832 | tf_op jit(solution)/shard_map/ppermute | solution.py:428
  14.3 18.2 %collective-permute-start.7 = (f32[128,384]{1,0:T(8,128)S(1)}, f32[128,384]{1,0:T(8,128)S(1)}, u32[]{:S(2)}, u32[]{:S(2)}) collective-permute-start(f32[128,384]{1,0:T(8,128)S(1)} %get-tuple-element.39.refs_1_), channel_id=1, source_target_pairs={{16,8},{0,24},{17,9},{1,25},{18,10},{2,26},{19,11},{3,27},{20,12},... | collective-permute-start | bytes 589832 | tf_op jit(solution)/shard_map/ppermute | solution.py:428
  16.7 15.8 %collective-permute-start.8 = (f32[128,384]{1,0:T(8,128)S(1)}, f32[128,384]{1,0:T(8,128)S(1)}, u32[]{:S(2)}, u32[]{:S(2)}) collective-permute-start(f32[128,384]{1,0:T(8,128)S(1)} %get-tuple-element.38), channel_id=1, source_target_pairs={{16,8},{8,16},{17,9},{9,17},{18,10},{10,18},{19,11},{11,19},{20,12... | collective-permute-start | bytes 589832 | tf_op jit(solution)/shard_map/ppermute | solution.py:428
  21.6 10.9 %collective-permute-start.9 = (f32[128,384]{1,0:T(8,128)S(1)}, f32[128,384]{1,0:T(8,128)S(1)}, u32[]{:S(2)}, u32[]{:S(2)}) collective-permute-start(f32[128,384]{1,0:T(8,128)S(1)} %get-tuple-element.37), channel_id=1, source_target_pairs={{16,24},{17,25},{18,26},{19,27},{20,28},{21,29},{22,30},{23,31}} | collective-permute-start | bytes 589832 | tf_op jit(solution)/shard_map/ppermute | solution.py:428
  25.2 3.0 %collective-permute-start.3 = (f32[256,768]{1,0:T(8,128)S(1)}, f32[256,768]{1,0:T(8,128)S(1)}, u32[]{:S(2)}, u32[]{:S(2)}) collective-permute-start(f32[256,768]{1,0:T(8,128)S(1)} %join.3.shards_ref), channel_id=1, source_target_pairs={{0,1},{1,0},{2,3},{3,2},{4,5},{5,4},{6,7},{7,6},{8,9},{9,8},{10,11... | collective-permute-start | bytes 2359304 | tf_op jit(solution)/shard_map/ppermute | solution.py:369
